TPU v7x, 32 devices: a whole 2x2x4 slice. The times are simulated.
32 devices in a mesh: lat: 4 (over y, x), lon: 8 (over z, core).
Axes of the slice: x: 2, y: 2, z: 4, core: 2. Of those that a mesh axis runs over, the one named last changes fastest.
Arguments:
- fields: bfloat16 [448, 896, 768], P('lat', 'lon'), may hold values from -6 to 6
- cotangent: bfloat16 [448, 896, 768], P('lat', 'lon'), may hold values from -6 to 6
- inner_weight: bfloat16 [8, 2, 96, 96], replicated, may hold values from -0.4375 to 0.4375
- outer_weight: bfloat16 [8, 2, 96, 96], replicated, may hold values from -0.4375 to 0.4375
Outputs:
- field_gradient: bfloat16 [448, 896, 768], P('lat', 'lon')
- inner_gradient: float32 [8, 2, 96, 96], replicated
- outer_gradient: float32 [8, 2, 96, 96], replicated
All inputs are finite; a program needn't handle non-finite values.
Results may differ from a plain program's by a relative error of at most 0.012.
Values may be sent and summed in bfloat16 or wider, within the bound.
No kernel may reach another device: no remote copies, remote signals or barrier semaphores. Data moves between devices by JAX's collectives and lax.ppermute only.
A program may use at most 256 MiB of HBM per device.

v0:
```python
import math

import jax
import jax.numpy as jnp
from jax import lax
from jax.sharding import PartitionSpec as P

LATS = 448
LONS = 896
MODES = 128
BLOCKS = 8
BLOCK_W = 96


def trig_rows(row_ids, col_ids, period):
    phase = (row_ids[:, None] * col_ids[None, :] % period).astype(jnp.float32) * (
        2.0 * math.pi / period
    )
    factor = 1.0 / math.sqrt(period)
    return (
        (jnp.cos(phase) * factor).astype(jnp.bfloat16),
        (jnp.sin(phase) * factor).astype(jnp.bfloat16),
    )


def tables(row_total, col_total, period, col_first):
    row_ids = jnp.arange(row_total, dtype=jnp.int32)
    col_ids = col_first + jnp.arange(col_total, dtype=jnp.int32)
    return trig_rows(row_ids, col_ids, period)


def gelu_pair(value):
    cdf = 0.5 * (1.0 + jax.scipy.special.erf(value * 0.7071067811865476))
    density = jnp.exp(-0.5 * value * value) * 0.3989422804014327
    return (value * cdf, cdf + value * density)


def product(form, left, right):
    return jnp.einsum(form, left, right, preferred_element_type=jnp.float32)


def complex_apply(left_r, left_i, weight):
    real = product("pbi,bij->pbj", left_r, weight[:, 0]) - product(
        "pbi,bij->pbj", left_i, weight[:, 1]
    )
    imag = product("pbi,bij->pbj", left_r, weight[:, 1]) + product(
        "pbi,bij->pbj", left_i, weight[:, 0]
    )
    return (real, imag)


def complex_adjoint(adj_r, adj_i, weight):
    real = product("pbj,bij->pbi", adj_r, weight[:, 0]) + product(
        "pbj,bij->pbi", adj_i, weight[:, 1]
    )
    imag = product("pbj,bij->pbi", adj_i, weight[:, 0]) - product(
        "pbj,bij->pbi", adj_r, weight[:, 1]
    )
    return (real, imag)


def complex_outer(left_r, left_i, adj_r, adj_i):
    real = product("pbi,pbj->bij", left_r, adj_r) + product("pbi,pbj->bij", left_i, adj_i)
    imag = product("pbi,pbj->bij", left_r, adj_i) - product("pbi,pbj->bij", left_i, adj_r)
    return jnp.stack([real, imag], axis=1)


def local(fields, cotangent, inner_weight, outer_weight):
    lat_count = lax.axis_size("lat")
    lon_count = lax.axis_size("lon")
    row_count, col_count, width = fields.shape
    per_group = MODES // (lat_count * lon_count)
    slot_ids = jnp.arange(2 * MODES, dtype=jnp.int32)
    group_ids = slot_ids // (2 * per_group)
    part_ids = slot_ids // per_group % 2
    mode_ids = group_ids * per_group + slot_ids % per_group
    cos_rows, sin_rows = trig_rows(mode_ids, jnp.arange(LONS, dtype=jnp.int32), LONS)
    group_table = jnp.where((part_ids == 0)[:, None], cos_rows, -sin_rows)
    stacked = jnp.concatenate([fields, cotangent], axis=0).reshape(lon_count, -1, col_count, width)
    spectra = product(
        "kw,xhwc->xhkc",
        group_table,
        lax.all_to_all(stacked, "lon", split_axis=0, concat_axis=2, tiled=True),
    ).astype(jnp.bfloat16)
    spectra = spectra.reshape(spectra.shape[1], 2 * MODES, width)
    banded = lax.all_to_all(
        lax.all_to_all(spectra, "lon", split_axis=1, concat_axis=0, tiled=True),
        "lat",
        split_axis=1,
        concat_axis=0,
        tiled=True,
    )
    data = banded.reshape(lat_count, 2, row_count, -1)
    lat_cos, lat_sin = tables(LATS, LATS, LATS, 0)
    square = jnp.stack([lat_cos, lat_sin], axis=0)
    lat_table = square.reshape(2, LATS, lat_count, row_count)
    mixed = product("tmbr,bsrx->tmsx", lat_table, data).reshape(2, LATS, 2, 2, per_group, width)
    cos_part = mixed[0]
    sin_part = mixed[1]
    group_now = lax.axis_index("lon") * lat_count + lax.axis_index("lat")
    own_modes = group_now * per_group + jnp.arange(per_group, dtype=jnp.int32)
    weight_now = jnp.where(own_modes == 0, 1.0, 2.0).astype(jnp.bfloat16)[:, None]

    def blocked(value):
        return value.reshape(-1, BLOCKS, BLOCK_W)

    z_r = blocked((cos_part[:, 0, 0] + sin_part[:, 0, 1]).astype(jnp.bfloat16))
    z_i = blocked((cos_part[:, 0, 1] - sin_part[:, 0, 0]).astype(jnp.bfloat16))
    back_r = blocked((cos_part[:, 1, 0] + sin_part[:, 1, 1]).astype(jnp.bfloat16) * weight_now)
    back_i = blocked((cos_part[:, 1, 1] - sin_part[:, 1, 0]).astype(jnp.bfloat16) * weight_now)
    u_r, u_i = complex_apply(z_r, z_i, inner_weight)
    gelu_r, slope_r = gelu_pair(u_r)
    gelu_i, slope_i = gelu_pair(u_i)
    hidden_r = gelu_r.astype(jnp.bfloat16)
    hidden_i = gelu_i.astype(jnp.bfloat16)
    hidden_adj_r, hidden_adj_i = complex_adjoint(back_r, back_i, outer_weight)
    u_adj_r = (hidden_adj_r * slope_r).astype(jnp.bfloat16)
    u_adj_i = (hidden_adj_i * slope_i).astype(jnp.bfloat16)
    outer_part = complex_outer(hidden_r, hidden_i, back_r, back_i)
    inner_part = complex_outer(z_r, z_i, u_adj_r, u_adj_i)
    inner_total, outer_total = lax.psum((inner_part, outer_part), ("lat", "lon"))
    scale = 1.0 / math.sqrt(LATS * MODES)
    inner_gradient = inner_total * scale
    outer_gradient = outer_total * scale
    z_adj_r, z_adj_i = complex_adjoint(u_adj_r, u_adj_i, inner_weight)
    adj_stack = jnp.stack(
        [
            z_adj_r.astype(jnp.bfloat16).reshape(LATS, per_group, width),
            z_adj_i.astype(jnp.bfloat16).reshape(LATS, per_group, width),
        ],
        axis=1,
    )
    mixed_back = product("tmh,mx->thx", square, adj_stack.reshape(LATS, -1)).reshape(
        2, LATS, 2, per_group, width
    )
    adj_r = mixed_back[0][:, 0] - mixed_back[1][:, 1]
    adj_i = mixed_back[1][:, 0] + mixed_back[0][:, 1]
    spectral_adj = jnp.stack([adj_r, adj_i], axis=1).astype(jnp.bfloat16)
    returned = lax.all_to_all(spectral_adj, "lat", split_axis=0, concat_axis=2, tiled=True)
    col_first = lax.axis_index("lon") * col_count
    piece = lax.all_gather(returned, "lon", axis=2, tiled=True)
    amount = piece.shape[2]
    cos_piece, sin_piece = tables(amount, col_count, LONS, col_first)
    panel = jnp.concatenate([cos_piece, -sin_piece], axis=0)
    merged = piece.reshape(row_count, 2 * amount, width)
    summed = product("hkc,kw->hwc", merged, panel)
    field_gradient = summed.astype(jnp.bfloat16)
    return (field_gradient, inner_gradient, outer_gradient)


def solution(mesh):
    return jax.shard_map(
        local,
        mesh=mesh,
        in_specs=(P("lat", "lon", None), P("lat", "lon", None), P(), P()),
        out_specs=(P("lat", "lon", None), P(), P()),
        check_vma=False,
    )
```

profile of v0, /device:TPU:0, one launch (start us, length us, event | category | flops | bytes accessed | tf_op | source)
XLA Modules:
  0.0 2277.9 jit_solution(12470919340473381360)
XLA Ops:
  8.0 26.3 %pad_maximum_fusion = bf16[224,112,768]{2,1,0:T(8,128)(2,1)} fusion(bf16[112,112,768]{2,1,0:T(8,128)(2,1)} %param.5, bf16[112,112,768]{2,1,0:T(8,128)(2,1)} %param.4), kind=kLoop, calls=%fused_computation | loop fusion | flops 19267584 | bytes 77070336 | tf_op jit(solution)/shard_map/concatenate | solution.py:79
  34.3 7.5 all-to-all-start
  41.8 830.7 %all-to-all-done = bf16[8,28,112,768]{3,2,1,0:T(8,128)(2,1)} async-done(((bf16[8,28,112,768]{3,2,1,0:T(8,128)(2,1)}), bf16[8,28,112,768]{3,2,1,0:T(8,128)(2,1)}, u32[]{:S(2)}, u32[]{:S(2)}) %all-to-all-start) | async-done | bytes 38535200 | tf_op jit(solution)/shard_map/all_to_all | solution.py:83
  872.5 26.2 %copy.157 = bf16[1,28,8,112,768]{4,3,2,1,0:T(8,128)(2,1)} copy(bf16[1,28,8,112,768]{4,3,1,2,0:T(8,128)(2,1)} %bitcast.5) | data formatting | bytes 77070336 | tf_op jit(solution)/shard_map/all_to_all | solution.py:83
  898.7 30.9 %convert_bitcast_fusion.1 = bf16[28,256,768]{1,2,0:T(8,128)(2,1)} fusion(bf16[28,896,768]{2,1,0:T(8,128)(2,1)} %bitcast.220, s32[256]{0:T(256)S(1)} %fusion.139, pred[256]{0:T(512)(128)(4,1)S(1)} %fusion.143), kind=kOutput, calls=%fused_computation.6 | convolution fusion | flops 9874407424 | bytes 49546496 | tf_op jit(solution)/shard_map/kw,xhwc->xhkc/dot_general | solution.py:39
  929.6 16.3 copy.159
  945.9 278.2 %all_to_all.66 = bf16[28,256,768]{2,0,1:T(8,128)(2,1)S(1)} all-to-all(bf16[28,256,768]{2,0,1:T(8,128)(2,1)} %copy.159), channel_id=1, replica_groups=mesh['lat'=4,'lon'=8] {'lon'}, dimensions={1} | all-to-all | bytes 22020096 | tf_op jit(solution)/shard_map/all_to_all | solution.py:87
  1224.1 21.7 copy.161
  1245.8 19.2 copy.162
  1280.5 111.7 %all-to-all-done.2 = bf16[224,32,768]{2,0,1:T(8,128)(2,1)} async-done(((bf16[224,32,768]{2,0,1:T(8,128)(2,1)}), bf16[224,32,768]{2,0,1:T(8,128)(2,1)}, u32[]{:S(2)}, u32[]{:S(2)}) %all-to-all-start.2) | async-done | bytes 11010080 | tf_op jit(solution)/shard_map/all_to_all | solution.py:86
  1392.1 12.6 copy.222
  1404.8 16.6 reshape.255
  1421.4 22.1 convolution_bitcast_fusion
  1443.5 27.9 %fusion.152 = (f32[1,448,2,6144]{3,1,2,0:T(8,128)}, f32[1,448,2,6144]{3,1,2,0:T(8,128)}) fusion(f32[2,448,2,6144]{3,1,2,0:T(8,128)} %convolution_bitcast_fusion), kind=kLoop, calls=%fused_computation.208 | loop fusion | bytes 88080384 | tf_op jit(solution)/shard_map/slice | solution.py:98
  1471.5 25.8 %squeeze.16 = f32[448,2,2,4,768]{4,3,2,0,1:T(4,128)} reshape(f32[1,448,2,6144]{3,1,2,0:T(8,128)} %get-tuple-element.24) | data formatting | bytes 44040192 | tf_op jit(solution)/shard_map/squeeze | solution.py:98
  1497.3 25.8 %squeeze.17 = f32[448,2,2,4,768]{4,3,2,0,1:T(4,128)} reshape(f32[1,448,2,6144]{3,1,2,0:T(8,128)} %get-tuple-element.25) | data formatting | bytes 44040192 | tf_op jit(solution)/shard_map/squeeze | solution.py:99
  1523.1 19.4 fusion.23
  1558.2 7.3 convert_element_type.185
  1597.0 7.3 convert_element_type.178
  1637.2 7.5 stack_reshape.6
  1656.5 7.5 stack_reshape.7
  1675.1 10.1 reshape.262
  1685.1 7.9 fusion.76
  1693.1 8.5 fusion.153
  1701.6 13.5 squeeze.22
  1715.0 13.7 squeeze.23
  1728.7 8.7 fusion.15
  1761.8 52.0 %all-to-all-done.3 = bf16[448,2,4,768]{3,2,1,0:T(4,128)(2,1)} async-done(((bf16[448,2,4,768]{3,2,1,0:T(4,128)(2,1)}), bf16[448,2,4,768]{3,2,1,0:T(4,128)(2,1)}, u32[]{:S(2)}, u32[]{:S(2)}) %all-to-all-start.3) | async-done | bytes 5505056 | tf_op jit(solution)/shard_map/all_to_all | solution.py:139
  1813.8 8.1 copy.190
  1822.0 9.8 all_to_all.61
  1832.4 410.6 %all-reduce.3.cloned.1.call-done = (f32[8,2,96,96]{3,2,0,1:T(8,128)}, f32[8,2,96,96]{3,2,0,1:T(8,128)}) async-done(((f32[8,2,96,96]{3,2,0,1:T(8,128)}, f32[8,2,96,96]{3,2,0,1:T(8,128)}), (f32[8,2,96,96]{3,2,0,1:T(8,128)}, f32[8,2,96,96]{3,2,0,1:T(8,128)})) %all-reduce.3.cloned.1.call-update) | async-done | bytes 1179664 | tf_op jit(solution)/shard_map/psum | solution.py:121
  2246.4 23.6 %convert_bitcast_fusion = bf16[112,112,768]{2,1,0:T(8,128)(2,1)} fusion(bf16[112,256,768]{2,1,0:T(8,128)(2,1)} %bitcast.216, bf16[128,112]{0,1:T(8,128)(2,1)S(1)} %fusion.136, bf16[128,112]{0,1:T(8,128)(2,1)S(1)} %multiply_convert_fusion.7), kind=kOutput, calls=%fused_computation.1 | convolution fusion | flops 4942249984 | bytes 63365120 | tf_op jit(solution)/shard_map/hkc,kw->hwc/dot_general | solution.py:39
  (89 shorter events, 146.4 us)
Async XLA Ops:
  34.3 838.2 %all-to-all-start = ((bf16[8,28,112,768]{3,2,1,0:T(8,128)(2,1)}), bf16[8,28,112,768]{3,2,1,0:T(8,128)(2,1)}, u32[]{:S(2)}, u32[]{:S(2)}) async-start(bf16[8,28,112,768]{3,2,1,0:T(8,128)(2,1)} %bitcast.215), calls=%async_computation | async-start | bytes 77070336 | tf_op jit(solution)/shard_map/all_to_all | solution.py:83
  1265.0 127.1 %all-to-all-start.2 = ((bf16[224,32,768]{2,0,1:T(8,128)(2,1)}), bf16[224,32,768]{2,0,1:T(8,128)(2,1)}, u32[]{:S(2)}, u32[]{:S(2)}) async-start(bf16[224,32,768]{2,0,1:T(8,128)(2,1)} %copy.162), calls=%async_computation.2 | async-start | bytes 22020096 | tf_op jit(solution)/shard_map/all_to_all | solution.py:86
  1542.5 9.0 copy-start.10
  1584.5 6.6 copy-start
  1597.0 13.2 copy-start.14
  1610.2 2.8 copy-start.6
  1613.0 7.4 slice-start
  1613.9 6.5 slice-start.1
  1619.4 6.1 copy-start.2
  1619.4 2.8 copy-start.8
  1625.5 3.4 copy-start.4
  1675.1 10.1 copy-start.13
  1743.5 70.4 %all-to-all-start.3 = ((bf16[448,2,4,768]{3,2,1,0:T(4,128)(2,1)}), bf16[448,2,4,768]{3,2,1,0:T(4,128)(2,1)}, u32[]{:S(2)}, u32[]{:S(2)}) async-start(bf16[448,2,4,768]{3,2,1,0:T(4,128)(2,1)} %pad_maximum_fusion.2), calls=%async_computation.3 | async-start | bytes 11010048 | tf_op jit(solution)/shard_map/all_to_all | solution.py:139
  1748.6 494.4 %all-reduce.3.cloned.1.call-start = ((), (), s32[]{:S(2)}) async-start(), calls=%async_computation.5 | async-start | bytes 3145728 | tf_op jit(solution)/shard_map/psum | solution.py:121
  1748.7 3.7 copy-start.7
  1748.7 4.2 copy-start.12
  1748.7 5.1 copy-start.9
  1752.9 2.0 copy-start.11
  1754.9 1.8 copy-start.3
  1754.9 2.9 copy-start.5
  1756.7 2.0 copy-start.1
  1761.5 484.9 %all-gather.2.cloned.1.call-start = ((), (), s32[]{:S(2)}) async-start(), calls=%async_computation.4 | async-start | bytes 49545216 | tf_op jit(solution)/shard_map/all_gather | solution.py:141
Sparse Core Ops, SparseCore 0:
  1761.6 481.3 all-reduce.2
Sparse Core Ops, SparseCore 1:
  1831.8 374.9 all-gather.1
where the time goes:
time: 2290 us; the launch traced here: 2280 us
  waiting for transfers between devices  1410 us (62%)
  local copies, waits for them, and re-layouts  341 us (15%)
  blocking collectives  278 us (12%)
  matrix products  138 us (6%)
  other arithmetic  80.1 us (3%)
    all_to_all x1, waiting for transfers between devices, local(): lax.all_to_all(stacked, 'lon', split_axis=0, concat_axis=2, tiled=True)  831 us
    psum x1, waiting for transfers between devices, local(): lax.psum((inner_part, outer_part), ('lat', 'lon'))  411 us
    all_to_all x1, blocking collectives, local(): lax.all_to_all(spectra, 'lon', split_axis=1, concat_axis=0, tiled=True)  278 us
    dot_general x24, matrix products, product(): return jnp.einsum(form, left, right, preferred_element_type=jnp.float32)  138 us
    all_to_all x1, waiting for transfers between devices, local(): lax.all_to_all(lax.all_to_all(spectra, 'lon', split_axis=1, concat_axis=0...  112 us
    all_to_all x1, waiting for transfers between devices, local(): lax.all_to_all(spectral_adj, 'lat', split_axis=0, concat_axis=2, tiled=True)  52 us
  transfers between devices with their start and end apart: 5, of which 4 were waited for; matrix products, arithmetic and copies ran while one was open for 1% of the time, Pallas kernels for 0%

commit v1 on v0

v1 whole, which is shorter than its diff:
```python
import functools
import math

import jax
import jax.numpy as jnp
from jax import lax
from jax.experimental import pallas as pl
from jax.experimental.pallas import tpu as pltpu
from jax.sharding import PartitionSpec as P

LATS = 448
LONS = 896
MODES = 128
BLOCKS = 8
BLOCK_W = 96
PARTS = 2
DELAY = 2
LANES = 128
VMEM = 58 * 1024 * 1024
F32 = jnp.float32
BF16 = jnp.bfloat16


def trig_rows(row_ids, col_ids, period):
    phase = (row_ids[:, None] * col_ids[None, :] % period).astype(F32) * (2.0 * math.pi / period)
    factor = 1.0 / math.sqrt(period)
    return (
        (jnp.cos(phase) * factor).astype(BF16),
        (jnp.sin(phase) * factor).astype(BF16),
    )


def gelu_pair(value):
    cdf = 0.5 * (1.0 + lax.erf(value * 0.7071067811865476))
    density = jnp.exp(-0.5 * value * value) * 0.3989422804014327
    return (value * cdf, cdf + value * density)


def dot(left, right, left_dim=1, right_dim=0):
    return lax.dot_general(
        left, right, (((left_dim,), (right_dim,)), ((), ())), preferred_element_type=F32
    )


def params():
    return pltpu.CompilerParams(vmem_limit_bytes=VMEM)


def hop_body(t, row_block, has_recv, has_prev, has_final, scal, *refs):
    refs = list(refs)
    up_in, down_in = refs[0:5], refs[5:10]
    at = 10
    recv_up = recv_down = None
    if has_recv:
        recv_up, recv_down = refs[at : at + 2]
        at += 2
    if has_prev:
        at += 1
    up_out, down_out = refs[at : at + 2]
    at += 2
    final = None
    if has_final:
        final = refs[at]
        at += 1
    up_sum, down_sum = refs[at : at + 2]
    step = pl.program_id(0)
    sub, _, half = up_in[0].shape
    coefs = up_out.shape[0]
    tiles = half // LANES
    for column, (fields, cot, fields_other, cot_other, table), total in (
        (0, up_in, up_sum),
        (3, down_in, down_sum),
    ):
        def work(mine, other, table=table, total=total):
            own_table = table[0, 0, 0, 0]
            other_table = table[0, 0, 0, 1]
            for h in range(sub):
                value = dot(own_table, mine[h]) + dot(other_table, other[h])
                for j in range(tiles):
                    total[j, pl.ds(step * sub + h, coefs, stride=row_block), :] = value[
                        :, j * LANES : (j + 1) * LANES
                    ]

        pl.when(scal[t, column] == 0)(functools.partial(work, fields, fields_other))
        pl.when(scal[t, column] != 0)(functools.partial(work, cot, cot_other))

    @pl.when(step == pl.num_programs(0) - 1)
    def _():
        for total, recv, out in ((up_sum, recv_up, up_out), (down_sum, recv_down, down_out)):
            for j in range(tiles):
                lanes = pl.ds(j * LANES, LANES)
                value = total[j].reshape(coefs, row_block, LANES)
                if has_recv:
                    value = value + recv[:, :, lanes].astype(F32)
                out[:, :, lanes] = value.astype(BF16)
        if has_final:
            @pl.when(scal[t, 7] == 0)
            def _():
                final[...] = down_out[...]

            @pl.when(scal[t, 7] != 0)
            def _():
                final[...] = up_out[...]


def hop(t, scal, arrays, tables, recv, prev, final_at, row_block, rows):
    fields, cot, fields_other, cot_other = arrays
    cols = fields.shape[1]
    half = fields_other.shape[2]
    coefs = tables.shape[4]
    sub = 4
    steps = row_block // sub
    has_final = final_at is not None
    once = pl.Buffered(1)

    def mine(column):
        return pl.BlockSpec(
            (sub, cols, half), lambda i, s: (s[t, column + 1] * steps + i, 0, s[t, 6])
        )

    def other(column):
        return pl.BlockSpec((sub, cols, half), lambda i, s: (s[t, column + 1] * steps + i, 0, 0))

    def table(column, end):
        return pl.BlockSpec(
            (1, 1, 1, 2, coefs, cols),
            lambda i, s: (s[t, column + 2], s[t, column], end, 0, 0, 0),
            pipeline_mode=once,
        )

    piece = pl.BlockSpec((coefs, row_block, half), lambda i, s: (0, 0, 0), pipeline_mode=once)
    in_specs = []
    operands = []
    for column, end in ((0, 1), (3, 0)):
        in_specs += [mine(column), mine(column), other(column), other(column), table(column, end)]
        operands += [fields, cot, fields_other, cot_other, tables]
    if recv is not None:
        in_specs += [piece, piece]
        operands += list(recv)
    aliases = {}
    if prev is not None:
        in_specs.append(pl.BlockSpec(memory_space=pl.ANY))
        aliases[1 + len(operands)] = 2
        operands.append(prev)
    out_shape = [jax.ShapeDtypeStruct((coefs, row_block, half), BF16)] * 2
    out_specs = [piece, piece]
    if has_final:
        out_shape.append(jax.ShapeDtypeStruct((coefs, rows, half), BF16))
        out_specs.append(
            pl.BlockSpec((coefs, row_block, half), lambda i, s: (0, final_at, 0))
        )
    chunk = pltpu.VMEM((half // LANES, coefs * row_block, LANES), F32)
    return pl.pallas_call(
        functools.partial(
            hop_body, t, row_block, recv is not None, prev is not None, has_final
        ),
        grid_spec=pltpu.PrefetchScalarGridSpec(
            num_scalar_prefetch=1,
            grid=(steps,),
            in_specs=in_specs,
            out_specs=out_specs,
            scratch_shapes=[chunk, chunk],
        ),
        out_shape=out_shape,
        input_output_aliases=aliases,
        compiler_params=params(),
        cost_estimate=pl.CostEstimate(
            flops=8 * row_block * coefs * cols * half,
            bytes_accessed=16 * row_block * cols * half,
            transcendentals=0,
        ),
        name="longitude_hop",
    )(scal, *operands)


def filter_body(
    spectrum, pulled, forward, backward, inner, inner_t, outer_t,
    adjoint, inner_gradient, outer_gradient, stack, z, back, hidden, u_adj,
):
    bands, _, _, rows, half = spectrum.shape
    lats = bands * rows
    tile = lats // 4

    @pl.when(pl.program_id(0) == 0)
    def _():
        inner_gradient[...] = jnp.zeros_like(inner_gradient)
        outer_gradient[...] = jnp.zeros_like(outer_gradient)

    for source, target in ((spectrum, z), (pulled, back)):
        for part in range(2):
            for band in range(bands):
                first = part * lats + band * rows
                stack[first : first + rows, :] = source[band, part, 0]
        for part in range(2):
            @pl.loop(0, 2)
            def _(i, part=part, target=target):
                at = pl.multiple_of(i * 2 * tile, 16)
                value = dot(forward[pl.ds(part * lats + at, 2 * tile), :], stack[...])
                target[pl.ds(at, 2 * tile), part * half : (part + 1) * half] = value.astype(BF16)

    @pl.loop(0, 4)
    def _(i):
        at = pl.ds(pl.multiple_of(i * tile, 16), tile)
        gelu, slope = gelu_pair(dot(z[at, :], inner[...]))
        hidden[at, :] = gelu.astype(BF16)
        u_adj[at, :] = (dot(back[at, :], outer_t[...]) * slope).astype(BF16)
        z_adj = dot(u_adj[at, :], inner_t[...]).astype(BF16)
        for part in range(2):
            where = pl.ds(pl.multiple_of(part * lats + i * tile, 16), tile)
            stack[where, :] = z_adj[:, part * half : (part + 1) * half]

    outer_gradient[...] += dot(hidden[...], back[...], 0, 0)
    inner_gradient[...] += dot(z[...], u_adj[...], 0, 0)
    for part in range(2):
        for band in range(bands):
            first = part * lats + band * rows
            value = dot(backward[first : first + rows, :], stack[...])
            adjoint[band, part, 0] = value.astype(BF16)


def spectral_filter(spectrum, pulled, forward, backward, inner, inner_t, outer_t):
    bands, _, modes, rows, half = spectrum.shape
    lats = bands * rows
    wide = 2 * half
    data = pl.BlockSpec((bands, 2, 1, rows, half), lambda i: (0, 0, i, 0, 0))

    def whole(*shape):
        return pl.BlockSpec(shape, lambda i: (0,) * len(shape), pipeline_mode=pl.Buffered(1))

    square = whole(2 * lats, 2 * lats)
    weight = whole(wide, wide)
    return pl.pallas_call(
        filter_body,
        grid=(modes,),
        in_specs=[data, data, square, square, weight, weight, weight],
        out_specs=[data, weight, weight],
        out_shape=[
            jax.ShapeDtypeStruct(spectrum.shape, BF16),
            jax.ShapeDtypeStruct((wide, wide), F32),
            jax.ShapeDtypeStruct((wide, wide), F32),
        ],
        scratch_shapes=[
            pltpu.VMEM((2 * lats, half), BF16),
            pltpu.VMEM((lats, wide), BF16),
            pltpu.VMEM((lats, wide), BF16),
            pltpu.VMEM((lats, wide), BF16),
            pltpu.VMEM((lats, wide), BF16),
        ],
        compiler_params=params(),
        cost_estimate=pl.CostEstimate(
            flops=modes * 2 * (3 * 4 * lats * lats * half + 5 * lats * wide * wide),
            bytes_accessed=6 * modes * 2 * lats * half,
            transcendentals=modes * 2 * lats * half * 2,
        ),
        name="spectral_filter",
    )(spectrum, pulled, forward, backward, inner, inner_t, outer_t)


def relay_body(t, has_own, has_recv, has_prev, scal, *refs):
    refs = list(refs)
    own = refs.pop(0) if has_own else None
    recv = (refs.pop(0), refs.pop(0)) if has_recv else None
    if has_prev:
        refs = refs[2:]
    sends, kept = refs[0:2], refs[2:4]
    for way in range(2):
        def put(value, way=way):
            sends[way][...] = value[...]
            kept[way][0] = value[...]

        if own is None:
            put(recv[way])
        elif recv is None:
            put(own)
        else:
            pl.when(scal[t, 2 + way] != 0)(functools.partial(put, own))
            pl.when(scal[t, 2 + way] == 0)(functools.partial(put, recv[way]))


def relay(t, scal, own, own_at, recv, prev, count, shape):
    coefs, row_block, half = shape
    piece = pl.BlockSpec(shape, lambda i, s: (0, 0, 0))
    in_specs, operands = [], []
    if own is not None:
        in_specs.append(pl.BlockSpec(shape, lambda i, s: (0, own_at, 0)))
        operands.append(own)
    if recv is not None:
        in_specs += [piece, piece]
        operands += list(recv)
    aliases = {}
    if prev is not None:
        for i, array in enumerate(prev):
            aliases[1 + len(operands)] = 2 + i
            in_specs.append(pl.BlockSpec(memory_space=pl.ANY))
            operands.append(array)

    def kept(way):
        return pl.BlockSpec((1,) + shape, lambda i, s: (s[t, way], 0, 0, 0))

    return pl.pallas_call(
        functools.partial(relay_body, t, own is not None, recv is not None, prev is not None),
        grid_spec=pltpu.PrefetchScalarGridSpec(
            num_scalar_prefetch=1,
            grid=(1,),
            in_specs=in_specs,
            out_specs=[piece, piece, kept(0), kept(1)],
        ),
        out_shape=[jax.ShapeDtypeStruct(shape, BF16)] * 2
        + [jax.ShapeDtypeStruct((count + 1,) + shape, BF16)] * 2,
        input_output_aliases=aliases,
        compiler_params=params(),
        cost_estimate=pl.CostEstimate(
            flops=0, bytes_accessed=8 * coefs * row_block * half, transcendentals=0
        ),
        name="relay",
    )(scal, *operands)


def grid_body(core, *refs):
    pieces, panels, (own_out, other_out, *totals) = (
        refs[: 2 * PARTS], refs[2 * PARTS], refs[2 * PARTS + 1 :]
    )
    _, coefs, row_block, half = pieces[0].shape
    tiles = half // LANES
    for total, piece in zip(totals, pieces):
        for j in range(tiles):
            value = piece[0, :, :, pl.ds(j * LANES, LANES)].astype(F32)
            total[j] = value.reshape(coefs * row_block, LANES)
    for h in range(row_block):
        rows = [
            jnp.concatenate(
                [total[j, pl.ds(h, coefs, stride=row_block), :] for j in range(tiles)], axis=1
            ).astype(BF16)
            for total in totals
        ]
        value = jnp.concatenate(rows, axis=0)
        own_out[h] = dot(panels[0], value).astype(BF16)
        other_out[h] = dot(panels[1], value).astype(BF16)


def to_grid(core, kept, panels, rows, width):
    _, coefs, row_block, half = kept[0].shape
    blocks = rows // row_block
    cols = panels.shape[1]

    def piece(part):
        return pl.BlockSpec(
            (1, coefs, row_block, half), lambda i, s: (part * blocks + i, 0, 0, 0)
        )

    total = pltpu.VMEM((half // LANES, coefs * row_block, LANES), F32)
    return pl.pallas_call(
        grid_body,
        grid_spec=pltpu.PrefetchScalarGridSpec(
            num_scalar_prefetch=1,
            grid=(blocks,),
            in_specs=[piece(part) for _ in range(2) for part in range(PARTS)]
            + [pl.BlockSpec(panels.shape, lambda i, s: (0, 0, 0))],
            out_specs=[
                pl.BlockSpec((row_block, cols, half), lambda i, s: (i, 0, s[0])),
                pl.BlockSpec((row_block, cols, half), lambda i, s: (i, 0, 0)),
            ],
            scratch_shapes=[total] * (2 * PARTS),
        ),
        out_shape=[
            jax.ShapeDtypeStruct((rows, cols, width), BF16),
            jax.ShapeDtypeStruct((rows, cols, half), BF16),
        ],
        compiler_params=params(),
        cost_estimate=pl.CostEstimate(
            flops=8 * PARTS * rows * coefs * cols * half,
            bytes_accessed=4 * (PARTS * coefs + cols) * rows * half,
            transcendentals=0,
        ),
        name="longitude_grid",
    )(core, *[array for array in kept for _ in range(PARTS)], panels)


def place_body(core, piece, whole, out):
    out[...] = piece[...]


def place(core, piece, whole, row_block):
    rows, cols, half = piece.shape
    return pl.pallas_call(
        place_body,
        grid_spec=pltpu.PrefetchScalarGridSpec(
            num_scalar_prefetch=1,
            grid=(rows // row_block,),
            in_specs=[
                pl.BlockSpec((row_block, cols, half), lambda i, s: (i, 0, 0)),
                pl.BlockSpec(memory_space=pl.ANY),
            ],
            out_specs=pl.BlockSpec((row_block, cols, half), lambda i, s: (i, 0, 1 - s[0])),
        ),
        out_shape=jax.ShapeDtypeStruct(whole.shape, BF16),
        input_output_aliases={2: 0},
        compiler_params=params(),
        name="place",
    )(core, piece, whole)


def block_diagonal(blocks):
    count, size, _ = blocks.shape
    eye = jnp.eye(count, dtype=blocks.dtype)
    wide = blocks[:, :, None, :] * eye[:, None, :, None]
    return wide.reshape(count * size, count * size)


def complex_weight(weight):
    real = block_diagonal(weight[:, 0])
    imag = block_diagonal(weight[:, 1])
    return jnp.concatenate(
        [
            jnp.concatenate([real, imag], axis=1),
            jnp.concatenate([-imag, real], axis=1),
        ],
        axis=0,
    )


def gradient_blocks(total, half):
    real = total[:half, :half] + total[half:, half:]
    imag = total[:half, half:] - total[half:, :half]
    parts = []
    for b in range(half // BLOCK_W):
        at = slice(b * BLOCK_W, (b + 1) * BLOCK_W)
        parts.append(jnp.stack([real[at, at], imag[at, at]], axis=0))
    return jnp.stack(parts, axis=0)


def local(fields, cotangent, inner_weight, outer_weight):
    lat_count = lax.axis_size("lat")
    lon_count = lax.axis_size("lon")
    rows, cols, width = fields.shape
    chips = lon_count // 2
    half = width // 2
    lon = lax.axis_index("lon")
    chip = lon // 2
    core = lon % 2
    row_block = 16 if rows % 16 == 0 else 8
    blocks = rows // row_block
    per_end = MODES // 2
    per_group = per_end // lat_count
    per_part = per_group // PARTS
    coefs = lat_count * 2 * per_part
    swap = [(i, i ^ 1) for i in range(lon_count)]
    upward = [(i, i + 2) for i in range(lon_count - 2)]
    downward = [(i + 2, i) for i in range(lon_count - 2)]

    def other_half(array):
        return lax.dynamic_slice_in_dim(array, (1 - core) * half, half, axis=2)

    fields_other = lax.ppermute(other_half(fields), "lon", swap)
    cot_other = lax.ppermute(other_half(cotangent), "lon", swap)

    q = jnp.arange(coefs, dtype=jnp.int32)
    part_of = q // per_part % 2
    ids = q // (2 * per_part) * per_group + q % per_part
    ends = jnp.arange(2, dtype=jnp.int32)[:, None, None] * per_end
    pieces = jnp.arange(PARTS, dtype=jnp.int32)[None, :, None] * per_part
    mode_ids = (ends + pieces + ids).reshape(-1)
    imag_row = jnp.tile(part_of, 2 * PARTS) == 1
    places = jnp.concatenate(
        [lon * cols + jnp.arange(cols, dtype=jnp.int32),
         (lon ^ 1) * cols + jnp.arange(cols, dtype=jnp.int32)]
    )
    cos_rows, sin_rows = trig_rows(mode_ids, places, LONS)
    base = jnp.where(imag_row[:, None], -sin_rows, cos_rows)
    weights = jnp.where(mode_ids == 0, 1.0, 2.0).astype(BF16)
    both = jnp.stack([base, base * weights[:, None]], axis=0)
    tables = both.reshape(2, 2, PARTS, coefs, 2, cols).transpose(2, 0, 1, 4, 3, 5)
    panels = base.T.reshape(2, cols, 2 * PARTS * coefs)

    lat_ids = jnp.arange(LATS, dtype=jnp.int32)
    lat_cos, lat_sin = trig_rows(lat_ids, lat_ids, LATS)
    forward = jnp.concatenate(
        [jnp.concatenate([lat_cos, lat_sin], axis=1),
         jnp.concatenate([-lat_sin, lat_cos], axis=1)], axis=0
    )
    backward = jnp.concatenate(
        [jnp.concatenate([lat_cos, -lat_sin], axis=1),
         jnp.concatenate([lat_sin, lat_cos], axis=1)], axis=0
    )
    own_blocks = half // BLOCK_W
    inner = complex_weight(
        lax.dynamic_slice_in_dim(inner_weight, core * own_blocks, own_blocks, axis=0)
    )
    outer = complex_weight(
        lax.dynamic_slice_in_dim(outer_weight, core * own_blocks, own_blocks, axis=0)
    )
    inner_t, outer_t = inner.T, outer.T

    order = [(s, a, r) for s in range(PARTS) for a in range(2) for r in range(blocks)]
    count = len(order)
    slots = count + DELAY * (chips - 1)
    slot_ids = jnp.arange(slots, dtype=jnp.int32)

    def schedule(late):
        v = jnp.clip(slot_ids - DELAY * late, 0, count - 1)
        return [v // blocks % 2, v % blocks, v // (2 * blocks)]

    flat = jnp.zeros_like(slot_ids)
    scal = jnp.stack(
        schedule(chip) + schedule(chips - 1 - chip) + [flat + core, flat + chip], axis=1
    )
    sent = {}
    gathered = {}
    for t in range(slots):
        v = t - DELAY * (chips - 1)
        early = t < blocks
        arrays = (
            fields,
            fields if early else cotangent,
            fields_other,
            fields_other if early else cot_other,
        )
        recv = sent.pop(t - DELAY, None)
        key, final_at, prev = None, None, None
        if v >= 0:
            key, final_at = order[v][:2], order[v][2]
            prev = gathered.get(key)
        result = hop(t, scal, arrays, tables, recv, prev, final_at, row_block, rows)
        if v >= 0:
            gathered[key] = result[2]
        if t < count + DELAY * (chips - 2):
            sent[t] = (
                lax.ppermute(result[0], "lon", upward),
                lax.ppermute(result[1], "lon", downward),
            )

    def across(array):
        return lax.all_to_all(array, "lat", split_axis=0, concat_axis=0, tiled=True)

    spread = []
    inner_total = outer_total = 0.0
    for s in range(PARTS):
        shape = (lat_count, 2, per_part, rows, half)
        adjoint, inner_part, outer_part = spectral_filter(
            across(gathered[s, 0]).reshape(shape),
            across(gathered[s, 1]).reshape(shape),
            forward, backward, inner, inner_t, outer_t,
        )
        inner_total = inner_total + inner_part
        outer_total = outer_total + outer_part
        spread.append(across(adjoint.reshape(coefs, rows, half)))
    at_end = (chip == 0) | (chip == chips - 1)
    sums = jnp.stack([gradient_blocks(inner_total, half), gradient_blocks(outer_total, half)])
    sums = jnp.where(at_end, sums, 0.0)
    empty = jnp.zeros((2, BLOCKS) + sums.shape[2:], F32)
    sums = lax.dynamic_update_slice_in_dim(empty, sums, core * own_blocks, axis=1)
    sums = lax.psum(sums, ("lat", "lon")) * (1.0 / math.sqrt(LATS * MODES))

    count = PARTS * blocks
    slots = count + DELAY * (chips - 1)
    slot_ids = jnp.arange(slots, dtype=jnp.int32)

    def place_of(late):
        v = slot_ids - DELAY * late
        return jnp.where((v >= 0) & (v < count), v, count)

    flat = jnp.zeros_like(slot_ids)
    scal = jnp.stack(
        [place_of(chip), place_of(chips - 1 - chip),
         flat + (chip == 0), flat + (chip == chips - 1)], axis=1
    ).astype(jnp.int32)
    sent = {}
    kept = None
    for t in range(slots):
        own, own_at = (spread[t // blocks], t % blocks) if t < count else (None, None)
        up, down, *kept = relay(
            t, scal, own, own_at, sent.pop(t - DELAY, None), kept, count,
            (coefs, row_block, half),
        )
        if t < count + DELAY * (chips - 2):
            sent[t] = (lax.ppermute(up, "lon", upward), lax.ppermute(down, "lon", downward))

    core_now = core.reshape(1).astype(jnp.int32)
    whole, for_other = to_grid(core_now, kept, panels, rows, width)
    field_gradient = place(core_now, lax.ppermute(for_other, "lon", swap), whole, row_block)
    return (field_gradient, sums[0], sums[1])


def solution(mesh):
    return jax.shard_map(
        local,
        mesh=mesh,
        in_specs=(P("lat", "lon", None), P("lat", "lon", None), P(), P()),
        out_specs=(P("lat", "lon", None), P(), P()),
        check_vma=False,
    )
```

time: 2290 us -> 1360 us (0.59)
  waiting for transfers between devices: 1410 us -> 367 us
  Pallas kernels: 0 us -> 613 us
  blocking collectives: 278 us -> 0 us
  local copies, waits for them, and re-layouts: 341 us -> 71.6 us
  starting transfers between devices: 19.3 us -> 251 us
  matrix products: 138 us -> 0 us
  other arithmetic: 80.1 us -> 22.9 us
    all_to_all x3 -> x6, waiting for transfers between devices: 994 us -> 0.02 us  [across(): return lax.all_to_all(array, 'lat', split_axis=0, concat_axis=0, tiled=True)]
    pallas_call x0 -> x58, Pallas kernels: none -> 613 us  [the longest x34 335 us: hop(): pl.pallas_call(functools.partial(hop_body, t, row_block, recv is not None...]
    psum x1, waiting for transfers between devices: 411 us -> 132 us  [local(): sums = lax.psum(sums, ('lat', 'lon')) * (1.0 / math.sqrt(LATS * MODES))]
    all_to_all x1 -> x0, blocking collectives: 278 us -> none  [local(): lax.all_to_all(spectra, 'lon', split_axis=1, concat_axis=0, tiled=True)]
    ppermute x0 -> x103, waiting for transfers between devices: none -> 235 us  [the longest x18 78.7 us: local(): lax.ppermute(down, 'lon', downward)]
    ppermute x0 -> x103, starting transfers between devices: none -> 220 us  [the longest x32 118 us: local(): lax.ppermute(result[0], 'lon', upward)]
    dot_general x24 -> x0, matrix products: 138 us -> none  [product(): return jnp.einsum(form, left, right, preferred_element_type=jnp.float32)]
    all_to_all x6 -> x0, local copies, waits for them, and re-layouts: 97.6 us -> none  [the longest x2 40.9 us: local(): lax.all_to_all(spectra, 'lon', split_axis=1, concat_axis=0, tiled=True)]
  transfers between devices with their start and end apart: 5 -> 110, of which waited for: 4 -> 66; matrix products, arithmetic and copies ran while one was open for 1% -> 3% of each run, Pallas kernels for 0% -> 41%
where the time goes in v1:
time: 1360 us; the launch traced here: 1340 us
  Pallas kernels  613 us (45%)
  waiting for transfers between devices  367 us (27%)
  starting transfers between devices  251 us (18%)
  local copies, waits for them, and re-layouts  71.6 us (5%)
  other arithmetic  22.9 us (2%)
  between operations  16.6 us (1%)
    pallas_call x34, Pallas kernels, hop(): pl.pallas_call(functools.partial(hop_body, t, row_block, recv is not None...  335 us
    pallas_call x2, Pallas kernels, spectral_filter(): pl.pallas_call(filter_body, grid=(modes,), in_specs=[data, data, square,...  150 us
    psum x1, waiting for transfers between devices, local(): sums = lax.psum(sums, ('lat', 'lon')) * (1.0 / math.sqrt(LATS * MODES))  132 us
    ppermute x32, starting transfers between devices, local(): lax.ppermute(result[0], 'lon', upward)  118 us
    pallas_call x20, Pallas kernels, relay(): pl.pallas_call(functools.partial(relay_body, t, own is not None, recv is...  85.1 us
    ppermute x18, waiting for transfers between devices, local(): lax.ppermute(down, 'lon', downward)  78.7 us
    ppermute x18, waiting for transfers between devices, local(): lax.ppermute(up, 'lon', upward)  66.2 us
    ppermute x32, waiting for transfers between devices, local(): lax.ppermute(result[1], 'lon', downward)  57.9 us
  transfers between devices with their start and end apart: 110, of which 66 were waited for; matrix products, arithmetic and copies ran while one was open for 3% of the time, Pallas kernels for 41%

profile of v1, /device:TPU:0, one launch (start us, length us, event | category | flops | bytes accessed | tf_op | source)
XLA Modules:
  0.0 1343.0 jit_solution(3041312818718281962)
XLA Ops:
  31.1 10.5 longitude_hop.34
  47.7 10.1 longitude_hop.38
  69.7 10.1 longitude_hop.35
  87.4 10.1 longitude_hop.39
  105.3 10.3 longitude_hop.36
  123.2 10.1 longitude_hop.40
  141.2 10.6 longitude_hop.37
  158.8 9.8 longitude_hop.41
  193.4 9.7 longitude_hop.43
  268.3 11.0 collective-permute-done.26.refs_10_
  299.1 9.8 longitude_hop.48
  315.9 9.7 longitude_hop.49
  332.9 9.8 longitude_hop.50
  350.4 9.7 longitude_hop.51
  367.2 9.7 longitude_hop.52
  380.1 9.7 longitude_hop.54
  405.8 11.0 collective-permute-done.36.refs_10_
  421.8 9.7 longitude_hop.53
  437.5 9.7 longitude_hop.55
  473.7 9.7 longitude_hop.57
  555.1 9.8 longitude_hop.61
  571.7 9.7 longitude_hop.62
  588.8 9.8 longitude_hop.63
  606.3 9.8 longitude_hop.64
  623.4 9.9 longitude_hop.65
  641.5 9.7 longitude_hop.66
  652.4 10.6 longitude_hop.67
  683.0 75.2 %spectral_filter.3 = (bf16[4,2,8,112,384]{4,3,2,1,0:T(8,128)(2,1)}, f32[768,768]{1,0:T(8,128)}, f32[768,768]{1,0:T(8,128)}) custom-call(bf16[4,2,8,112,384]{4,3,2,1,0:T(8,128)(2,1)} %bitcast.11.spectrum, bf16[4,2,8,112,384]{4,3,2,1,0:T(8,128)(2,1)} %bitcast.12.pulled, bf16[896,896]{1,0:T(8,128)(2,1)} %get-tuple-element.362.forward, ...), custom_call_target="tpu_custom_call" | custom-call | flops 35936796672 | bytes 16515072 | tf_op jit(solution)/shard_map/spectral_filter/pallas_call | solution.py:232
  763.6 75.3 %spectral_filter.2 = (bf16[4,2,8,112,384]{4,3,2,1,0:T(8,128)(2,1)}, f32[768,768]{1,0:T(8,128)}, f32[768,768]{1,0:T(8,128)}) custom-call(bf16[4,2,8,112,384]{4,3,2,1,0:T(8,128)(2,1)} %bitcast.2.spectrum, bf16[4,2,8,112,384]{4,3,2,1,0:T(8,128)(2,1)} %bitcast.3.pulled, bf16[896,896]{1,0:T(8,128)(2,1)} %get-tuple-element.362.forward, ...), custom_call_target="tpu_custom_call" | custom-call | flops 35936796672 | bytes 16515072 | tf_op jit(solution)/shard_map/spectral_filter/pallas_call | solution.py:232
  1151.7 32.7 %longitude_grid.1 = (bf16[112,112,768]{2,1,0:T(8,128)(2,1)}, bf16[112,112,384]{2,1,0:T(8,128)(2,1)}) custom-call(s32[1]{0:T(128)} %bitcast.core, bf16[15,64,16,384]{3,2,1,0:T(8,128)(2,1)} %get-tuple-element.347.refs_0_.refs_1_, bf16[15,64,16,384]{3,2,1,0:T(8,128)(2,1)} %get-tuple-element.347.refs_0_.refs_1_, ...), custom_call_target="tpu_custom_call" | custom-call | flops 4932501504 | bytes 41287680 | tf_op jit(solution)/shard_map/longitude_grid/pallas_call | solution.py:352
  1190.8 131.8 %all-reduce.2.cloned.1.call-done = f32[2,8,2,96,96]{4,3,2,1,0:T(8,128)} async-done(((f32[2,8,2,96,96]{4,3,2,1,0:T(8,128)}), f32[2,8,2,96,96]{4,3,2,1,0:T(8,128)}) %all-reduce.2.cloned.1.call-update) | async-done | bytes 1179664 | tf_op jit(solution)/shard_map/psum | solution.py:552
  1325.5 10.1 place.1
  (552 shorter events, 731.4 us)
Async XLA Ops:
  24.5 133.2 %collective-permute-start.1 = (bf16[112,112,384]{2,1,0:T(8,128)(2,1)}, bf16[112,112,384]{2,1,0:T(8,128)(2,1)}, u32[]{:S(2)}, u32[]{:S(2)}) collective-permute-start(bf16[112,112,384]{2,1,0:T(8,128)(2,1)} %constant_dynamic-slice_fusion), channel_id=1, source_target_pairs={{0,1},{1,0},{2,3},{3,2},{4,5},{5,4},{6,7},{7,6},{8,9},{9,8},{10,11... | collective-permute-start | bytes 28901384 | tf_op jit(solution)/shard_map/ppermute | solution.py:455
  57.8 27.8 %collective-permute-start.10 = (bf16[64,16,384]{2,1,0:T(8,128)(2,1)}, bf16[64,16,384]{2,1,0:T(8,128)(2,1)S(1)}, u32[]{:S(2)}, u32[]{:S(2)}) collective-permute-start(bf16[64,16,384]{2,1,0:T(8,128)(2,1)} %get-tuple-element.187), channel_id=1, source_target_pairs={{0,2},{1,3},{2,4},{3,5},{4,6},{5,7},{8,10},{9,11},{10,12},{11,13},... | collective-permute-start | bytes 2359304 | tf_op jit(solution)/shard_map/ppermute | solution.py:528
  252.3 137.5 %all-to-all-start.3 = ((bf16[64,112,384]{2,1,0:T(8,128)(2,1)}), bf16[64,112,384]{2,1,0:T(8,128)(2,1)}, u32[]{:S(2)}, u32[]{:S(2)}) async-start(bf16[64,112,384]{2,1,0:T(8,128)(2,1)} %get-tuple-element.270), calls=%async_computation.3 | async-start | bytes 11010048 | tf_op jit(solution)/shard_map/all_to_all | solution.py:533
  262.4 35.6 %collective-permute-start.24 = (bf16[64,16,384]{2,1,0:T(8,128)(2,1)S(1)}, bf16[64,16,384]{2,1,0:T(8,128)(2,1)S(1)}, u32[]{:S(2)}, u32[]{:S(2)}) collective-permute-start(bf16[64,16,384]{2,1,0:T(8,128)(2,1)S(1)} %copy-done.112), channel_id=1, source_target_pairs={{0,2},{1,3},{2,4},{3,5},{4,6},{5,7},{8,10},{9,11},{10,12},{11,13},... | collective-permute-start | bytes 2359304 | tf_op jit(solution)/shard_map/ppermute | solution.py:528
  267.0 31.0 %collective-permute-start.25 = (bf16[64,16,384]{2,1,0:T(8,128)(2,1)S(1)}, bf16[64,16,384]{2,1,0:T(8,128)(2,1)S(1)}, u32[]{:S(2)}, u32[]{:S(2)}) collective-permute-start(bf16[64,16,384]{2,1,0:T(8,128)(2,1)S(1)} %copy-done.111), channel_id=1, source_target_pairs={{2,0},{3,1},{4,2},{5,3},{6,4},{7,5},{10,8},{11,9},{12,10},{13,11},... | collective-permute-start | bytes 2359304 | tf_op jit(solution)/shard_map/ppermute | solution.py:529
  389.9 138.5 %all-to-all-start.4 = ((bf16[64,112,384]{2,1,0:T(8,128)(2,1)}), bf16[64,112,384]{2,1,0:T(8,128)(2,1)}, u32[]{:S(2)}, u32[]{:S(2)}) async-start(bf16[64,112,384]{2,1,0:T(8,128)(2,1)} %get-tuple-element.271), calls=%async_computation.4 | async-start | bytes 11010048 | tf_op jit(solution)/shard_map/all_to_all | solution.py:533
  399.9 35.1 %collective-permute-start.42 = (bf16[64,16,384]{2,1,0:T(8,128)(2,1)S(1)}, bf16[64,16,384]{2,1,0:T(8,128)(2,1)S(1)}, u32[]{:S(2)}, u32[]{:S(2)}) collective-permute-start(bf16[64,16,384]{2,1,0:T(8,128)(2,1)S(1)} %copy-done.109), channel_id=1, source_target_pairs={{0,2},{1,3},{2,4},{3,5},{4,6},{5,7},{8,10},{9,11},{10,12},{11,13},... | collective-permute-start | bytes 2359304 | tf_op jit(solution)/shard_map/ppermute | solution.py:528
  404.5 32.2 %collective-permute-start.43 = (bf16[64,16,384]{2,1,0:T(8,128)(2,1)S(1)}, bf16[64,16,384]{2,1,0:T(8,128)(2,1)S(1)}, u32[]{:S(2)}, u32[]{:S(2)}) collective-permute-start(bf16[64,16,384]{2,1,0:T(8,128)(2,1)S(1)} %copy-done.107), channel_id=1, source_target_pairs={{2,0},{3,1},{4,2},{5,3},{6,4},{7,5},{10,8},{11,9},{12,10},{13,11},... | collective-permute-start | bytes 2359304 | tf_op jit(solution)/shard_map/ppermute | solution.py:529
  528.4 134.7 %all-to-all-start = ((bf16[64,112,384]{2,1,0:T(8,128)(2,1)}), bf16[64,112,384]{2,1,0:T(8,128)(2,1)}, u32[]{:S(2)}, u32[]{:S(2)}) async-start(bf16[64,112,384]{2,1,0:T(8,128)(2,1)} %get-tuple-element.247), calls=%async_computation | async-start | bytes 11010048 | tf_op jit(solution)/shard_map/all_to_all | solution.py:533
  537.1 31.3 %collective-permute-start.56 = (bf16[64,16,384]{2,1,0:T(8,128)(2,1)S(1)}, bf16[64,16,384]{2,1,0:T(8,128)(2,1)S(1)}, u32[]{:S(2)}, u32[]{:S(2)}) collective-permute-start(bf16[64,16,384]{2,1,0:T(8,128)(2,1)S(1)} %copy-done.110), channel_id=1, source_target_pairs={{0,2},{1,3},{2,4},{3,5},{4,6},{5,7},{8,10},{9,11},{10,12},{11,13},... | collective-permute-start | bytes 2359304 | tf_op jit(solution)/shard_map/ppermute | solution.py:528
  541.7 29.1 %collective-permute-start.57 = (bf16[64,16,384]{2,1,0:T(8,128)(2,1)S(1)}, bf16[64,16,384]{2,1,0:T(8,128)(2,1)S(1)}, u32[]{:S(2)}, u32[]{:S(2)}) collective-permute-start(bf16[64,16,384]{2,1,0:T(8,128)(2,1)S(1)} %copy-done.108), channel_id=1, source_target_pairs={{2,0},{3,1},{4,2},{5,3},{6,4},{7,5},{10,8},{11,9},{12,10},{13,11},... | collective-permute-start | bytes 2359304 | tf_op jit(solution)/shard_map/ppermute | solution.py:529
  663.1 95.2 %all-to-all-start.1 = ((bf16[64,112,384]{2,1,0:T(8,128)(2,1)}), bf16[64,112,384]{2,1,0:T(8,128)(2,1)}, u32[]{:S(2)}, u32[]{:S(2)}) async-start(bf16[64,112,384]{2,1,0:T(8,128)(2,1)} %get-tuple-element.268), calls=%async_computation.1 | async-start | bytes 11010048 | tf_op jit(solution)/shard_map/all_to_all | solution.py:533
  758.2 80.6 %all-to-all-start.5 = ((bf16[64,112,384]{2,1,0:T(8,128)(2,1)}), bf16[64,112,384]{2,1,0:T(8,128)(2,1)}, u32[]{:S(2)}, u32[]{:S(2)}) async-start(bf16[64,112,384]{2,1,0:T(8,128)(2,1)} %bitcast.88), calls=%async_computation.5 | async-start | bytes 11010048 | tf_op jit(solution)/shard_map/all_to_all | solution.py:533
  838.8 118.7 %all-to-all-start.2 = ((bf16[64,112,384]{2,1,0:T(8,128)(2,1)}), bf16[64,112,384]{2,1,0:T(8,128)(2,1)}, u32[]{:S(2)}, u32[]{:S(2)}) async-start(bf16[64,112,384]{2,1,0:T(8,128)(2,1)} %bitcast.87), calls=%async_computation.2 | async-start | bytes 11010048 | tf_op jit(solution)/shard_map/all_to_all | solution.py:533
  844.0 478.6 %all-reduce.2.cloned.1.call-start = ((), (), s32[]{:S(2)}) async-start(), calls=%async_computation.6 | async-start | bytes 3145728 | tf_op jit(solution)/shard_map/psum | solution.py:552
  858.1 27.4 %collective-permute-start.66 = (bf16[64,16,384]{2,1,0:T(8,128)(2,1)}, bf16[64,16,384]{2,1,0:T(8,128)(2,1)S(1)}, u32[]{:S(2)}, u32[]{:S(2)}) collective-permute-start(bf16[64,16,384]{2,1,0:T(8,128)(2,1)} %get-tuple-element.275), channel_id=1, source_target_pairs={{0,2},{1,3},{2,4},{3,5},{4,6},{5,7},{8,10},{9,11},{10,12},{11,13},... | collective-permute-start | bytes 2359304 | tf_op jit(solution)/shard_map/ppermute | solution.py:576
  862.8 27.3 %collective-permute-start.67 = (bf16[64,16,384]{2,1,0:T(8,128)(2,1)}, bf16[64,16,384]{2,1,0:T(8,128)(2,1)S(1)}, u32[]{:S(2)}, u32[]{:S(2)}) collective-permute-start(bf16[64,16,384]{2,1,0:T(8,128)(2,1)} %get-tuple-element.276), channel_id=1, source_target_pairs={{2,0},{3,1},{4,2},{5,3},{6,4},{7,5},{10,8},{11,9},{12,10},{13,11},... | collective-permute-start | bytes 2359304 | tf_op jit(solution)/shard_map/ppermute | solution.py:576
  880.2 26.8 %collective-permute-start.73 = (bf16[64,16,384]{2,1,0:T(8,128)(2,1)}, bf16[64,16,384]{2,1,0:T(8,128)(2,1)S(1)}, u32[]{:S(2)}, u32[]{:S(2)}) collective-permute-start(bf16[64,16,384]{2,1,0:T(8,128)(2,1)} %get-tuple-element.286), channel_id=1, source_target_pairs={{2,0},{3,1},{4,2},{5,3},{6,4},{7,5},{10,8},{11,9},{12,10},{13,11},... | collective-permute-start | bytes 2359304 | tf_op jit(solution)/shard_map/ppermute | solution.py:576
  897.0 26.8 %collective-permute-start.71 = (bf16[64,16,384]{2,1,0:T(8,128)(2,1)}, bf16[64,16,384]{2,1,0:T(8,128)(2,1)S(1)}, u32[]{:S(2)}, u32[]{:S(2)}) collective-permute-start(bf16[64,16,384]{2,1,0:T(8,128)(2,1)} %get-tuple-element.284), channel_id=1, source_target_pairs={{2,0},{3,1},{4,2},{5,3},{6,4},{7,5},{10,8},{11,9},{12,10},{13,11},... | collective-permute-start | bytes 2359304 | tf_op jit(solution)/shard_map/ppermute | solution.py:576
  913.9 26.7 %collective-permute-start.77 = (bf16[64,16,384]{2,1,0:T(8,128)(2,1)}, bf16[64,16,384]{2,1,0:T(8,128)(2,1)S(1)}, u32[]{:S(2)}, u32[]{:S(2)}) collective-permute-start(bf16[64,16,384]{2,1,0:T(8,128)(2,1)} %get-tuple-element.294), channel_id=1, source_target_pairs={{2,0},{3,1},{4,2},{5,3},{6,4},{7,5},{10,8},{11,9},{12,10},{13,11},... | collective-permute-start | bytes 2359304 | tf_op jit(solution)/shard_map/ppermute | solution.py:576
  930.8 26.8 %collective-permute-start.75 = (bf16[64,16,384]{2,1,0:T(8,128)(2,1)}, bf16[64,16,384]{2,1,0:T(8,128)(2,1)S(1)}, u32[]{:S(2)}, u32[]{:S(2)}) collective-permute-start(bf16[64,16,384]{2,1,0:T(8,128)(2,1)} %get-tuple-element.292), channel_id=1, source_target_pairs={{2,0},{3,1},{4,2},{5,3},{6,4},{7,5},{10,8},{11,9},{12,10},{13,11},... | collective-permute-start | bytes 2359304 | tf_op jit(solution)/shard_map/ppermute | solution.py:576
  947.7 26.7 %collective-permute-start.81 = (bf16[64,16,384]{2,1,0:T(8,128)(2,1)}, bf16[64,16,384]{2,1,0:T(8,128)(2,1)S(1)}, u32[]{:S(2)}, u32[]{:S(2)}) collective-permute-start(bf16[64,16,384]{2,1,0:T(8,128)(2,1)} %get-tuple-element.302), channel_id=1, source_target_pairs={{2,0},{3,1},{4,2},{5,3},{6,4},{7,5},{10,8},{11,9},{12,10},{13,11},... | collective-permute-start | bytes 2359304 | tf_op jit(solution)/shard_map/ppermute | solution.py:576
  964.5 26.8 %collective-permute-start.79 = (bf16[64,16,384]{2,1,0:T(8,128)(2,1)}, bf16[64,16,384]{2,1,0:T(8,128)(2,1)S(1)}, u32[]{:S(2)}, u32[]{:S(2)}) collective-permute-start(bf16[64,16,384]{2,1,0:T(8,128)(2,1)} %get-tuple-element.300), channel_id=1, source_target_pairs={{2,0},{3,1},{4,2},{5,3},{6,4},{7,5},{10,8},{11,9},{12,10},{13,11},... | collective-permute-start | bytes 2359304 | tf_op jit(solution)/shard_map/ppermute | solution.py:576
  981.3 26.8 %collective-permute-start.85 = (bf16[64,16,384]{2,1,0:T(8,128)(2,1)}, bf16[64,16,384]{2,1,0:T(8,128)(2,1)S(1)}, u32[]{:S(2)}, u32[]{:S(2)}) collective-permute-start(bf16[64,16,384]{2,1,0:T(8,128)(2,1)} %get-tuple-element.310), channel_id=1, source_target_pairs={{2,0},{3,1},{4,2},{5,3},{6,4},{7,5},{10,8},{11,9},{12,10},{13,11},... | collective-permute-start | bytes 2359304 | tf_op jit(solution)/shard_map/ppermute | solution.py:576
  998.2 26.8 %collective-permute-start.83 = (bf16[64,16,384]{2,1,0:T(8,128)(2,1)}, bf16[64,16,384]{2,1,0:T(8,128)(2,1)S(1)}, u32[]{:S(2)}, u32[]{:S(2)}) collective-permute-start(bf16[64,16,384]{2,1,0:T(8,128)(2,1)} %get-tuple-element.308), channel_id=1, source_target_pairs={{2,0},{3,1},{4,2},{5,3},{6,4},{7,5},{10,8},{11,9},{12,10},{13,11},... | collective-permute-start | bytes 2359304 | tf_op jit(solution)/shard_map/ppermute | solution.py:576
  1015.0 26.8 %collective-permute-start.89 = (bf16[64,16,384]{2,1,0:T(8,128)(2,1)}, bf16[64,16,384]{2,1,0:T(8,128)(2,1)S(1)}, u32[]{:S(2)}, u32[]{:S(2)}) collective-permute-start(bf16[64,16,384]{2,1,0:T(8,128)(2,1)} %get-tuple-element.318), channel_id=1, source_target_pairs={{2,0},{3,1},{4,2},{5,3},{6,4},{7,5},{10,8},{11,9},{12,10},{13,11},... | collective-permute-start | bytes 2359304 | tf_op jit(solution)/shard_map/ppermute | solution.py:576
  1031.9 26.7 %collective-permute-start.87 = (bf16[64,16,384]{2,1,0:T(8,128)(2,1)}, bf16[64,16,384]{2,1,0:T(8,128)(2,1)S(1)}, u32[]{:S(2)}, u32[]{:S(2)}) collective-permute-start(bf16[64,16,384]{2,1,0:T(8,128)(2,1)} %get-tuple-element.316), channel_id=1, source_target_pairs={{2,0},{3,1},{4,2},{5,3},{6,4},{7,5},{10,8},{11,9},{12,10},{13,11},... | collective-permute-start | bytes 2359304 | tf_op jit(solution)/shard_map/ppermute | solution.py:576
  1048.8 26.7 %collective-permute-start.93 = (bf16[64,16,384]{2,1,0:T(8,128)(2,1)}, bf16[64,16,384]{2,1,0:T(8,128)(2,1)S(1)}, u32[]{:S(2)}, u32[]{:S(2)}) collective-permute-start(bf16[64,16,384]{2,1,0:T(8,128)(2,1)} %get-tuple-element.326), channel_id=1, source_target_pairs={{2,0},{3,1},{4,2},{5,3},{6,4},{7,5},{10,8},{11,9},{12,10},{13,11},... | collective-permute-start | bytes 2359304 | tf_op jit(solution)/shard_map/ppermute | solution.py:576
  1065.6 26.8 %collective-permute-start.91 = (bf16[64,16,384]{2,1,0:T(8,128)(2,1)}, bf16[64,16,384]{2,1,0:T(8,128)(2,1)S(1)}, u32[]{:S(2)}, u32[]{:S(2)}) collective-permute-start(bf16[64,16,384]{2,1,0:T(8,128)(2,1)} %get-tuple-element.324), channel_id=1, source_target_pairs={{2,0},{3,1},{4,2},{5,3},{6,4},{7,5},{10,8},{11,9},{12,10},{13,11},... | collective-permute-start | bytes 2359304 | tf_op jit(solution)/shard_map/ppermute | solution.py:576
  1082.0 27.2 %collective-permute-start.97 = (bf16[64,16,384]{2,1,0:T(8,128)(2,1)}, bf16[64,16,384]{2,1,0:T(8,128)(2,1)S(1)}, u32[]{:S(2)}, u32[]{:S(2)}) collective-permute-start(bf16[64,16,384]{2,1,0:T(8,128)(2,1)} %get-tuple-element.334), channel_id=1, source_target_pairs={{2,0},{3,1},{4,2},{5,3},{6,4},{7,5},{10,8},{11,9},{12,10},{13,11},... | collective-permute-start | bytes 2359304 | tf_op jit(solution)/shard_map/ppermute | solution.py:576
  1098.9 27.1 %collective-permute-start.95 = (bf16[64,16,384]{2,1,0:T(8,128)(2,1)}, bf16[64,16,384]{2,1,0:T(8,128)(2,1)S(1)}, u32[]{:S(2)}, u32[]{:S(2)}) collective-permute-start(bf16[64,16,384]{2,1,0:T(8,128)(2,1)} %get-tuple-element.332), channel_id=1, source_target_pairs={{2,0},{3,1},{4,2},{5,3},{6,4},{7,5},{10,8},{11,9},{12,10},{13,11},... | collective-permute-start | bytes 2359304 | tf_op jit(solution)/shard_map/ppermute | solution.py:576
  1184.4 141.1 %collective-permute-start.102 = (bf16[112,112,384]{2,1,0:T(8,128)(2,1)}, bf16[112,112,384]{2,1,0:T(8,128)(2,1)}, u32[]{:S(2)}, u32[]{:S(2)}) collective-permute-start(bf16[112,112,384]{2,1,0:T(8,128)(2,1)} %get-tuple-element.349), channel_id=1, source_target_pairs={{0,1},{1,0},{2,3},{3,2},{4,5},{5,4},{6,7},{7,6},{8,9},{9,8},{10,11... | collective-permute-start | bytes 28901384 | tf_op jit(solution)/shard_map/ppermute | solution.py:580
  (194 other events, 1998.4 us)
Sparse Core Ops, SparseCore 0:
  1191.0 131.6 all-reduce.1

commit v2 on v1

v2 whole, which is shorter than its diff:
```python
import functools
import math

import jax
import jax.numpy as jnp
from jax import lax
from jax.experimental import pallas as pl
from jax.experimental.pallas import tpu as pltpu
from jax.sharding import PartitionSpec as P

LATS = 448
LONS = 896
MODES = 128
BLOCKS = 8
BLOCK_W = 96
PARTS = 2
PIECES = 4
CHUNK = 8
EARLY = (-10, -8, -6, -4)
LATE = (5, 7, 9, 11)
DELAY = 2
LANES = 128
VMEM = 62 * 1024 * 1024
F32 = jnp.float32
BF16 = jnp.bfloat16


def trig_rows(row_ids, col_ids, period):
    phase = (row_ids[:, None] * col_ids[None, :] % period).astype(F32) * (2.0 * math.pi / period)
    factor = 1.0 / math.sqrt(period)
    return (
        (jnp.cos(phase) * factor).astype(BF16),
        (jnp.sin(phase) * factor).astype(BF16),
    )


def gelu_pair(value):
    cdf = 0.5 * (1.0 + lax.erf(value * 0.7071067811865476))
    density = jnp.exp(-0.5 * value * value) * 0.3989422804014327
    return (value * cdf, cdf + value * density)


def dot(left, right, left_dim=1, right_dim=0):
    return lax.dot_general(
        left, right, (((left_dim,), (right_dim,)), ((), ())), preferred_element_type=F32
    )


def params():
    return pltpu.CompilerParams(vmem_limit_bytes=VMEM)


def hop_body(t, row_block, has_recv, has_prev, has_final, ties, scal, *refs):
    refs = list(refs)
    fields, cot, fields_other, cot_other, tables = refs[:5]
    at = 5
    recv = refs[at : at + 2] if has_recv else None
    at += 2 * has_recv + has_prev + ties
    outs = refs[at : at + 2]
    at += 2
    final = None
    if has_final is not None:
        final = refs[at]
        at += 1
    x, table, recv_now, total, out, x_sem, table_sem, recv_sem, out_sem, final_sem = refs[at:]
    half = x.shape[-1]
    coefs = out.shape[1]
    tiles = half // LANES
    part_rows = row_block // 2
    mine = pl.ds(pl.multiple_of(scal[t, 6] * half, LANES), half)

    def row_copy(way, who, part, array):
        first = scal[t, 3 * way + 1] * row_block + part * part_rows
        rows = pl.ds(first, part_rows)
        source = array.at[rows] if who else array.at[rows, :, mine]
        return pltpu.make_async_copy(
            source, x.at[way, who, pl.ds(part * part_rows, part_rows)], x_sem.at[way, who, part]
        )

    def table_copy(way):
        source = tables.at[scal[t, 3 * way + 2], scal[t, 3 * way], 1 - way]
        return pltpu.make_async_copy(source, table.at[way], table_sem.at[way])

    def recv_copy(way):
        return pltpu.make_async_copy(recv[way], recv_now.at[way], recv_sem.at[way])

    def out_copy(way):
        return pltpu.make_async_copy(out.at[way], outs[way], out_sem.at[way])

    def final_copy(way):
        target = final.at[:, pl.ds(has_final * row_block, row_block), :]
        return pltpu.make_async_copy(out.at[way], target, final_sem)

    for way in range(2):
        table_copy(way).start()
        for part in range(2):
            for which, pair in enumerate(((fields, fields_other), (cot, cot_other))):
                @pl.when((scal[t, 3 * way] != 0) if which else (scal[t, 3 * way] == 0))
                def _(way=way, part=part, pair=pair):
                    for who in range(2):
                        row_copy(way, who, part, pair[who]).start()
        if has_recv:
            recv_copy(way).start()
    for way in range(2):
        table_copy(way).wait()
        for part in range(2):
            for who in range(2):
                row_copy(way, who, part, (fields, fields_other)[who]).wait()
            for h in range(part * part_rows, (part + 1) * part_rows):
                value = dot(table[way, 0], x[way, 0, h]) + dot(table[way, 1], x[way, 1, h])
                for j in range(tiles):
                    total[j, pl.ds(h, coefs, stride=row_block), :] = value[
                        :, j * LANES : (j + 1) * LANES
                    ]
        if has_recv:
            recv_copy(way).wait()
        for j in range(tiles):
            lanes = pl.ds(j * LANES, LANES)
            value = total[j].reshape(coefs, row_block, LANES)
            if has_recv:
                value = value + recv_now[way, :, :, lanes].astype(F32)
            out[way, :, :, lanes] = value.astype(BF16)
        out_copy(way).start()
    if has_final is not None:
        pl.when(scal[t, 7] == 0)(lambda: final_copy(1).start())
        pl.when(scal[t, 7] != 0)(lambda: final_copy(0).start())
    for way in range(2):
        out_copy(way).wait()
    if has_final is not None:
        final_copy(0).wait()


def hop(t, scal, arrays, tables, recv, prev, final_at, row_block, rows, ties=()):
    fields, _, fields_other, _ = arrays
    cols = fields.shape[1]
    half = fields_other.shape[2]
    coefs = tables.shape[4]
    operands = list(arrays) + [tables]
    if recv is not None:
        operands += list(recv)
    aliases = {}
    if prev is not None:
        aliases[1 + len(operands)] = 2
        operands.append(prev)
    operands += list(ties)
    out_shape = [jax.ShapeDtypeStruct((coefs, row_block, half), BF16)] * 2
    if final_at is not None:
        out_shape.append(jax.ShapeDtypeStruct((coefs, rows, half), BF16))
    anywhere = pl.BlockSpec(memory_space=pl.ANY)
    piece = pltpu.VMEM((2, coefs, row_block, half), BF16)
    return pl.pallas_call(
        functools.partial(
            hop_body, t, row_block, recv is not None, prev is not None, final_at, len(ties)
        ),
        grid_spec=pltpu.PrefetchScalarGridSpec(
            num_scalar_prefetch=1,
            grid=(),
            in_specs=[anywhere] * len(operands),
            out_specs=[anywhere] * len(out_shape),
            scratch_shapes=[
                pltpu.VMEM((2, 2, row_block, cols, half), BF16),
                pltpu.VMEM((2, 2, coefs, cols), BF16),
                piece,
                pltpu.VMEM((half // LANES, coefs * row_block, LANES), F32),
                piece,
                pltpu.SemaphoreType.DMA((2, 2, 2)),
                pltpu.SemaphoreType.DMA((2,)),
                pltpu.SemaphoreType.DMA((2,)),
                pltpu.SemaphoreType.DMA((2,)),
                pltpu.SemaphoreType.DMA,
            ],
        ),
        out_shape=out_shape,
        input_output_aliases=aliases,
        compiler_params=params(),
        cost_estimate=pl.CostEstimate(
            flops=8 * row_block * coefs * cols * half,
            bytes_accessed=16 * row_block * cols * half,
            transcendentals=0,
        ),
        name="longitude_hop",
    )(scal, *operands)


def filter_body(
    spectrum, pulled, forward, backward, inner, inner_t, outer_t,
    *refs,
):
    (adjoint, gradients, stack, z, back, hidden, u_adj, inner_total, outer_total) = refs[-9:]
    bands, _, _, rows, half = spectrum.shape
    lats = bands * rows
    tile = lats // 2

    @pl.when(pl.program_id(0) == 0)
    def _():
        inner_total[...] = jnp.zeros_like(inner_total)
        outer_total[...] = jnp.zeros_like(outer_total)

    for source, target in ((spectrum, z), (pulled, back)):
        for part in range(2):
            for band in range(bands):
                first = part * lats + band * rows
                stack[first : first + rows, :] = source[band, part, 0]
        for part in range(2):
            @pl.loop(0, 2)
            def _(i, part=part, target=target):
                at = pl.multiple_of(i * tile, 16)
                value = dot(forward[pl.ds(part * lats + at, tile), :], stack[...])
                target[pl.ds(at, tile), part * half : (part + 1) * half] = value.astype(BF16)

    @pl.loop(0, 2)
    def _(i):
        at = pl.ds(pl.multiple_of(i * tile, 16), tile)
        gelu, slope = gelu_pair(dot(z[at, :], inner[...]))
        hidden[at, :] = gelu.astype(BF16)
        u_adj[at, :] = (dot(back[at, :], outer_t[...]) * slope).astype(BF16)
        z_adj = dot(u_adj[at, :], inner_t[...]).astype(BF16)
        for part in range(2):
            where = pl.ds(pl.multiple_of(part * lats + i * tile, 16), tile)
            stack[where, :] = z_adj[:, part * half : (part + 1) * half]

    outer_total[...] += dot(hidden[...], back[...], 0, 0)
    inner_total[...] += dot(z[...], u_adj[...], 0, 0)
    for part in range(2):
        for band in range(bands):
            first = part * lats + band * rows
            value = dot(backward[first : first + rows, :], stack[...])
            adjoint[band, part, 0] = value.astype(BF16)

    @pl.when(pl.program_id(0) == pl.num_programs(0) - 1)
    def _():
        for which, total in enumerate((inner_total, outer_total)):
            for b in range(half // BLOCK_W):
                low = slice(b * BLOCK_W, (b + 1) * BLOCK_W)
                high = slice(half + b * BLOCK_W, half + (b + 1) * BLOCK_W)
                gradients[which, b, 0] = total[low, low] + total[high, high]
                gradients[which, b, 1] = total[low, high] - total[high, low]


def spectral_filter(first, modes, spectrum, pulled, forward, backward, inner, inner_t, outer_t, *ties):
    bands, _, _, rows, half = spectrum.shape
    lats = bands * rows
    wide = 2 * half
    data = pl.BlockSpec((bands, 2, 1, rows, half), lambda i: (0, 0, first + i, 0, 0))

    def whole(*shape):
        return pl.BlockSpec(shape, lambda i: (0,) * len(shape), pipeline_mode=pl.Buffered(1))

    square = whole(2 * lats, 2 * lats)
    weight = whole(wide, wide)
    gradients = (2, half // BLOCK_W, 2, BLOCK_W, BLOCK_W)
    return pl.pallas_call(
        filter_body,
        grid=(modes,),
        in_specs=[data, data, square, square, weight, weight, weight]
        + [pl.BlockSpec(memory_space=pl.ANY)] * len(ties),
        out_specs=[
            pl.BlockSpec((bands, 2, 1, rows, half), lambda i: (0, 0, i, 0, 0)),
            whole(*gradients),
        ],
        out_shape=[
            jax.ShapeDtypeStruct((bands, 2, modes, rows, half), BF16),
            jax.ShapeDtypeStruct(gradients, F32),
        ],
        scratch_shapes=[
            pltpu.VMEM((2 * lats, half), BF16),
            pltpu.VMEM((lats, wide), BF16),
            pltpu.VMEM((lats, wide), BF16),
            pltpu.VMEM((lats, wide), BF16),
            pltpu.VMEM((lats, wide), BF16),
            pltpu.VMEM((wide, wide), F32),
            pltpu.VMEM((wide, wide), F32),
        ],
        compiler_params=params(),
        cost_estimate=pl.CostEstimate(
            flops=modes * 2 * (3 * 4 * lats * lats * half + 5 * lats * wide * wide),
            bytes_accessed=6 * modes * 2 * lats * half,
            transcendentals=modes * 2 * lats * half * 2,
        ),
        name="spectral_filter",
    )(spectrum, pulled, forward, backward, inner, inner_t, outer_t, *ties)


def relay_body(t, has_own, has_recv, has_prev, ties, scal, *refs):
    refs = list(refs)
    own = refs.pop(0) if has_own else None
    recv = (refs.pop(0), refs.pop(0)) if has_recv else None
    refs = refs[2 * has_prev + ties :]
    sends, kept = refs[0:2], refs[2:4]
    for way in range(2):
        def put(value, way=way):
            sends[way][...] = value[...]
            kept[way][0] = value[...]

        if own is None:
            put(recv[way])
        elif recv is None:
            put(own)
        else:
            pl.when(scal[t, 2 + way] != 0)(functools.partial(put, own))
            pl.when(scal[t, 2 + way] == 0)(functools.partial(put, recv[way]))


def relay(t, scal, own, own_at, recv, prev, count, shape, ties=()):
    coefs, rows, half = shape
    piece = pl.BlockSpec(shape, lambda i, s: (0, 0, 0))
    in_specs, operands = [], []
    if own is not None:
        in_specs.append(pl.BlockSpec(shape, lambda i, s: (own_at, 0, 0)))
        operands.append(own)
    if recv is not None:
        in_specs += [piece, piece]
        operands += list(recv)
    aliases = {}
    if prev is not None:
        for i, array in enumerate(prev):
            aliases[1 + len(operands)] = 2 + i
            in_specs.append(pl.BlockSpec(memory_space=pl.ANY))
            operands.append(array)
    for array in ties:
        in_specs.append(pl.BlockSpec(memory_space=pl.ANY))
        operands.append(array)

    def kept(way):
        return pl.BlockSpec((1,) + shape, lambda i, s: (s[t, way], 0, 0, 0))

    return pl.pallas_call(
        functools.partial(
            relay_body, t, own is not None, recv is not None, prev is not None, len(ties)
        ),
        grid_spec=pltpu.PrefetchScalarGridSpec(
            num_scalar_prefetch=1,
            grid=(1,),
            in_specs=in_specs,
            out_specs=[piece, piece, kept(0), kept(1)],
        ),
        out_shape=[jax.ShapeDtypeStruct(shape, BF16)] * 2
        + [jax.ShapeDtypeStruct((count + 1,) + shape, BF16)] * 2,
        input_output_aliases=aliases,
        compiler_params=params(),
        cost_estimate=pl.CostEstimate(
            flops=0, bytes_accessed=8 * coefs * rows * half, transcendentals=0
        ),
        name="relay",
    )(scal, *operands)


def grid_body(core, *refs):
    pieces, panels, (own_out, other_out, *totals) = refs[:2], refs[2], refs[-4:]
    count, chunk, row_block, half = pieces[0].shape
    coefs = count * chunk
    tiles = half // LANES
    for total, piece in zip(totals, pieces):
        for j in range(tiles):
            value = piece[:, :, :, pl.ds(j * LANES, LANES)].astype(F32)
            total[j] = value.reshape(coefs * row_block, LANES)
    for h in range(row_block):
        rows = [
            jnp.concatenate(
                [total[j, pl.ds(h, coefs, stride=row_block), :] for j in range(tiles)], axis=1
            ).astype(BF16)
            for total in totals
        ]
        value = jnp.concatenate(rows, axis=0)
        own_out[h] = dot(panels[0], value).astype(BF16)
        other_out[h] = dot(panels[1], value).astype(BF16)


def to_grid(core, kept, panels, first, blocks, row_block, rows, width, whole, ties=()):
    count, chunk, _, half = kept[0].shape
    count -= 1
    cols = panels.shape[1]
    in_specs = [
        pl.BlockSpec((count, chunk, row_block, half), lambda i, s: (0, 0, first + i, 0))
    ] * 2 + [pl.BlockSpec(panels.shape, lambda i, s: (0, 0, 0))]
    operands = list(kept) + [panels]
    aliases = {}
    if whole is not None:
        aliases[1 + len(operands)] = 0
        ties = (whole,) + tuple(ties)
    for array in ties:
        in_specs.append(pl.BlockSpec(memory_space=pl.ANY))
        operands.append(array)
    total = pltpu.VMEM((half // LANES, count * chunk * row_block, LANES), F32)
    return pl.pallas_call(
        grid_body,
        grid_spec=pltpu.PrefetchScalarGridSpec(
            num_scalar_prefetch=1,
            grid=(blocks,),
            in_specs=in_specs,
            out_specs=[
                pl.BlockSpec((row_block, cols, half), lambda i, s: (first + i, 0, s[0])),
                pl.BlockSpec((row_block, cols, half), lambda i, s: (i, 0, 0)),
            ],
            scratch_shapes=[total] * 2,
        ),
        out_shape=[
            jax.ShapeDtypeStruct((rows, cols, width), BF16),
            jax.ShapeDtypeStruct((blocks * row_block, cols, half), BF16),
        ],
        input_output_aliases=aliases,
        compiler_params=params(),
        cost_estimate=pl.CostEstimate(
            flops=8 * blocks * row_block * count * chunk * cols * half,
            bytes_accessed=4 * (count * chunk + cols) * blocks * row_block * half,
            transcendentals=0,
        ),
        name="longitude_grid",
    )(core, *operands)


def place_body(core, piece, whole, out):
    out[...] = piece[...]


def place(core, piece, whole, first, row_block):
    rows, cols, half = piece.shape
    return pl.pallas_call(
        place_body,
        grid_spec=pltpu.PrefetchScalarGridSpec(
            num_scalar_prefetch=1,
            grid=(rows // row_block,),
            in_specs=[
                pl.BlockSpec((row_block, cols, half), lambda i, s: (i, 0, 0)),
                pl.BlockSpec(memory_space=pl.ANY),
            ],
            out_specs=pl.BlockSpec((row_block, cols, half), lambda i, s: (first + i, 0, 1 - s[0])),
        ),
        out_shape=jax.ShapeDtypeStruct(whole.shape, BF16),
        input_output_aliases={2: 0},
        compiler_params=params(),
        name="place",
    )(core, piece, whole)


def pick_body(core, array, *refs):
    out, sems = refs[-2:]
    rows, _, half = out.shape
    step = rows // sems.shape[0]
    lanes = pl.ds(pl.multiple_of((1 - core[0]) * half, LANES), half)
    copies = [
        pltpu.make_async_copy(
            array.at[pl.ds(i * step, step), :, lanes], out.at[pl.ds(i * step, step)], sems.at[i]
        )
        for i in range(sems.shape[0])
    ]
    for copy in copies:
        copy.start()
    for copy in copies:
        copy.wait()


def pick(core, array, rows, *ties):
    _, cols, width = array.shape
    anywhere = pl.BlockSpec(memory_space=pl.ANY)
    return pl.pallas_call(
        pick_body,
        grid_spec=pltpu.PrefetchScalarGridSpec(
            num_scalar_prefetch=1,
            grid=(),
            in_specs=[anywhere] * (1 + len(ties)),
            out_specs=anywhere,
            scratch_shapes=[pltpu.SemaphoreType.DMA((8,))],
        ),
        out_shape=jax.ShapeDtypeStruct((rows, cols, width // 2), BF16),
        compiler_params=params(),
        cost_estimate=pl.CostEstimate(
            flops=0, bytes_accessed=2 * rows * cols * width, transcendentals=0
        ),
        name="pick",
    )(core, array, *ties)


def block_diagonal(blocks):
    count, size, _ = blocks.shape
    eye = jnp.eye(count, dtype=blocks.dtype)
    wide = blocks[:, :, None, :] * eye[:, None, :, None]
    return wide.reshape(count * size, count * size)


def complex_weight(weight):
    real = block_diagonal(weight[:, 0])
    imag = block_diagonal(weight[:, 1])
    return jnp.concatenate(
        [
            jnp.concatenate([real, imag], axis=1),
            jnp.concatenate([-imag, real], axis=1),
        ],
        axis=0,
    )


def local(fields, cotangent, inner_weight, outer_weight):
    lat_count = lax.axis_size("lat")
    lon_count = lax.axis_size("lon")
    rows, cols, width = fields.shape
    chips = lon_count // 2
    half = width // 2
    lon = lax.axis_index("lon")
    chip = lon // 2
    core = lon % 2
    row_block = 16 if rows % 16 == 0 else 8
    blocks = rows // row_block
    per_end = MODES // 2
    per_group = per_end // lat_count
    per_part = per_group // PARTS
    coefs = lat_count * 2 * per_part
    swap = [(i, i ^ 1) for i in range(lon_count)]
    upward = [(i, i + 2) for i in range(lon_count - 2)]
    downward = [(i + 2, i) for i in range(lon_count - 2)]

    core_now = core.reshape(1).astype(jnp.int32)
    first_sent = pick(core_now, fields, DELAY * row_block)
    fields_sent = pick(core_now, fields, rows, first_sent)
    fields_first = lax.ppermute(first_sent, "lon", swap)
    fields_other = lax.ppermute(fields_sent, "lon", swap)
    cot_other = None

    q = jnp.arange(coefs, dtype=jnp.int32)
    part_of = q // per_part % 2
    ids = q // (2 * per_part) * per_group + q % per_part
    ends = jnp.arange(2, dtype=jnp.int32)[:, None, None] * per_end
    pieces = jnp.arange(PARTS, dtype=jnp.int32)[None, :, None] * per_part
    mode_ids = (ends + pieces + ids).reshape(-1)
    imag_row = jnp.tile(part_of, 2 * PARTS) == 1
    places = jnp.concatenate(
        [lon * cols + jnp.arange(cols, dtype=jnp.int32),
         (lon ^ 1) * cols + jnp.arange(cols, dtype=jnp.int32)]
    )
    cos_rows, sin_rows = trig_rows(mode_ids, places, LONS)
    per_piece = per_part // PIECES
    base = jnp.where(imag_row[:, None], -sin_rows, cos_rows)
    weights = jnp.where(mode_ids == 0, 1.0, 2.0).astype(BF16)
    both = jnp.stack([base, base * weights[:, None]], axis=0)
    tables = both.reshape(2, 2, PARTS, coefs, 2, cols).transpose(2, 0, 1, 4, 3, 5)
    panels = (
        base.reshape(2 * PARTS, 2 * lat_count, PIECES, per_piece, 2, cols)
        .transpose(4, 5, 0, 2, 1, 3)
        .reshape(2, cols, 2 * PARTS * coefs)
    )

    lat_ids = jnp.arange(LATS, dtype=jnp.int32)
    lat_cos, lat_sin = trig_rows(lat_ids, lat_ids, LATS)
    forward = jnp.concatenate(
        [jnp.concatenate([lat_cos, lat_sin], axis=1),
         jnp.concatenate([-lat_sin, lat_cos], axis=1)], axis=0
    )
    backward = jnp.concatenate(
        [jnp.concatenate([lat_cos, -lat_sin], axis=1),
         jnp.concatenate([lat_sin, lat_cos], axis=1)], axis=0
    )
    own_blocks = half // BLOCK_W
    inner = complex_weight(
        lax.dynamic_slice_in_dim(inner_weight, core * own_blocks, own_blocks, axis=0)
    )
    outer = complex_weight(
        lax.dynamic_slice_in_dim(outer_weight, core * own_blocks, own_blocks, axis=0)
    )
    inner_t, outer_t = inner.T, outer.T

    order = [(s, a, r) for s in range(PARTS) for a in range(2) for r in range(blocks)]
    count = len(order)
    slots = count + DELAY * (chips - 1)
    slot_ids = jnp.arange(slots, dtype=jnp.int32)

    def schedule(late):
        v = jnp.clip(slot_ids - DELAY * late, 0, count - 1)
        return [v // blocks % 2, v % blocks, v // (2 * blocks)]

    flat = jnp.zeros_like(slot_ids)
    scal = jnp.stack(
        schedule(chip) + schedule(chips - 1 - chip) + [flat + core, flat + chip], axis=1
    )
    def across(array):
        return lax.all_to_all(array, "lat", split_axis=0, concat_axis=0, tiled=True)

    spread = []
    gradients = 0.0

    def filter_piece(s, piece, *ties):
        nonlocal gradients
        shape = (lat_count, 2, per_part, rows, half)
        adjoint, part = spectral_filter(
            piece * per_piece, per_piece,
            every_row[s, 0].reshape(shape), every_row[s, 1].reshape(shape),
            forward, backward, inner, inner_t, outer_t, *ties,
        )
        gradients = gradients + part
        spread.append(across(adjoint.reshape(-1, rows, half)))
        return adjoint

    sent = {}
    gathered = {}
    every_row = {}
    for t in range(slots):
        v = t - DELAY * (chips - 1)
        if t < DELAY:
            arrays = (fields, fields, fields_first, fields_first)
        elif t < blocks:
            arrays = (fields, fields, fields_other, fields_other)
        else:
            arrays = (fields, cotangent, fields_other, cot_other)
        if t == DELAY:
            cot_other = lax.ppermute(pick(core_now, cotangent, rows, result[0]), "lon", swap)
        recv = sent.pop(t - DELAY, None)
        key, final_at, prev = None, None, None
        if v >= 0:
            key, final_at = order[v][:2], order[v][2]
            prev = gathered.get(key)
        ties = []
        if t - slots in EARLY:
            ties.append(filter_piece(0, EARLY.index(t - slots), result[0]))
        result = hop(t, scal, arrays, tables, recv, prev, final_at, row_block, rows, ties)
        if v >= 0:
            gathered[key] = result[2]
            if final_at == blocks - 1:
                every_row[key] = across(result[2])
        if t < count + DELAY * (chips - 2):
            sent[t] = (
                lax.ppermute(result[0], "lon", upward),
                lax.ppermute(result[1], "lon", downward),
            )
    def add_up(terms):
        at_end = (chip == 0) | (chip == chips - 1)
        terms = jnp.where(at_end, terms, 0.0).reshape(lat_count, -1, LANES)
        return jnp.sum(across(terms), axis=0)

    per_spread = coefs // (PIECES * CHUNK)
    count = PARTS * PIECES * per_spread
    slots = count + DELAY * (chips - 1)
    slot_ids = jnp.arange(slots, dtype=jnp.int32)

    def place_of(late):
        v = slot_ids - DELAY * late
        return jnp.where((v >= 0) & (v < count), v, count)

    flat = jnp.zeros_like(slot_ids)
    scal = jnp.stack(
        [place_of(chip), place_of(chips - 1 - chip),
         flat + (chip == 0), flat + (chip == chips - 1)], axis=1
    ).astype(jnp.int32)
    sent = {}
    kept = None
    for t in range(slots):
        own, own_at = (None, None)
        if t < count:
            own, own_at = spread[t // per_spread], t % per_spread
        ties = []
        if t in LATE:
            ties.append(filter_piece(1, LATE.index(t), up))
        if t == 0:
            ties.append(result[0])
        if t == LATE[-1] + 2:
            share = add_up(gradients)
            ties.append(share)
            by_core = lax.all_gather(share, "lon").reshape(chips, 2, -1, LANES)
            by_core = jnp.sum(by_core, axis=0)
            sums = lax.all_gather(by_core, "lat", axis=1, tiled=True)
        if t == slots - 1:
            ties.append(by_core)
        up, down, *kept = relay(
            t, scal, own, own_at, sent.pop(t - DELAY, None), kept, count,
            (CHUNK, rows, half), ties,
        )
        if t < count + DELAY * (chips - 2):
            sent[t] = (lax.ppermute(up, "lon", upward), lax.ppermute(down, "lon", downward))

    whole = None
    swapped = []
    for first, some in ((0, blocks - blocks // 2), (blocks - blocks // 2, blocks // 2)):
        whole, for_other = to_grid(
            core_now, kept, panels, first, some, row_block, rows, width, whole,
            (sums,) if first else (),
        )
        swapped.append((first, lax.ppermute(for_other, "lon", swap)))
    for first, piece in swapped:
        whole = place(core_now, piece, whole, first, row_block)
    sums = (sums * (1.0 / math.sqrt(LATS * MODES))).reshape(2, 2, own_blocks, 2, BLOCK_W, BLOCK_W)
    sums = jnp.swapaxes(sums, 0, 1).reshape(2, BLOCKS, 2, BLOCK_W, BLOCK_W)
    return (whole, sums[0], sums[1])


def solution(mesh):
    return jax.shard_map(
        local,
        mesh=mesh,
        in_specs=(P("lat", "lon", None), P("lat", "lon", None), P(), P()),
        out_specs=(P("lat", "lon", None), P(), P()),
        check_vma=False,
    )
```

time: 1360 us -> 1860 us (1.37)
  Pallas kernels: 613 us -> 1210 us
  waiting for transfers between devices: 367 us -> 248 us
  starting transfers between devices: 251 us -> 328 us
  local copies, waits for them, and re-layouts: 71.6 us -> 17.2 us
    pallas_call x0 -> x3, Pallas kernels: none -> 671 us  [pick(): pl.pallas_call(pick_body, grid_spec=pltpu.PrefetchScalarGridSpec(num_scal...]
    psum x1 -> x0, waiting for transfers between devices: 132 us -> none  [local(): sums = lax.psum(sums, ('lat', 'lon')) * (1.0 / math.sqrt(LATS * MODES))]
    pallas_call x34, Pallas kernels: 335 us -> 244 us  [hop(): pl.pallas_call(functools.partial(hop_body, t, row_block, recv is not None...]
    ppermute x32, waiting for transfers between devices: 57.9 us -> 107 us  [local(): lax.ppermute(result[1], 'lon', downward)]
    ppermute x18 -> x20, waiting for transfers between devices: 66.2 us -> 18.2 us  [local(): lax.ppermute(up, 'lon', upward)]
    ppermute x18 -> x20, starting transfers between devices: 34.8 us -> 75.3 us  [local(): lax.ppermute(up, 'lon', upward)]
    unnamed x232 -> x90, local copies, waits for them, and re-layouts: 48.1 us -> 7.7 us
    ppermute x32, waiting for transfers between devices: 30 us -> 63.4 us  [local(): lax.ppermute(result[0], 'lon', upward)]
  transfers between devices with their start and end apart: 110 -> 124, of which waited for: 66 -> 56; matrix products, arithmetic and copies ran while one was open for 3% -> 2% of each run, Pallas kernels for 41% -> 60%
where the time goes in v2:
time: 1860 us; the launch traced here: 1850 us
  Pallas kernels  1210 us (65%)
  starting transfers between devices  328 us (18%)
  waiting for transfers between devices  248 us (13%)
  other arithmetic  25.2 us (1%)
    pallas_call x3, Pallas kernels, pick(): pl.pallas_call(pick_body, grid_spec=pltpu.PrefetchScalarGridSpec(num_scal...  671 us
    pallas_call x34, Pallas kernels, hop(): pl.pallas_call(functools.partial(hop_body, t, row_block, recv is not None...  244 us
    pallas_call x8, Pallas kernels, spectral_filter(): pl.pallas_call(filter_body, grid=(modes,), in_specs=[data, data, square,...  164 us
    ppermute x32, starting transfers between devices, local(): lax.ppermute(result[0], 'lon', upward)  123 us
    ppermute x32, waiting for transfers between devices, local(): lax.ppermute(result[1], 'lon', downward)  107 us
    pallas_call x22, Pallas kernels, relay(): pl.pallas_call(functools.partial(relay_body, t, own is not None, recv is...  89.2 us
    ppermute x20, starting transfers between devices, local(): lax.ppermute(up, 'lon', upward)  75.3 us
    ppermute x32, waiting for transfers between devices, local(): lax.ppermute(result[0], 'lon', upward)  63.4 us
  transfers between devices with their start and end apart: 124, of which 56 were waited for; matrix products, arithmetic and copies ran while one was open for 2% of the time, Pallas kernels for 60%

profile of v2, /device:TPU:0, one launch (start us, length us, event | category | flops | bytes accessed | tf_op | source)
XLA Modules:
  0.0 1848.9 jit_solution(17080793962212140013)
XLA Ops:
  7.2 84.6 %pick.3.refs_0_ = bf16[32,112,384]{2,1,0:T(8,128)(2,1)} custom-call(s32[1]{0:T(128)} %bitcast.core, bf16[112,112,768]{2,1,0:T(8,128)(2,1)} %refs_0_.67), custom_call_target="tpu_custom_call" | custom-call | bytes 5505024 | tf_op jit(solution)/shard_map/pick/pallas_call | solution.py:456
  92.3 293.0 %pick.4 = bf16[112,112,384]{2,1,0:T(8,128)(2,1)} custom-call(s32[1]{0:T(128)} %bitcast.core, bf16[112,112,768]{2,1,0:T(8,128)(2,1)} %refs_0_.67, bf16[32,112,384]{2,1,0:T(8,128)(2,1)} %pick.3.refs_0_), custom_call_target="tpu_custom_call" | custom-call | bytes 19267584 | tf_op jit(solution)/shard_map/pick/pallas_call | solution.py:456
  395.8 293.0 %pick.5 = bf16[112,112,384]{2,1,0:T(8,128)(2,1)} custom-call(s32[1]{0:T(128)} %bitcast.core, bf16[112,112,768]{2,1,0:T(8,128)(2,1)} %refs_1_.67, bf16[64,16,384]{2,1,0:T(8,128)(2,1)} %get-tuple-element.200.refs_0_), custom_call_target="tpu_custom_call" | custom-call | bytes 19267584 | tf_op jit(solution)/shard_map/pick/pallas_call | solution.py:456
  707.1 12.2 collective-permute-done.3.refs_5_
  794.0 7.4 longitude_hop.38
  810.8 7.4 longitude_hop.41
  828.4 7.4 longitude_hop.42
  844.0 7.4 longitude_hop.43
  861.5 7.3 longitude_hop.44
  878.4 7.4 longitude_hop.45
  892.7 7.3 longitude_hop.46
  915.8 11.0 collective-permute-done.27.refs_5_
  1056.3 7.4 collective-permute-done.37.refs_5_
  1069.1 7.3 longitude_hop.53
  1112.0 7.4 longitude_hop.56
  1126.2 7.4 longitude_hop.57
  1140.6 20.5 %spectral_filter.8 = (bf16[4,2,2,112,384]{4,3,2,1,0:T(8,128)(2,1)}, f32[2,4,2,96,96]{4,3,2,1,0:T(8,128)}) custom-call(bf16[4,2,8,112,384]{4,3,2,1,0:T(8,128)(2,1)} %bitcast.2.spectrum, bf16[4,2,8,112,384]{4,3,2,1,0:T(8,128)(2,1)} %bitcast.3.pulled, bf16[896,896]{1,0:T(8,128)(2,1)} %get-tuple-element.400.forward, ...), custom_call_target="tpu_custom_call" | custom-call | flops 8984199168 | bytes 4128768 | tf_op jit(solution)/shard_map/spectral_filter/pallas_call | solution.py:252
  1165.2 7.3 longitude_hop.58
  1186.8 20.5 %spectral_filter.9 = (bf16[4,2,2,112,384]{4,3,2,1,0:T(8,128)(2,1)}, f32[2,4,2,96,96]{4,3,2,1,0:T(8,128)}) custom-call(bf16[4,2,8,112,384]{4,3,2,1,0:T(8,128)(2,1)} %bitcast.2.spectrum, bf16[4,2,8,112,384]{4,3,2,1,0:T(8,128)(2,1)} %bitcast.3.pulled, bf16[896,896]{1,0:T(8,128)(2,1)} %get-tuple-element.400.forward, ...), custom_call_target="tpu_custom_call" | custom-call | flops 8984199168 | bytes 4128768 | tf_op jit(solution)/shard_map/spectral_filter/pallas_call | solution.py:252
  1218.6 20.5 %spectral_filter.10 = (bf16[4,2,2,112,384]{4,3,2,1,0:T(8,128)(2,1)}, f32[2,4,2,96,96]{4,3,2,1,0:T(8,128)}) custom-call(bf16[4,2,8,112,384]{4,3,2,1,0:T(8,128)(2,1)} %bitcast.2.spectrum, bf16[4,2,8,112,384]{4,3,2,1,0:T(8,128)(2,1)} %bitcast.3.pulled, bf16[896,896]{1,0:T(8,128)(2,1)} %get-tuple-element.400.forward, ...), custom_call_target="tpu_custom_call" | custom-call | flops 8984199168 | bytes 4128768 | tf_op jit(solution)/shard_map/spectral_filter/pallas_call | solution.py:252
  1250.2 7.6 collective-permute-done.49.refs_5_
  1285.3 9.7 collective-permute-done.57.refs_5_
  1325.5 20.5 %spectral_filter.11 = (bf16[4,2,2,112,384]{4,3,2,1,0:T(8,128)(2,1)}, f32[2,4,2,96,96]{4,3,2,1,0:T(8,128)}) custom-call(bf16[4,2,8,112,384]{4,3,2,1,0:T(8,128)(2,1)} %bitcast.2.spectrum, bf16[4,2,8,112,384]{4,3,2,1,0:T(8,128)(2,1)} %bitcast.3.pulled, bf16[896,896]{1,0:T(8,128)(2,1)} %get-tuple-element.400.forward, ...), custom_call_target="tpu_custom_call" | custom-call | flops 8984199168 | bytes 4128768 | tf_op jit(solution)/shard_map/spectral_filter/pallas_call | solution.py:252
  1430.6 12.0 all-to-all-done.3
  1465.7 20.4 %spectral_filter.12 = (bf16[4,2,2,112,384]{4,3,2,1,0:T(8,128)(2,1)}, f32[2,4,2,96,96]{4,3,2,1,0:T(8,128)}) custom-call(bf16[4,2,8,112,384]{4,3,2,1,0:T(8,128)(2,1)} %bitcast.10.spectrum, bf16[4,2,8,112,384]{4,3,2,1,0:T(8,128)(2,1)} %bitcast.11.pulled, bf16[896,896]{1,0:T(8,128)(2,1)} %get-tuple-element.400.forward, ...), custom_call_target="tpu_custom_call" | custom-call | flops 8984199168 | bytes 4128768 | tf_op jit(solution)/shard_map/spectral_filter/pallas_call | solution.py:252
  1512.3 20.5 %spectral_filter.13 = (bf16[4,2,2,112,384]{4,3,2,1,0:T(8,128)(2,1)}, f32[2,4,2,96,96]{4,3,2,1,0:T(8,128)}) custom-call(bf16[4,2,8,112,384]{4,3,2,1,0:T(8,128)(2,1)} %bitcast.10.spectrum, bf16[4,2,8,112,384]{4,3,2,1,0:T(8,128)(2,1)} %bitcast.11.pulled, bf16[896,896]{1,0:T(8,128)(2,1)} %get-tuple-element.400.forward, ...), custom_call_target="tpu_custom_call" | custom-call | flops 8984199168 | bytes 4128768 | tf_op jit(solution)/shard_map/spectral_filter/pallas_call | solution.py:252
  1558.9 20.5 %spectral_filter.14 = (bf16[4,2,2,112,384]{4,3,2,1,0:T(8,128)(2,1)}, f32[2,4,2,96,96]{4,3,2,1,0:T(8,128)}) custom-call(bf16[4,2,8,112,384]{4,3,2,1,0:T(8,128)(2,1)} %bitcast.10.spectrum, bf16[4,2,8,112,384]{4,3,2,1,0:T(8,128)(2,1)} %bitcast.11.pulled, bf16[896,896]{1,0:T(8,128)(2,1)} %get-tuple-element.400.forward, ...), custom_call_target="tpu_custom_call" | custom-call | flops 8984199168 | bytes 4128768 | tf_op jit(solution)/shard_map/spectral_filter/pallas_call | solution.py:252
  1600.0 20.5 %spectral_filter.15 = (bf16[4,2,2,112,384]{4,3,2,1,0:T(8,128)(2,1)}, f32[2,4,2,96,96]{4,3,2,1,0:T(8,128)}) custom-call(bf16[4,2,8,112,384]{4,3,2,1,0:T(8,128)(2,1)} %bitcast.10.spectrum, bf16[4,2,8,112,384]{4,3,2,1,0:T(8,128)(2,1)} %bitcast.11.pulled, bf16[896,896]{1,0:T(8,128)(2,1)} %get-tuple-element.400.forward, ...), custom_call_target="tpu_custom_call" | custom-call | flops 8984199168 | bytes 4128768 | tf_op jit(solution)/shard_map/spectral_filter/pallas_call | solution.py:252
  1691.7 9.4 collective-permute-done.91.refs_1_
  1701.1 7.8 collective-permute-done.92.refs_2_
  1790.4 19.9 %longitude_grid.2 = (bf16[112,112,768]{2,1,0:T(8,128)(2,1)}, bf16[64,112,384]{2,1,0:T(8,128)(2,1)}) custom-call(s32[1]{0:T(128)} %bitcast.core, bf16[17,8,112,384]{3,2,1,0:T(8,128)(2,1)} %get-tuple-element.391.refs_0_, bf16[17,8,112,384]{3,2,1,0:T(8,128)(2,1)} %get-tuple-element.392.refs_1_, bf16[2,112,256]{2,1,0:T(8,128)(2,1)} %fusion.21.refs_2_), custom_call_target="tpu_custom_call" | custom-call | flops 2818572288 | bytes 23592960 | tf_op jit(solution)/shard_map/longitude_grid/pallas_call | solution.py:385
  1810.4 15.9 longitude_grid.3
  (437 shorter events, 803.9 us)
Async XLA Ops:
  91.7 297.1 %collective-permute-start.1 = (bf16[32,112,384]{2,1,0:T(8,128)(2,1)}, bf16[32,112,384]{2,1,0:T(8,128)(2,1)}, u32[]{:S(2)}, u32[]{:S(2)}) collective-permute-start(bf16[32,112,384]{2,1,0:T(8,128)(2,1)} %pick.3.refs_0_), channel_id=1, source_target_pairs={{0,1},{1,0},{2,3},{3,2},{4,5},{5,4},{6,7},{7,6},{8,9},{9,8},{10,11... | collective-permute-start | bytes 8257544 | tf_op jit(solution)/shard_map/ppermute | solution.py:515
  385.3 337.8 %collective-permute-start = (bf16[112,112,384]{2,1,0:T(8,128)(2,1)}, bf16[112,112,384]{2,1,0:T(8,128)(2,1)}, u32[]{:S(2)}, u32[]{:S(2)}) collective-permute-start(bf16[112,112,384]{2,1,0:T(8,128)(2,1)} %pick.4), channel_id=1, source_target_pairs={{0,1},{1,0},{2,3},{3,2},{4,5},{5,4},{6,7},{7,6},{8,9},{9,8},{10,11... | collective-permute-start | bytes 28901384 | tf_op jit(solution)/shard_map/ppermute | solution.py:516
  688.8 122.0 %collective-permute-start.2 = (bf16[112,112,384]{2,1,0:T(8,128)(2,1)}, bf16[112,112,384]{2,1,0:T(8,128)(2,1)}, u32[]{:S(2)}, u32[]{:S(2)}) collective-permute-start(bf16[112,112,384]{2,1,0:T(8,128)(2,1)} %pick.5), channel_id=1, source_target_pairs={{0,1},{1,0},{2,3},{3,2},{4,5},{5,4},{6,7},{7,6},{8,9},{9,8},{10,11... | collective-permute-start | bytes 28901384 | tf_op jit(solution)/shard_map/ppermute | solution.py:604
  900.0 136.1 %all-to-all-start = ((bf16[64,112,384]{2,1,0:T(8,128)(2,1)}), bf16[64,112,384]{2,1,0:T(8,128)(2,1)}, u32[]{:S(2)}, u32[]{:S(2)}) async-start(bf16[64,112,384]{2,1,0:T(8,128)(2,1)} %get-tuple-element.262), calls=%async_computation | async-start | bytes 11010048 | tf_op jit(solution)/shard_map/all_to_all | solution.py:575
  1036.2 104.4 %all-to-all-start.1 = ((bf16[64,112,384]{2,1,0:T(8,128)(2,1)}), bf16[64,112,384]{2,1,0:T(8,128)(2,1)}, u32[]{:S(2)}, u32[]{:S(2)}) async-start(bf16[64,112,384]{2,1,0:T(8,128)(2,1)} %get-tuple-element.263), calls=%async_computation.1 | async-start | bytes 11010048 | tf_op jit(solution)/shard_map/all_to_all | solution.py:575
  1119.4 45.8 %collective-permute-start.45 = (bf16[64,16,384]{2,1,0:T(8,128)(2,1)}, bf16[64,16,384]{2,1,0:T(8,128)(2,1)}, u32[]{:S(2)}, u32[]{:S(2)}) collective-permute-start(bf16[64,16,384]{2,1,0:T(8,128)(2,1)} %get-tuple-element.256), channel_id=1, source_target_pairs={{0,2},{1,3},{2,4},{3,5},{4,6},{5,7},{8,10},{9,11},{10,12},{11,13},... | collective-permute-start | bytes 2359304 | tf_op jit(solution)/shard_map/ppermute | solution.py:620
  1124.9 40.3 %collective-permute-start.46 = (bf16[64,16,384]{2,1,0:T(8,128)(2,1)}, bf16[64,16,384]{2,1,0:T(8,128)(2,1)}, u32[]{:S(2)}, u32[]{:S(2)}) collective-permute-start(bf16[64,16,384]{2,1,0:T(8,128)(2,1)} %get-tuple-element.257), channel_id=1, source_target_pairs={{2,0},{3,1},{4,2},{5,3},{6,4},{7,5},{10,8},{11,9},{12,10},{13,11},... | collective-permute-start | bytes 2359304 | tf_op jit(solution)/shard_map/ppermute | solution.py:621
  1133.6 38.9 %collective-permute-start.51 = (bf16[64,16,384]{2,1,0:T(8,128)(2,1)}, bf16[64,16,384]{2,1,0:T(8,128)(2,1)}, u32[]{:S(2)}, u32[]{:S(2)}) collective-permute-start(bf16[64,16,384]{2,1,0:T(8,128)(2,1)} %get-tuple-element.264.refs_0_), channel_id=1, source_target_pairs={{0,2},{1,3},{2,4},{3,5},{4,6},{5,7},{8,10},{9,11},{10,12},{11,13},... | collective-permute-start | bytes 2359304 | tf_op jit(solution)/shard_map/ppermute | solution.py:620
  1161.1 46.3 %all-to-all-start.7 = ((bf16[16,112,384]{2,1,0:T(8,128)(2,1)}), bf16[16,112,384]{2,1,0:T(8,128)(2,1)S(1)}, u32[]{:S(2)}, u32[]{:S(2)}) async-start(bf16[16,112,384]{2,1,0:T(8,128)(2,1)} %bitcast.57), calls=%async_computation.7 | async-start | bytes 2752512 | tf_op jit(solution)/shard_map/all_to_all | solution.py:575
  1271.5 124.3 %all-to-all-start.2 = ((bf16[64,112,384]{2,1,0:T(8,128)(2,1)}), bf16[64,112,384]{2,1,0:T(8,128)(2,1)}, u32[]{:S(2)}, u32[]{:S(2)}) async-start(bf16[64,112,384]{2,1,0:T(8,128)(2,1)} %get-tuple-element.273), calls=%async_computation.2 | async-start | bytes 11010048 | tf_op jit(solution)/shard_map/all_to_all | solution.py:575
  1305.9 40.1 %collective-permute-start.61 = (bf16[64,16,384]{2,1,0:T(8,128)(2,1)}, bf16[64,16,384]{2,1,0:T(8,128)(2,1)S(1)}, u32[]{:S(2)}, u32[]{:S(2)}) collective-permute-start(bf16[64,16,384]{2,1,0:T(8,128)(2,1)} %get-tuple-element.284), channel_id=1, source_target_pairs={{0,2},{1,3},{2,4},{3,5},{4,6},{5,7},{8,10},{9,11},{10,12},{11,13},... | collective-permute-start | bytes 2359304 | tf_op jit(solution)/shard_map/ppermute | solution.py:620
  1307.3 38.8 %collective-permute-start.62 = (bf16[64,16,384]{2,1,0:T(8,128)(2,1)}, bf16[64,16,384]{2,1,0:T(8,128)(2,1)}, u32[]{:S(2)}, u32[]{:S(2)}) collective-permute-start(bf16[64,16,384]{2,1,0:T(8,128)(2,1)} %get-tuple-element.285), channel_id=1, source_target_pairs={{2,0},{3,1},{4,2},{5,3},{6,4},{7,5},{10,8},{11,9},{12,10},{13,11},... | collective-permute-start | bytes 2359304 | tf_op jit(solution)/shard_map/ppermute | solution.py:621
  1322.7 37.3 %collective-permute-start.59 = (bf16[64,16,384]{2,1,0:T(8,128)(2,1)}, bf16[64,16,384]{2,1,0:T(8,128)(2,1)S(1)}, u32[]{:S(2)}, u32[]{:S(2)}) collective-permute-start(bf16[64,16,384]{2,1,0:T(8,128)(2,1)} %get-tuple-element.282.refs_0_), channel_id=1, source_target_pairs={{0,2},{1,3},{2,4},{3,5},{4,6},{5,7},{8,10},{9,11},{10,12},{11,13},... | collective-permute-start | bytes 2359304 | tf_op jit(solution)/shard_map/ppermute | solution.py:620
  1395.8 46.7 %all-to-all-start.3 = ((bf16[64,112,384]{2,1,0:T(8,128)(2,1)}), bf16[64,112,384]{2,1,0:T(8,128)(2,1)}, u32[]{:S(2)}, u32[]{:S(2)}) async-start(bf16[64,112,384]{2,1,0:T(8,128)(2,1)} %get-tuple-element.295), calls=%async_computation.3 | async-start | bytes 11010048 | tf_op jit(solution)/shard_map/all_to_all | solution.py:575
  1442.6 43.6 %all-to-all-start.4 = ((bf16[16,112,384]{2,1,0:T(8,128)(2,1)}), bf16[16,112,384]{2,1,0:T(8,128)(2,1)S(1)}, u32[]{:S(2)}, u32[]{:S(2)}) async-start(bf16[16,112,384]{2,1,0:T(8,128)(2,1)} %bitcast.50), calls=%async_computation.4 | async-start | bytes 2752512 | tf_op jit(solution)/shard_map/all_to_all | solution.py:575
  1450.3 40.2 %collective-permute-start.75 = (bf16[8,112,384]{2,1,0:T(8,128)(2,1)}, bf16[8,112,384]{2,1,0:T(8,128)(2,1)}, u32[]{:S(2)}, u32[]{:S(2)}) collective-permute-start(bf16[8,112,384]{2,1,0:T(8,128)(2,1)} %get-tuple-element.313), channel_id=1, source_target_pairs={{0,2},{1,3},{2,4},{3,5},{4,6},{5,7},{8,10},{9,11},{10,12},{11,13},... | collective-permute-start | bytes 2064392 | tf_op jit(solution)/shard_map/ppermute | solution.py:666
  1453.1 37.4 %collective-permute-start.76 = (bf16[8,112,384]{2,1,0:T(8,128)(2,1)}, bf16[8,112,384]{2,1,0:T(8,128)(2,1)}, u32[]{:S(2)}, u32[]{:S(2)}) collective-permute-start(bf16[8,112,384]{2,1,0:T(8,128)(2,1)} %get-tuple-element.314), channel_id=1, source_target_pairs={{2,0},{3,1},{4,2},{5,3},{6,4},{7,5},{10,8},{11,9},{12,10},{13,11},... | collective-permute-start | bytes 2064392 | tf_op jit(solution)/shard_map/ppermute | solution.py:666
  1458.6 42.8 %collective-permute-start.73 = (bf16[8,112,384]{2,1,0:T(8,128)(2,1)}, bf16[8,112,384]{2,1,0:T(8,128)(2,1)}, u32[]{:S(2)}, u32[]{:S(2)}) collective-permute-start(bf16[8,112,384]{2,1,0:T(8,128)(2,1)} %get-tuple-element.311.refs_0_), channel_id=1, source_target_pairs={{0,2},{1,3},{2,4},{3,5},{4,6},{5,7},{8,10},{9,11},{10,12},{11,13},... | collective-permute-start | bytes 2064392 | tf_op jit(solution)/shard_map/ppermute | solution.py:666
  1464.0 37.4 %collective-permute-start.74 = (bf16[8,112,384]{2,1,0:T(8,128)(2,1)}, bf16[8,112,384]{2,1,0:T(8,128)(2,1)}, u32[]{:S(2)}, u32[]{:S(2)}) collective-permute-start(bf16[8,112,384]{2,1,0:T(8,128)(2,1)} %get-tuple-element.312), channel_id=1, source_target_pairs={{2,0},{3,1},{4,2},{5,3},{6,4},{7,5},{10,8},{11,9},{12,10},{13,11},... | collective-permute-start | bytes 2064392 | tf_op jit(solution)/shard_map/ppermute | solution.py:666
  1486.2 46.6 %all-to-all-start.9 = ((bf16[16,112,384]{2,1,0:T(8,128)(2,1)}), bf16[16,112,384]{2,1,0:T(8,128)(2,1)}, u32[]{:S(2)}, u32[]{:S(2)}) async-start(bf16[16,112,384]{2,1,0:T(8,128)(2,1)} %bitcast.55), calls=%async_computation.9 | async-start | bytes 2752512 | tf_op jit(solution)/shard_map/all_to_all | solution.py:575
  1494.7 42.2 %collective-permute-start.79 = (bf16[8,112,384]{2,1,0:T(8,128)(2,1)}, bf16[8,112,384]{2,1,0:T(8,128)(2,1)}, u32[]{:S(2)}, u32[]{:S(2)}) collective-permute-start(bf16[8,112,384]{2,1,0:T(8,128)(2,1)} %get-tuple-element.323), channel_id=1, source_target_pairs={{0,2},{1,3},{2,4},{3,5},{4,6},{5,7},{8,10},{9,11},{10,12},{11,13},... | collective-permute-start | bytes 2064392 | tf_op jit(solution)/shard_map/ppermute | solution.py:666
  1500.1 36.8 %collective-permute-start.80 = (bf16[8,112,384]{2,1,0:T(8,128)(2,1)}, bf16[8,112,384]{2,1,0:T(8,128)(2,1)}, u32[]{:S(2)}, u32[]{:S(2)}) collective-permute-start(bf16[8,112,384]{2,1,0:T(8,128)(2,1)} %get-tuple-element.324), channel_id=1, source_target_pairs={{2,0},{3,1},{4,2},{5,3},{6,4},{7,5},{10,8},{11,9},{12,10},{13,11},... | collective-permute-start | bytes 2064392 | tf_op jit(solution)/shard_map/ppermute | solution.py:666
  1505.8 42.2 %collective-permute-start.77 = (bf16[8,112,384]{2,1,0:T(8,128)(2,1)}, bf16[8,112,384]{2,1,0:T(8,128)(2,1)}, u32[]{:S(2)}, u32[]{:S(2)}) collective-permute-start(bf16[8,112,384]{2,1,0:T(8,128)(2,1)} %get-tuple-element.320.refs_0_), channel_id=1, source_target_pairs={{0,2},{1,3},{2,4},{3,5},{4,6},{5,7},{8,10},{9,11},{10,12},{11,13},... | collective-permute-start | bytes 2064392 | tf_op jit(solution)/shard_map/ppermute | solution.py:666
  1511.1 36.9 %collective-permute-start.78 = (bf16[8,112,384]{2,1,0:T(8,128)(2,1)}, bf16[8,112,384]{2,1,0:T(8,128)(2,1)}, u32[]{:S(2)}, u32[]{:S(2)}) collective-permute-start(bf16[8,112,384]{2,1,0:T(8,128)(2,1)} %get-tuple-element.322), channel_id=1, source_target_pairs={{2,0},{3,1},{4,2},{5,3},{6,4},{7,5},{10,8},{11,9},{12,10},{13,11},... | collective-permute-start | bytes 2064392 | tf_op jit(solution)/shard_map/ppermute | solution.py:666
  1532.8 57.4 %all-to-all-start.8 = ((bf16[16,112,384]{2,1,0:T(8,128)(2,1)}), bf16[16,112,384]{2,1,0:T(8,128)(2,1)S(1)}, u32[]{:S(2)}, u32[]{:S(2)}) async-start(bf16[16,112,384]{2,1,0:T(8,128)(2,1)} %bitcast.52), calls=%async_computation.8 | async-start | bytes 2752512 | tf_op jit(solution)/shard_map/all_to_all | solution.py:575
  1541.3 38.0 %collective-permute-start.83 = (bf16[8,112,384]{2,1,0:T(8,128)(2,1)}, bf16[8,112,384]{2,1,0:T(8,128)(2,1)}, u32[]{:S(2)}, u32[]{:S(2)}) collective-permute-start(bf16[8,112,384]{2,1,0:T(8,128)(2,1)} %get-tuple-element.331), channel_id=1, source_target_pairs={{0,2},{1,3},{2,4},{3,5},{4,6},{5,7},{8,10},{9,11},{10,12},{11,13},... | collective-permute-start | bytes 2064392 | tf_op jit(solution)/shard_map/ppermute | solution.py:666
  1552.2 43.3 %collective-permute-start.81 = (bf16[8,112,384]{2,1,0:T(8,128)(2,1)}, bf16[8,112,384]{2,1,0:T(8,128)(2,1)}, u32[]{:S(2)}, u32[]{:S(2)}) collective-permute-start(bf16[8,112,384]{2,1,0:T(8,128)(2,1)} %get-tuple-element.329.refs_0_), channel_id=1, source_target_pairs={{0,2},{1,3},{2,4},{3,5},{4,6},{5,7},{8,10},{9,11},{10,12},{11,13},... | collective-permute-start | bytes 2064392 | tf_op jit(solution)/shard_map/ppermute | solution.py:666
  1557.6 38.0 %collective-permute-start.82 = (bf16[8,112,384]{2,1,0:T(8,128)(2,1)}, bf16[8,112,384]{2,1,0:T(8,128)(2,1)}, u32[]{:S(2)}, u32[]{:S(2)}) collective-permute-start(bf16[8,112,384]{2,1,0:T(8,128)(2,1)} %get-tuple-element.330), channel_id=1, source_target_pairs={{2,0},{3,1},{4,2},{5,3},{6,4},{7,5},{10,8},{11,9},{12,10},{13,11},... | collective-permute-start | bytes 2064392 | tf_op jit(solution)/shard_map/ppermute | solution.py:666
  1583.6 52.3 %collective-permute-start.85 = (bf16[8,112,384]{2,1,0:T(8,128)(2,1)}, bf16[8,112,384]{2,1,0:T(8,128)(2,1)}, u32[]{:S(2)}, u32[]{:S(2)}) collective-permute-start(bf16[8,112,384]{2,1,0:T(8,128)(2,1)} %get-tuple-element.340), channel_id=1, source_target_pairs={{0,2},{1,3},{2,4},{3,5},{4,6},{5,7},{8,10},{9,11},{10,12},{11,13},... | collective-permute-start | bytes 2064392 | tf_op jit(solution)/shard_map/ppermute | solution.py:666
  1589.0 47.0 %collective-permute-start.86 = (bf16[8,112,384]{2,1,0:T(8,128)(2,1)}, bf16[8,112,384]{2,1,0:T(8,128)(2,1)}, u32[]{:S(2)}, u32[]{:S(2)}) collective-permute-start(bf16[8,112,384]{2,1,0:T(8,128)(2,1)} %get-tuple-element.341), channel_id=1, source_target_pairs={{2,0},{3,1},{4,2},{5,3},{6,4},{7,5},{10,8},{11,9},{12,10},{13,11},... | collective-permute-start | bytes 2064392 | tf_op jit(solution)/shard_map/ppermute | solution.py:666
  1651.0 124.0 %all-gather.6.cloned.1.call-start = ((), (), s32[]{:S(2)}) async-start(), calls=%async_computation.14 | async-start | bytes 1327104 | tf_op jit(solution)/shard_map/all_gather | solution.py:656
  1677.8 132.6 %all-gather.4.cloned.1.call-start = ((), (), s32[]{:S(2)}) async-start(), calls=%async_computation.13 | async-start | bytes 1474560 | tf_op jit(solution)/shard_map/all_gather | solution.py:658
  (137 other events, 2481.3 us)
Sparse Core Ops, SparseCore 0:
  1677.9 30.4 all-gather.5
  1777.3 29.2 all-gather.3

commit v3 on v2

--- a/solution.py
+++ b/solution.py
@@ -16,8 +16,6 @@
 PARTS = 2
 PIECES = 4
 CHUNK = 8
-EARLY = (-10, -8, -6, -4)
-LATE = (5, 7, 9, 11)
 DELAY = 2
 LANES = 128
 VMEM = 62 * 1024 * 1024
@@ -91,17 +89,18 @@
         target = final.at[:, pl.ds(has_final * row_block, row_block), :]
         return pltpu.make_async_copy(out.at[way], target, final_sem)
 
-    for way in range(2):
+    def fetch(way):
         table_copy(way).start()
         for part in range(2):
             for which, pair in enumerate(((fields, fields_other), (cot, cot_other))):
                 @pl.when((scal[t, 3 * way] != 0) if which else (scal[t, 3 * way] == 0))
-                def _(way=way, part=part, pair=pair):
+                def _(part=part, pair=pair):
                     for who in range(2):
                         row_copy(way, who, part, pair[who]).start()
         if has_recv:
             recv_copy(way).start()
-    for way in range(2):
+
+    def work(way):
         table_copy(way).wait()
         for part in range(2):
             for who in range(2):
@@ -121,11 +120,15 @@
                 value = value + recv_now[way, :, :, lanes].astype(F32)
             out[way, :, :, lanes] = value.astype(BF16)
         out_copy(way).start()
+
+    for step in (fetch, work):
+        for way in range(2):
+            pl.when(scal[t, 8 + way] != 0)(functools.partial(step, way))
     if has_final is not None:
         pl.when(scal[t, 7] == 0)(lambda: final_copy(1).start())
         pl.when(scal[t, 7] != 0)(lambda: final_copy(0).start())
     for way in range(2):
-        out_copy(way).wait()
+        pl.when(scal[t, 8 + way] != 0)(lambda way=way: out_copy(way).wait())
     if has_final is not None:
         final_copy(0).wait()
 
@@ -434,35 +437,23 @@
 
 
 def pick_body(core, array, *refs):
-    out, sems = refs[-2:]
-    rows, _, half = out.shape
-    step = rows // sems.shape[0]
-    lanes = pl.ds(pl.multiple_of((1 - core[0]) * half, LANES), half)
-    copies = [
-        pltpu.make_async_copy(
-            array.at[pl.ds(i * step, step), :, lanes], out.at[pl.ds(i * step, step)], sems.at[i]
-        )
-        for i in range(sems.shape[0])
-    ]
-    for copy in copies:
-        copy.start()
-    for copy in copies:
-        copy.wait()
-
-
-def pick(core, array, rows, *ties):
+    refs[-1][...] = array[...]
+
+
+def pick(core, array, rows, row_block, *ties):
     _, cols, width = array.shape
+    half = width // 2
     anywhere = pl.BlockSpec(memory_space=pl.ANY)
     return pl.pallas_call(
         pick_body,
         grid_spec=pltpu.PrefetchScalarGridSpec(
             num_scalar_prefetch=1,
-            grid=(),
-            in_specs=[anywhere] * (1 + len(ties)),
-            out_specs=anywhere,
-            scratch_shapes=[pltpu.SemaphoreType.DMA((8,))],
-        ),
-        out_shape=jax.ShapeDtypeStruct((rows, cols, width // 2), BF16),
+            grid=(rows // row_block,),
+            in_specs=[pl.BlockSpec((row_block, cols, half), lambda i, s: (i, 0, 1 - s[0]))]
+            + [anywhere] * len(ties),
+            out_specs=pl.BlockSpec((row_block, cols, half), lambda i, s: (i, 0, 0)),
+        ),
+        out_shape=jax.ShapeDtypeStruct((rows, cols, half), BF16),
         compiler_params=params(),
         cost_estimate=pl.CostEstimate(
             flops=0, bytes_accessed=2 * rows * cols * width, transcendentals=0
@@ -510,8 +501,8 @@
     downward = [(i + 2, i) for i in range(lon_count - 2)]
 
     core_now = core.reshape(1).astype(jnp.int32)
-    first_sent = pick(core_now, fields, DELAY * row_block)
-    fields_sent = pick(core_now, fields, rows, first_sent)
+    first_sent = pick(core_now, fields, DELAY * row_block, row_block)
+    fields_sent = pick(core_now, fields, rows, row_block, first_sent)
     fields_first = lax.ppermute(first_sent, "lon", swap)
     fields_other = lax.ppermute(fields_sent, "lon", swap)
     cot_other = None
@@ -567,50 +558,39 @@
         v = jnp.clip(slot_ids - DELAY * late, 0, count - 1)
         return [v // blocks % 2, v % blocks, v // (2 * blocks)]
 
+    def has_chunk(late):
+        v = slot_ids - DELAY * late
+        return ((v >= 0) & (v < count)).astype(jnp.int32)
+
     flat = jnp.zeros_like(slot_ids)
-    scal = jnp.stack(
-        schedule(chip) + schedule(chips - 1 - chip) + [flat + core, flat + chip], axis=1
+    hop_plan = jnp.stack(
+        schedule(chip)
+        + schedule(chips - 1 - chip)
+        + [flat + core, flat + chip, has_chunk(chip), has_chunk(chips - 1 - chip)],
+        axis=1,
     )
     def across(array):
         return lax.all_to_all(array, "lat", split_axis=0, concat_axis=0, tiled=True)
 
-    spread = []
-    gradients = 0.0
-
-    def filter_piece(s, piece, *ties):
-        nonlocal gradients
-        shape = (lat_count, 2, per_part, rows, half)
-        adjoint, part = spectral_filter(
-            piece * per_piece, per_piece,
-            every_row[s, 0].reshape(shape), every_row[s, 1].reshape(shape),
-            forward, backward, inner, inner_t, outer_t, *ties,
-        )
-        gradients = gradients + part
-        spread.append(across(adjoint.reshape(-1, rows, half)))
-        return adjoint
-
-    sent = {}
-    gathered = {}
-    every_row = {}
-    for t in range(slots):
+    last = []
+    sent, gathered, every_row, spread, terms = {}, {}, {}, [], []
+    others = {"cot": None}
+
+    def hop_slot(t):
         v = t - DELAY * (chips - 1)
         if t < DELAY:
             arrays = (fields, fields, fields_first, fields_first)
         elif t < blocks:
             arrays = (fields, fields, fields_other, fields_other)
         else:
-            arrays = (fields, cotangent, fields_other, cot_other)
-        if t == DELAY:
-            cot_other = lax.ppermute(pick(core_now, cotangent, rows, result[0]), "lon", swap)
+            arrays = (fields, cotangent, fields_other, others["cot"])
         recv = sent.pop(t - DELAY, None)
         key, final_at, prev = None, None, None
         if v >= 0:
             key, final_at = order[v][:2], order[v][2]
             prev = gathered.get(key)
-        ties = []
-        if t - slots in EARLY:
-            ties.append(filter_piece(0, EARLY.index(t - slots), result[0]))
-        result = hop(t, scal, arrays, tables, recv, prev, final_at, row_block, rows, ties)
+        result = hop(t, hop_plan, arrays, tables, recv, prev, final_at, row_block, rows, last)
+        last[:] = [result[0]]
         if v >= 0:
             gathered[key] = result[2]
             if final_at == blocks - 1:
@@ -620,50 +600,78 @@
                 lax.ppermute(result[0], "lon", upward),
                 lax.ppermute(result[1], "lon", downward),
             )
-    def add_up(terms):
+        if t == DELAY - 1:
+            cot_sent = pick(core_now, cotangent, rows, row_block, *last)
+            last[:] = [cot_sent]
+            others["cot"] = lax.ppermute(cot_sent, "lon", swap)
+
+    def filter_piece(n):
+        s, piece = n // PIECES, n % PIECES
+        shape = (lat_count, 2, per_part, rows, half)
+        adjoint, part = spectral_filter(
+            piece * per_piece, per_piece,
+            every_row[s, 0].reshape(shape), every_row[s, 1].reshape(shape),
+            forward, backward, inner, inner_t, outer_t, *last,
+        )
+        last[:] = [adjoint]
+        terms.append(part)
+        spread.append(across(adjoint.reshape(-1, rows, half)))
+
+    def add_up():
         at_end = (chip == 0) | (chip == chips - 1)
-        terms = jnp.where(at_end, terms, 0.0).reshape(lat_count, -1, LANES)
-        return jnp.sum(across(terms), axis=0)
+        now = jnp.where(at_end, sum(terms), 0.0).reshape(lat_count, -1, LANES)
+        return jnp.sum(across(now), axis=0)
 
     per_spread = coefs // (PIECES * CHUNK)
-    count = PARTS * PIECES * per_spread
-    slots = count + DELAY * (chips - 1)
-    slot_ids = jnp.arange(slots, dtype=jnp.int32)
+    relay_count = PARTS * PIECES * per_spread
+    relay_slots = relay_count + DELAY * (chips - 1)
+    relay_ids = jnp.arange(relay_slots, dtype=jnp.int32)
 
     def place_of(late):
-        v = slot_ids - DELAY * late
-        return jnp.where((v >= 0) & (v < count), v, count)
-
-    flat = jnp.zeros_like(slot_ids)
-    scal = jnp.stack(
+        v = relay_ids - DELAY * late
+        return jnp.where((v >= 0) & (v < relay_count), v, relay_count)
+
+    flat = jnp.zeros_like(relay_ids)
+    relay_plan = jnp.stack(
         [place_of(chip), place_of(chips - 1 - chip),
          flat + (chip == 0), flat + (chip == chips - 1)], axis=1
     ).astype(jnp.int32)
-    sent = {}
-    kept = None
+    passed = {}
+    kept = []
+
+    def relay_slot(t, *ties):
+        own, own_at = (None, None)
+        if t < relay_count:
+            own, own_at = spread[t // per_spread], t % per_spread
+        up, down, *kept[:] = relay(
+            t, relay_plan, own, own_at, passed.pop(t - DELAY, None), tuple(kept) or None,
+            relay_count, (CHUNK, rows, half), last + list(ties),
+        )
+        last[:] = [up]
+        if t < relay_count + DELAY * (chips - 2):
+            passed[t] = (lax.ppermute(up, "lon", upward), lax.ppermute(down, "lon", downward))
+
     for t in range(slots):
-        own, own_at = (None, None)
-        if t < count:
-            own, own_at = spread[t // per_spread], t % per_spread
+        if t in (slots - 9, slots - 6):
+            filter_piece(len(spread))
+        hop_slot(t)
+        if slots - 6 <= t < slots - 2:
+            relay_slot(t - slots + 6)
+    filter_piece(2)
+    filter_piece(3)
+    for t in range(4, relay_slots):
+        if t in (7, 8, 10, 12):
+            filter_piece(len(spread))
         ties = []
-        if t in LATE:
-            ties.append(filter_piece(1, LATE.index(t), up))
-        if t == 0:
-            ties.append(result[0])
-        if t == LATE[-1] + 2:
-            share = add_up(gradients)
+        if t == 13:
+            share = add_up()
             ties.append(share)
             by_core = lax.all_gather(share, "lon").reshape(chips, 2, -1, LANES)
             by_core = jnp.sum(by_core, axis=0)
             sums = lax.all_gather(by_core, "lat", axis=1, tiled=True)
-        if t == slots - 1:
+        if t == relay_slots - 1:
             ties.append(by_core)
-        up, down, *kept = relay(
-            t, scal, own, own_at, sent.pop(t - DELAY, None), kept, count,
-            (CHUNK, rows, half), ties,
-        )
-        if t < count + DELAY * (chips - 2):
-            sent[t] = (lax.ppermute(up, "lon", upward), lax.ppermute(down, "lon", downward))
+        relay_slot(t, *ties)
 
     whole = None
     swapped = []

time: 1860 us -> 1260 us (0.68)
  Pallas kernels: 1210 us -> 543 us
  blocking collectives: 0 us -> 61.1 us
  waiting for transfers between devices: 248 us -> 211 us
  starting transfers between devices: 328 us -> 361 us
    pallas_call x3, Pallas kernels: 671 us -> 23.4 us  [pick(): pl.pallas_call(pick_body, grid_spec=pltpu.PrefetchScalarGridSpec(num_scal...]
    all_to_all x0 -> x2, blocking collectives: none -> 61.1 us  [across(): return lax.all_to_all(array, 'lat', split_axis=0, concat_axis=0, tiled=True)]
    ppermute x105, starting transfers between devices: 269 us -> 310 us  [the longest x32 166 us: hop_slot(): lax.ppermute(result[0], 'lon', upward)]
    ppermute x105, waiting for transfers between devices: 236 us -> 211 us  [the longest x32 70.9 us: hop_slot(): lax.ppermute(result[1], 'lon', downward)]
    pallas_call x34, Pallas kernels: 244 us -> 220 us  [hop(): pl.pallas_call(functools.partial(hop_body, t, row_block, recv is not None...]
    all_to_all x13 -> x11, starting transfers between devices: 57.9 us -> 49.5 us  [across(): return lax.all_to_all(array, 'lat', split_axis=0, concat_axis=0, tiled=True)]
  transfers between devices with their start and end apart: 124 -> 122, of which waited for: 56 -> 55; matrix products, arithmetic and copies ran while one was open for 2% -> 3% of each run, Pallas kernels for 60% -> 43%
where the time goes in v3:
time: 1260 us; the launch traced here: 1240 us
  Pallas kernels  543 us (43%)
  starting transfers between devices  361 us (29%)
  waiting for transfers between devices  211 us (17%)
  blocking collectives  61.1 us (5%)
  other arithmetic  25.3 us (2%)
  local copies, waits for them, and re-layouts  21.8 us (2%)
  between operations  16.3 us (1%)
    pallas_call x34, Pallas kernels, hop(): pl.pallas_call(functools.partial(hop_body, t, row_block, recv is not None...  220 us
    ppermute x32, starting transfers between devices, hop_slot(): lax.ppermute(result[0], 'lon', upward)  166 us
    pallas_call x8, Pallas kernels, spectral_filter(): pl.pallas_call(filter_body, grid=(modes,), in_specs=[data, data, square,...  164 us
    pallas_call x22, Pallas kernels, relay(): pl.pallas_call(functools.partial(relay_body, t, own is not None, recv is...  89 us
    ppermute x20, starting transfers between devices, relay_slot(): lax.ppermute(up, 'lon', upward)  76.1 us
    ppermute x32, waiting for transfers between devices, hop_slot(): lax.ppermute(result[1], 'lon', downward)  70.9 us
    ppermute x20, waiting for transfers between devices, relay_slot(): lax.ppermute(down, 'lon', downward)  63.1 us
    all_to_all x2, blocking collectives, across(): return lax.all_to_all(array, 'lat', split_axis=0, concat_axis=0, tiled=True)  61.1 us
  transfers between devices with their start and end apart: 122, of which 55 were waited for; matrix products, arithmetic and copies ran while one was open for 3% of the time, Pallas kernels for 43%

profile of v3, /device:TPU:0, one launch (start us, length us, event | category | flops | bytes accessed | tf_op | source)
XLA Modules:
  0.0 1239.5 jit_solution(10935165941972634040)
XLA Ops:
  10.7 10.1 pick.4
  34.1 10.2 pick.5.refs_7_
  52.0 12.2 collective-permute-done.3.refs_5_
  110.0 10.4 collective-permute-start.9
  144.3 7.7 collective-permute-start.13
  171.3 7.5 longitude_hop.42
  188.3 7.5 longitude_hop.43
  205.5 7.4 longitude_hop.44
  238.0 7.4 longitude_hop.46
  263.8 9.9 collective-permute-done.27.refs_5_
  376.6 7.4 longitude_hop.53
  401.7 9.8 collective-permute-done.37.refs_5_
  476.6 7.4 longitude_hop.57
  489.9 7.5 longitude_hop.58
  504.2 20.5 %spectral_filter.8 = (bf16[4,2,2,112,384]{4,3,2,1,0:T(8,128)(2,1)}, f32[2,4,2,96,96]{4,3,2,1,0:T(8,128)}) custom-call(bf16[4,2,8,112,384]{4,3,2,1,0:T(8,128)(2,1)} %bitcast.2.spectrum, bf16[4,2,8,112,384]{4,3,2,1,0:T(8,128)(2,1)} %bitcast.3.pulled, bf16[896,896]{1,0:T(8,128)(2,1)} %get-tuple-element.404.forward, ...), custom_call_target="tpu_custom_call" | custom-call | flops 8984199168 | bytes 4128768 | tf_op jit(solution)/shard_map/spectral_filter/pallas_call | solution.py:255
  543.7 7.4 longitude_hop.60
  559.6 20.5 %spectral_filter.9 = (bf16[4,2,2,112,384]{4,3,2,1,0:T(8,128)(2,1)}, f32[2,4,2,96,96]{4,3,2,1,0:T(8,128)}) custom-call(bf16[4,2,8,112,384]{4,3,2,1,0:T(8,128)(2,1)} %bitcast.2.spectrum, bf16[4,2,8,112,384]{4,3,2,1,0:T(8,128)(2,1)} %bitcast.3.pulled, bf16[896,896]{1,0:T(8,128)(2,1)} %get-tuple-element.404.forward, ...), custom_call_target="tpu_custom_call" | custom-call | flops 8984199168 | bytes 4128768 | tf_op jit(solution)/shard_map/spectral_filter/pallas_call | solution.py:255
  580.1 31.6 %all_to_all.65.refs_0_ = bf16[16,112,384]{2,1,0:T(8,128)(2,1)} all-to-all(bf16[16,112,384]{2,1,0:T(8,128)(2,1)} %bitcast.55), channel_id=1, replica_groups=mesh['lat'=4,'lon'=8] {'lat'}, dimensions={0} | all-to-all | bytes 2752512 | tf_op jit(solution)/shard_map/all_to_all | solution.py:573
  658.3 7.4 collective-permute-start.59
  688.1 10.3 collective-permute-done.63.refs_1_
  721.5 19.0 %collective-permute-done.70.refs_2_ = bf16[8,112,384]{2,1,0:T(8,128)(2,1)} collective-permute-done((bf16[8,112,384]{2,1,0:T(8,128)(2,1)}, bf16[8,112,384]{2,1,0:T(8,128)(2,1)}, u32[]{:S(2)}, u32[]{:S(2)}) %collective-permute-start.70) | collective-permute-done | bytes 688160 | tf_op jit(solution)/shard_map/ppermute | solution.py:652
  755.9 20.5 %spectral_filter.10 = (bf16[4,2,2,112,384]{4,3,2,1,0:T(8,128)(2,1)}, f32[2,4,2,96,96]{4,3,2,1,0:T(8,128)}) custom-call(bf16[4,2,8,112,384]{4,3,2,1,0:T(8,128)(2,1)} %bitcast.2.spectrum, bf16[4,2,8,112,384]{4,3,2,1,0:T(8,128)(2,1)} %bitcast.3.pulled, bf16[896,896]{1,0:T(8,128)(2,1)} %get-tuple-element.404.forward, ...), custom_call_target="tpu_custom_call" | custom-call | flops 8984199168 | bytes 4128768 | tf_op jit(solution)/shard_map/spectral_filter/pallas_call | solution.py:255
  779.9 20.5 %spectral_filter.11 = (bf16[4,2,2,112,384]{4,3,2,1,0:T(8,128)(2,1)}, f32[2,4,2,96,96]{4,3,2,1,0:T(8,128)}) custom-call(bf16[4,2,8,112,384]{4,3,2,1,0:T(8,128)(2,1)} %bitcast.2.spectrum, bf16[4,2,8,112,384]{4,3,2,1,0:T(8,128)(2,1)} %bitcast.3.pulled, bf16[896,896]{1,0:T(8,128)(2,1)} %get-tuple-element.404.forward, ...), custom_call_target="tpu_custom_call" | custom-call | flops 8984199168 | bytes 4128768 | tf_op jit(solution)/shard_map/spectral_filter/pallas_call | solution.py:255
  800.4 29.5 %all_to_all.66.refs_0_ = bf16[16,112,384]{2,1,0:T(8,128)(2,1)} all-to-all(bf16[16,112,384]{2,1,0:T(8,128)(2,1)} %bitcast.53), channel_id=1, replica_groups=mesh['lat'=4,'lon'=8] {'lat'}, dimensions={0} | all-to-all | bytes 2752512 | tf_op jit(solution)/shard_map/all_to_all | solution.py:573
  874.9 20.5 %spectral_filter.12 = (bf16[4,2,2,112,384]{4,3,2,1,0:T(8,128)(2,1)}, f32[2,4,2,96,96]{4,3,2,1,0:T(8,128)}) custom-call(bf16[4,2,8,112,384]{4,3,2,1,0:T(8,128)(2,1)} %bitcast.10.spectrum, bf16[4,2,8,112,384]{4,3,2,1,0:T(8,128)(2,1)} %bitcast.13.pulled, bf16[896,896]{1,0:T(8,128)(2,1)} %get-tuple-element.404.forward, ...), custom_call_target="tpu_custom_call" | custom-call | flops 8984199168 | bytes 4128768 | tf_op jit(solution)/shard_map/spectral_filter/pallas_call | solution.py:255
  916.9 20.5 %spectral_filter.13 = (bf16[4,2,2,112,384]{4,3,2,1,0:T(8,128)(2,1)}, f32[2,4,2,96,96]{4,3,2,1,0:T(8,128)}) custom-call(bf16[4,2,8,112,384]{4,3,2,1,0:T(8,128)(2,1)} %bitcast.10.spectrum, bf16[4,2,8,112,384]{4,3,2,1,0:T(8,128)(2,1)} %bitcast.13.pulled, bf16[896,896]{1,0:T(8,128)(2,1)} %get-tuple-element.404.forward, ...), custom_call_target="tpu_custom_call" | custom-call | flops 8984199168 | bytes 4128768 | tf_op jit(solution)/shard_map/spectral_filter/pallas_call | solution.py:255
  964.5 20.5 %spectral_filter.14 = (bf16[4,2,2,112,384]{4,3,2,1,0:T(8,128)(2,1)}, f32[2,4,2,96,96]{4,3,2,1,0:T(8,128)}) custom-call(bf16[4,2,8,112,384]{4,3,2,1,0:T(8,128)(2,1)} %bitcast.10.spectrum, bf16[4,2,8,112,384]{4,3,2,1,0:T(8,128)(2,1)} %bitcast.13.pulled, bf16[896,896]{1,0:T(8,128)(2,1)} %get-tuple-element.404.forward, ...), custom_call_target="tpu_custom_call" | custom-call | flops 8984199168 | bytes 4128768 | tf_op jit(solution)/shard_map/spectral_filter/pallas_call | solution.py:255
  998.8 20.4 %spectral_filter.15 = (bf16[4,2,2,112,384]{4,3,2,1,0:T(8,128)(2,1)}, f32[2,4,2,96,96]{4,3,2,1,0:T(8,128)}) custom-call(bf16[4,2,8,112,384]{4,3,2,1,0:T(8,128)(2,1)} %bitcast.10.spectrum, bf16[4,2,8,112,384]{4,3,2,1,0:T(8,128)(2,1)} %bitcast.13.pulled, bf16[896,896]{1,0:T(8,128)(2,1)} %get-tuple-element.404.forward, ...), custom_call_target="tpu_custom_call" | custom-call | flops 8984199168 | bytes 4128768 | tf_op jit(solution)/shard_map/spectral_filter/pallas_call | solution.py:255
  1090.5 9.5 collective-permute-done.91.refs_1_
  1100.0 7.8 collective-permute-done.92.refs_2_
  1181.1 20.0 %longitude_grid.2 = (bf16[112,112,768]{2,1,0:T(8,128)(2,1)}, bf16[64,112,384]{2,1,0:T(8,128)(2,1)}) custom-call(s32[1]{0:T(128)} %bitcast.core, bf16[17,8,112,384]{3,2,1,0:T(8,128)(2,1)} %get-tuple-element.395.refs_0_, bf16[17,8,112,384]{3,2,1,0:T(8,128)(2,1)} %get-tuple-element.396.refs_1_, bf16[2,112,256]{2,1,0:T(8,128)(2,1)} %fusion.21.refs_2_), custom_call_target="tpu_custom_call" | custom-call | flops 2818572288 | bytes 23592960 | tf_op jit(solution)/shard_map/longitude_grid/pallas_call | solution.py:388
  1201.1 15.9 %longitude_grid.3 = (bf16[112,112,768]{2,1,0:T(8,128)(2,1)}, bf16[48,112,384]{2,1,0:T(8,128)(2,1)}) custom-call(s32[1]{0:T(128)} %bitcast.core, bf16[17,8,112,384]{3,2,1,0:T(8,128)(2,1)} %get-tuple-element.395.refs_0_, bf16[17,8,112,384]{3,2,1,0:T(8,128)(2,1)} %get-tuple-element.396.refs_1_, ...), custom_call_target="tpu_custom_call", output_to_operand_aliasing={{0}: (4, {})} | custom-call | flops 2113929216 | bytes 17694720 | tf_op jit(solution)/shard_map/longitude_grid/pallas_call | solution.py:388
  (456 shorter events, 779.1 us)
Async XLA Ops:
  20.8 46.9 %collective-permute-start = (bf16[112,112,384]{2,1,0:T(8,128)(2,1)}, bf16[112,112,384]{2,1,0:T(8,128)(2,1)}, u32[]{:S(2)}, u32[]{:S(2)}) collective-permute-start(bf16[112,112,384]{2,1,0:T(8,128)(2,1)} %pick.4), channel_id=1, source_target_pairs={{0,1},{1,0},{2,3},{3,2},{4,5},{5,4},{6,7},{7,6},{8,9},{9,8},{10,11... | collective-permute-start | bytes 28901384 | tf_op jit(solution)/shard_map/ppermute | solution.py:507
  44.3 109.0 %collective-permute-start.2 = (bf16[112,112,384]{2,1,0:T(8,128)(2,1)}, bf16[112,112,384]{2,1,0:T(8,128)(2,1)}, u32[]{:S(2)}, u32[]{:S(2)}) collective-permute-start(bf16[112,112,384]{2,1,0:T(8,128)(2,1)} %pick.5.refs_7_), channel_id=1, source_target_pairs={{0,1},{1,0},{2,3},{3,2},{4,5},{5,4},{6,7},{7,6},{8,9},{9,8},{10,11... | collective-permute-start | bytes 28901384 | tf_op jit(solution)/shard_map/ppermute | solution.py:606
  245.4 138.7 %all-to-all-start = ((bf16[64,112,384]{2,1,0:T(8,128)(2,1)}), bf16[64,112,384]{2,1,0:T(8,128)(2,1)}, u32[]{:S(2)}, u32[]{:S(2)}) async-start(bf16[64,112,384]{2,1,0:T(8,128)(2,1)} %get-tuple-element.269), calls=%async_computation | async-start | bytes 11010048 | tf_op jit(solution)/shard_map/all_to_all | solution.py:573
  384.1 120.2 %all-to-all-start.1 = ((bf16[64,112,384]{2,1,0:T(8,128)(2,1)}), bf16[64,112,384]{2,1,0:T(8,128)(2,1)}, u32[]{:S(2)}, u32[]{:S(2)}) async-start(bf16[64,112,384]{2,1,0:T(8,128)(2,1)} %get-tuple-element.270), calls=%async_computation.1 | async-start | bytes 11010048 | tf_op jit(solution)/shard_map/all_to_all | solution.py:573
  394.9 36.6 %collective-permute-start.43 = (bf16[64,16,384]{2,1,0:T(8,128)(2,1)}, bf16[64,16,384]{2,1,0:T(8,128)(2,1)}, u32[]{:S(2)}, u32[]{:S(2)}) collective-permute-start(bf16[64,16,384]{2,1,0:T(8,128)(2,1)} %get-tuple-element.252.refs_7_), channel_id=1, source_target_pairs={{0,2},{1,3},{2,4},{3,5},{4,6},{5,7},{8,10},{9,11},{10,12},{11,13},... | collective-permute-start | bytes 2359304 | tf_op jit(solution)/shard_map/ppermute | solution.py:600
  484.0 40.7 %collective-permute-start.51 = (bf16[64,16,384]{2,1,0:T(8,128)(2,1)}, bf16[64,16,384]{2,1,0:T(8,128)(2,1)S(1)}, u32[]{:S(2)}, u32[]{:S(2)}) collective-permute-start(bf16[64,16,384]{2,1,0:T(8,128)(2,1)} %get-tuple-element.264.refs_8_), channel_id=1, source_target_pairs={{0,2},{1,3},{2,4},{3,5},{4,6},{5,7},{8,10},{9,11},{10,12},{11,13},... | collective-permute-start | bytes 2359304 | tf_op jit(solution)/shard_map/ppermute | solution.py:600
  488.6 36.2 %collective-permute-start.52 = (bf16[64,16,384]{2,1,0:T(8,128)(2,1)}, bf16[64,16,384]{2,1,0:T(8,128)(2,1)S(1)}, u32[]{:S(2)}, u32[]{:S(2)}) collective-permute-start(bf16[64,16,384]{2,1,0:T(8,128)(2,1)} %get-tuple-element.267), channel_id=1, source_target_pairs={{2,0},{3,1},{4,2},{5,3},{6,4},{7,5},{10,8},{11,9},{12,10},{13,11},... | collective-permute-start | bytes 2359304 | tf_op jit(solution)/shard_map/ppermute | solution.py:601
  497.4 46.3 %collective-permute-start.49 = (bf16[64,16,384]{2,1,0:T(8,128)(2,1)}, bf16[64,16,384]{2,1,0:T(8,128)(2,1)}, u32[]{:S(2)}, u32[]{:S(2)}) collective-permute-start(bf16[64,16,384]{2,1,0:T(8,128)(2,1)} %get-tuple-element.265.refs_0_), channel_id=1, source_target_pairs={{0,2},{1,3},{2,4},{3,5},{4,6},{5,7},{8,10},{9,11},{10,12},{11,13},... | collective-permute-start | bytes 2359304 | tf_op jit(solution)/shard_map/ppermute | solution.py:600
  502.7 41.0 %collective-permute-start.50 = (bf16[64,16,384]{2,1,0:T(8,128)(2,1)}, bf16[64,16,384]{2,1,0:T(8,128)(2,1)}, u32[]{:S(2)}, u32[]{:S(2)}) collective-permute-start(bf16[64,16,384]{2,1,0:T(8,128)(2,1)} %get-tuple-element.266), channel_id=1, source_target_pairs={{2,0},{3,1},{4,2},{5,3},{6,4},{7,5},{10,8},{11,9},{12,10},{13,11},... | collective-permute-start | bytes 2359304 | tf_op jit(solution)/shard_map/ppermute | solution.py:601
  539.6 40.5 %all-to-all-start.3 = ((bf16[16,112,384]{2,1,0:T(8,128)(2,1)}), bf16[16,112,384]{2,1,0:T(8,128)(2,1)S(1)}, u32[]{:S(2)}, u32[]{:S(2)}) async-start(bf16[16,112,384]{2,1,0:T(8,128)(2,1)} %bitcast.52), calls=%async_computation.3 | async-start | bytes 2752512 | tf_op jit(solution)/shard_map/all_to_all | solution.py:573
  611.7 164.7 %all-to-all-start.2 = ((bf16[64,112,384]{2,1,0:T(8,128)(2,1)}), bf16[64,112,384]{2,1,0:T(8,128)(2,1)}, u32[]{:S(2)}, u32[]{:S(2)}) async-start(bf16[64,112,384]{2,1,0:T(8,128)(2,1)} %get-tuple-element.274), calls=%async_computation.2 | async-start | bytes 11010048 | tf_op jit(solution)/shard_map/all_to_all | solution.py:573
  658.3 49.9 %collective-permute-start.59 = (bf16[64,16,384]{2,1,0:T(8,128)(2,1)}, bf16[64,16,384]{2,1,0:T(8,128)(2,1)}, u32[]{:S(2)}, u32[]{:S(2)}) collective-permute-start(bf16[64,16,384]{2,1,0:T(8,128)(2,1)} %get-tuple-element.285.refs_3_), channel_id=1, source_target_pairs={{0,2},{1,3},{2,4},{3,5},{4,6},{5,7},{8,10},{9,11},{10,12},{11,13},... | collective-permute-start | bytes 2359304 | tf_op jit(solution)/shard_map/ppermute | solution.py:600
  665.8 42.5 %collective-permute-start.60 = (bf16[64,16,384]{2,1,0:T(8,128)(2,1)}, bf16[64,16,384]{2,1,0:T(8,128)(2,1)}, u32[]{:S(2)}, u32[]{:S(2)}) collective-permute-start(bf16[64,16,384]{2,1,0:T(8,128)(2,1)} %get-tuple-element.286), channel_id=1, source_target_pairs={{2,0},{3,1},{4,2},{5,3},{6,4},{7,5},{10,8},{11,9},{12,10},{13,11},... | collective-permute-start | bytes 2359304 | tf_op jit(solution)/shard_map/ppermute | solution.py:601
  677.4 42.8 %collective-permute-start.69 = (bf16[8,112,384]{2,1,0:T(8,128)(2,1)}, bf16[8,112,384]{2,1,0:T(8,128)(2,1)}, u32[]{:S(2)}, u32[]{:S(2)}) collective-permute-start(bf16[8,112,384]{2,1,0:T(8,128)(2,1)} %get-tuple-element.291.refs_8_), channel_id=1, source_target_pairs={{0,2},{1,3},{2,4},{3,5},{4,6},{5,7},{8,10},{9,11},{10,12},{11,13},... | collective-permute-start | bytes 2064392 | tf_op jit(solution)/shard_map/ppermute | solution.py:652
  698.3 46.3 %collective-permute-start.67 = (bf16[64,16,384]{2,1,0:T(8,128)(2,1)}, bf16[64,16,384]{2,1,0:T(8,128)(2,1)S(1)}, u32[]{:S(2)}, u32[]{:S(2)}) collective-permute-start(bf16[64,16,384]{2,1,0:T(8,128)(2,1)} %get-tuple-element.296.refs_5_), channel_id=1, source_target_pairs={{0,2},{1,3},{2,4},{3,5},{4,6},{5,7},{8,10},{9,11},{10,12},{11,13},... | collective-permute-start | bytes 2359304 | tf_op jit(solution)/shard_map/ppermute | solution.py:600
  702.8 41.8 %collective-permute-start.68 = (bf16[64,16,384]{2,1,0:T(8,128)(2,1)}, bf16[64,16,384]{2,1,0:T(8,128)(2,1)S(1)}, u32[]{:S(2)}, u32[]{:S(2)}) collective-permute-start(bf16[64,16,384]{2,1,0:T(8,128)(2,1)} %get-tuple-element.300), channel_id=1, source_target_pairs={{2,0},{3,1},{4,2},{5,3},{6,4},{7,5},{10,8},{11,9},{12,10},{13,11},... | collective-permute-start | bytes 2359304 | tf_op jit(solution)/shard_map/ppermute | solution.py:601
  713.4 37.4 %collective-permute-start.65 = (bf16[64,16,384]{2,1,0:T(8,128)(2,1)}, bf16[64,16,384]{2,1,0:T(8,128)(2,1)}, u32[]{:S(2)}, u32[]{:S(2)}) collective-permute-start(bf16[64,16,384]{2,1,0:T(8,128)(2,1)} %get-tuple-element.298.refs_5_), channel_id=1, source_target_pairs={{0,2},{1,3},{2,4},{3,5},{4,6},{5,7},{8,10},{9,11},{10,12},{11,13},... | collective-permute-start | bytes 2359304 | tf_op jit(solution)/shard_map/ppermute | solution.py:600
  829.9 45.0 %all-to-all-start.5 = ((bf16[64,112,384]{2,1,0:T(8,128)(2,1)}), bf16[64,112,384]{2,1,0:T(8,128)(2,1)}, u32[]{:S(2)}, u32[]{:S(2)}) async-start(bf16[64,112,384]{2,1,0:T(8,128)(2,1)} %get-tuple-element.308), calls=%async_computation.5 | async-start | bytes 11010048 | tf_op jit(solution)/shard_map/all_to_all | solution.py:573
  862.7 43.1 %collective-permute-start.75 = (bf16[8,112,384]{2,1,0:T(8,128)(2,1)}, bf16[8,112,384]{2,1,0:T(8,128)(2,1)}, u32[]{:S(2)}, u32[]{:S(2)}) collective-permute-start(bf16[8,112,384]{2,1,0:T(8,128)(2,1)} %get-tuple-element.319.refs_5_), channel_id=1, source_target_pairs={{0,2},{1,3},{2,4},{3,5},{4,6},{5,7},{8,10},{9,11},{10,12},{11,13},... | collective-permute-start | bytes 2064392 | tf_op jit(solution)/shard_map/ppermute | solution.py:652
  868.1 37.7 %collective-permute-start.76 = (bf16[8,112,384]{2,1,0:T(8,128)(2,1)}, bf16[8,112,384]{2,1,0:T(8,128)(2,1)}, u32[]{:S(2)}, u32[]{:S(2)}) collective-permute-start(bf16[8,112,384]{2,1,0:T(8,128)(2,1)} %get-tuple-element.320), channel_id=1, source_target_pairs={{2,0},{3,1},{4,2},{5,3},{6,4},{7,5},{10,8},{11,9},{12,10},{13,11},... | collective-permute-start | bytes 2064392 | tf_op jit(solution)/shard_map/ppermute | solution.py:652
  895.4 42.0 %all-to-all-start.9 = ((bf16[16,112,384]{2,1,0:T(8,128)(2,1)}), bf16[16,112,384]{2,1,0:T(8,128)(2,1)S(1)}, u32[]{:S(2)}, u32[]{:S(2)}) async-start(bf16[16,112,384]{2,1,0:T(8,128)(2,1)} %bitcast.54), calls=%async_computation.9 | async-start | bytes 2752512 | tf_op jit(solution)/shard_map/all_to_all | solution.py:573
  899.2 43.5 %collective-permute-start.81 = (bf16[8,112,384]{2,1,0:T(8,128)(2,1)}, bf16[8,112,384]{2,1,0:T(8,128)(2,1)}, u32[]{:S(2)}, u32[]{:S(2)}) collective-permute-start(bf16[8,112,384]{2,1,0:T(8,128)(2,1)} %get-tuple-element.326.refs_0_), channel_id=1, source_target_pairs={{0,2},{1,3},{2,4},{3,5},{4,6},{5,7},{8,10},{9,11},{10,12},{11,13},... | collective-permute-start | bytes 2064392 | tf_op jit(solution)/shard_map/ppermute | solution.py:652
  904.5 38.2 %collective-permute-start.82 = (bf16[8,112,384]{2,1,0:T(8,128)(2,1)}, bf16[8,112,384]{2,1,0:T(8,128)(2,1)}, u32[]{:S(2)}, u32[]{:S(2)}) collective-permute-start(bf16[8,112,384]{2,1,0:T(8,128)(2,1)} %get-tuple-element.331), channel_id=1, source_target_pairs={{2,0},{3,1},{4,2},{5,3},{6,4},{7,5},{10,8},{11,9},{12,10},{13,11},... | collective-permute-start | bytes 2064392 | tf_op jit(solution)/shard_map/ppermute | solution.py:652
  910.0 43.6 %collective-permute-start.79 = (bf16[8,112,384]{2,1,0:T(8,128)(2,1)}, bf16[8,112,384]{2,1,0:T(8,128)(2,1)}, u32[]{:S(2)}, u32[]{:S(2)}) collective-permute-start(bf16[8,112,384]{2,1,0:T(8,128)(2,1)} %get-tuple-element.328.refs_0_), channel_id=1, source_target_pairs={{0,2},{1,3},{2,4},{3,5},{4,6},{5,7},{8,10},{9,11},{10,12},{11,13},... | collective-permute-start | bytes 2064392 | tf_op jit(solution)/shard_map/ppermute | solution.py:652
  915.4 38.1 %collective-permute-start.80 = (bf16[8,112,384]{2,1,0:T(8,128)(2,1)}, bf16[8,112,384]{2,1,0:T(8,128)(2,1)}, u32[]{:S(2)}, u32[]{:S(2)}) collective-permute-start(bf16[8,112,384]{2,1,0:T(8,128)(2,1)} %get-tuple-element.330), channel_id=1, source_target_pairs={{2,0},{3,1},{4,2},{5,3},{6,4},{7,5},{10,8},{11,9},{12,10},{13,11},... | collective-permute-start | bytes 2064392 | tf_op jit(solution)/shard_map/ppermute | solution.py:652
  938.5 46.4 %all-to-all-start.8 = ((bf16[16,112,384]{2,1,0:T(8,128)(2,1)}), bf16[16,112,384]{2,1,0:T(8,128)(2,1)S(1)}, u32[]{:S(2)}, u32[]{:S(2)}) async-start(bf16[16,112,384]{2,1,0:T(8,128)(2,1)} %bitcast.51), calls=%async_computation.8 | async-start | bytes 2752512 | tf_op jit(solution)/shard_map/all_to_all | solution.py:573
  946.9 43.3 %collective-permute-start.85 = (bf16[8,112,384]{2,1,0:T(8,128)(2,1)}, bf16[8,112,384]{2,1,0:T(8,128)(2,1)}, u32[]{:S(2)}, u32[]{:S(2)}) collective-permute-start(bf16[8,112,384]{2,1,0:T(8,128)(2,1)} %get-tuple-element.336.refs_5_), channel_id=1, source_target_pairs={{0,2},{1,3},{2,4},{3,5},{4,6},{5,7},{8,10},{9,11},{10,12},{11,13},... | collective-permute-start | bytes 2064392 | tf_op jit(solution)/shard_map/ppermute | solution.py:652
  952.3 37.9 %collective-permute-start.86 = (bf16[8,112,384]{2,1,0:T(8,128)(2,1)}, bf16[8,112,384]{2,1,0:T(8,128)(2,1)}, u32[]{:S(2)}, u32[]{:S(2)}) collective-permute-start(bf16[8,112,384]{2,1,0:T(8,128)(2,1)} %get-tuple-element.339), channel_id=1, source_target_pairs={{2,0},{3,1},{4,2},{5,3},{6,4},{7,5},{10,8},{11,9},{12,10},{13,11},... | collective-permute-start | bytes 2064392 | tf_op jit(solution)/shard_map/ppermute | solution.py:652
  957.8 36.8 %collective-permute-start.83 = (bf16[8,112,384]{2,1,0:T(8,128)(2,1)}, bf16[8,112,384]{2,1,0:T(8,128)(2,1)}, u32[]{:S(2)}, u32[]{:S(2)}) collective-permute-start(bf16[8,112,384]{2,1,0:T(8,128)(2,1)} %get-tuple-element.337.refs_0_), channel_id=1, source_target_pairs={{0,2},{1,3},{2,4},{3,5},{4,6},{5,7},{8,10},{9,11},{10,12},{11,13},... | collective-permute-start | bytes 2064392 | tf_op jit(solution)/shard_map/ppermute | solution.py:652
  986.0 38.0 %all-to-all-start.11 = ((bf16[16,112,384]{2,1,0:T(8,128)(2,1)}), bf16[16,112,384]{2,1,0:T(8,128)(2,1)S(1)}, u32[]{:S(2)}, u32[]{:S(2)}) async-start(bf16[16,112,384]{2,1,0:T(8,128)(2,1)} %bitcast.50), calls=%async_computation.11 | async-start | bytes 2752512 | tf_op jit(solution)/shard_map/all_to_all | solution.py:573
  1045.9 119.8 %all-gather.6.cloned.1.call-start = ((), (), s32[]{:S(2)}) async-start(), calls=%async_computation.14 | async-start | bytes 1327104 | tf_op jit(solution)/shard_map/all_gather | solution.py:669
  1075.8 125.3 %all-gather.4.cloned.1.call-start = ((), (), s32[]{:S(2)}) async-start(), calls=%async_computation.13 | async-start | bytes 1474560 | tf_op jit(solution)/shard_map/all_gather | solution.py:671
  (145 other events, 2403.1 us)
Sparse Core Ops, SparseCore 0:
  1075.9 30.0 all-gather.5
  1167.9 28.1 all-gather.3

commit v4 on v3

--- a/solution.py
+++ b/solution.py
@@ -13,9 +13,9 @@
 MODES = 128
 BLOCKS = 8
 BLOCK_W = 96
-PARTS = 2
-PIECES = 4
+PARTS = 4
 CHUNK = 8
+FIRST = 3
 DELAY = 2
 LANES = 128
 VMEM = 62 * 1024 * 1024
@@ -48,7 +48,7 @@
     return pltpu.CompilerParams(vmem_limit_bytes=VMEM)
 
 
-def hop_body(t, row_block, has_recv, has_prev, has_final, ties, scal, *refs):
+def hop_body(t, bands, row_block, has_recv, has_prev, has_final, ties, scal, *refs):
     refs = list(refs)
     fields, cot, fields_other, cot_other, tables = refs[:5]
     at = 5
@@ -63,20 +63,18 @@
     x, table, recv_now, total, out, x_sem, table_sem, recv_sem, out_sem, final_sem = refs[at:]
     half = x.shape[-1]
     coefs = out.shape[1]
+    share = coefs // (2 * bands)
     tiles = half // LANES
-    part_rows = row_block // 2
-    mine = pl.ds(pl.multiple_of(scal[t, 6] * half, LANES), half)
-
-    def row_copy(way, who, part, array):
-        first = scal[t, 3 * way + 1] * row_block + part * part_rows
-        rows = pl.ds(first, part_rows)
+    mine = pl.ds(pl.multiple_of(scal[t, 4] * half, LANES), half)
+
+    def row_copy(way, which, who):
+        rows = pl.ds(scal[t, 2 * way] * row_block, row_block)
+        array = ((fields, fields_other), (cot, cot_other))[which][who]
         source = array.at[rows] if who else array.at[rows, :, mine]
-        return pltpu.make_async_copy(
-            source, x.at[way, who, pl.ds(part * part_rows, part_rows)], x_sem.at[way, who, part]
-        )
+        return pltpu.make_async_copy(source, x.at[way, which, who], x_sem.at[way, which, who])
 
     def table_copy(way):
-        source = tables.at[scal[t, 3 * way + 2], scal[t, 3 * way], 1 - way]
+        source = tables.at[scal[t, 2 * way + 1], 1 - way]
         return pltpu.make_async_copy(source, table.at[way], table_sem.at[way])
 
     def recv_copy(way):
@@ -91,26 +89,26 @@
 
     def fetch(way):
         table_copy(way).start()
-        for part in range(2):
-            for which, pair in enumerate(((fields, fields_other), (cot, cot_other))):
-                @pl.when((scal[t, 3 * way] != 0) if which else (scal[t, 3 * way] == 0))
-                def _(part=part, pair=pair):
-                    for who in range(2):
-                        row_copy(way, who, part, pair[who]).start()
+        for which in range(2):
+            for who in range(2):
+                row_copy(way, which, who).start()
         if has_recv:
             recv_copy(way).start()
 
     def work(way):
         table_copy(way).wait()
-        for part in range(2):
+        for which in range(2):
             for who in range(2):
-                row_copy(way, who, part, (fields, fields_other)[who]).wait()
-            for h in range(part * part_rows, (part + 1) * part_rows):
-                value = dot(table[way, 0], x[way, 0, h]) + dot(table[way, 1], x[way, 1, h])
-                for j in range(tiles):
-                    total[j, pl.ds(h, coefs, stride=row_block), :] = value[
-                        :, j * LANES : (j + 1) * LANES
-                    ]
+                row_copy(way, which, who).wait()
+            for h in range(row_block):
+                value = dot(table[way, which, 0], x[way, which, 0, h])
+                value = value + dot(table[way, which, 1], x[way, which, 1, h])
+                for band in range(bands):
+                    first = (2 * band + which) * share * row_block + h
+                    for j in range(tiles):
+                        total[j, pl.ds(first, share, stride=row_block), :] = value[
+                            band * share : (band + 1) * share, j * LANES : (j + 1) * LANES
+                        ]
         if has_recv:
             recv_copy(way).wait()
         for j in range(tiles):
@@ -123,21 +121,21 @@
 
     for step in (fetch, work):
         for way in range(2):
-            pl.when(scal[t, 8 + way] != 0)(functools.partial(step, way))
+            pl.when(scal[t, 6 + way] != 0)(functools.partial(step, way))
     if has_final is not None:
-        pl.when(scal[t, 7] == 0)(lambda: final_copy(1).start())
-        pl.when(scal[t, 7] != 0)(lambda: final_copy(0).start())
+        pl.when(scal[t, 5] == 0)(lambda: final_copy(1).start())
+        pl.when(scal[t, 5] != 0)(lambda: final_copy(0).start())
     for way in range(2):
-        pl.when(scal[t, 8 + way] != 0)(lambda way=way: out_copy(way).wait())
+        pl.when(scal[t, 6 + way] != 0)(lambda way=way: out_copy(way).wait())
     if has_final is not None:
         final_copy(0).wait()
 
 
-def hop(t, scal, arrays, tables, recv, prev, final_at, row_block, rows, ties=()):
+def hop(t, bands, scal, arrays, tables, recv, prev, final_at, row_block, rows, ties=()):
     fields, _, fields_other, _ = arrays
     cols = fields.shape[1]
     half = fields_other.shape[2]
-    coefs = tables.shape[4]
+    coefs = 2 * tables.shape[4]
     operands = list(arrays) + [tables]
     if recv is not None:
         operands += list(recv)
@@ -153,7 +151,7 @@
     piece = pltpu.VMEM((2, coefs, row_block, half), BF16)
     return pl.pallas_call(
         functools.partial(
-            hop_body, t, row_block, recv is not None, prev is not None, final_at, len(ties)
+            hop_body, t, bands, row_block, recv is not None, prev is not None, final_at, len(ties)
         ),
         grid_spec=pltpu.PrefetchScalarGridSpec(
             num_scalar_prefetch=1,
@@ -161,8 +159,8 @@
             in_specs=[anywhere] * len(operands),
             out_specs=[anywhere] * len(out_shape),
             scratch_shapes=[
-                pltpu.VMEM((2, 2, row_block, cols, half), BF16),
-                pltpu.VMEM((2, 2, coefs, cols), BF16),
+                pltpu.VMEM((2, 2, 2, row_block, cols, half), BF16),
+                pltpu.VMEM((2,) + tables.shape[2:], BF16),
                 piece,
                 pltpu.VMEM((half // LANES, coefs * row_block, LANES), F32),
                 piece,
@@ -178,7 +176,7 @@
         compiler_params=params(),
         cost_estimate=pl.CostEstimate(
             flops=8 * row_block * coefs * cols * half,
-            bytes_accessed=16 * row_block * cols * half,
+            bytes_accessed=24 * row_block * cols * half,
             transcendentals=0,
         ),
         name="longitude_hop",
@@ -186,11 +184,10 @@
 
 
 def filter_body(
-    spectrum, pulled, forward, backward, inner, inner_t, outer_t,
-    *refs,
+    data, forward, backward, inner, inner_t, outer_t, *refs,
 ):
     (adjoint, gradients, stack, z, back, hidden, u_adj, inner_total, outer_total) = refs[-9:]
-    bands, _, _, rows, half = spectrum.shape
+    bands, _, _, _, rows, half = data.shape
     lats = bands * rows
     tile = lats // 2
 
@@ -199,11 +196,11 @@
         inner_total[...] = jnp.zeros_like(inner_total)
         outer_total[...] = jnp.zeros_like(outer_total)
 
-    for source, target in ((spectrum, z), (pulled, back)):
+    for which, target in enumerate((z, back)):
         for part in range(2):
             for band in range(bands):
                 first = part * lats + band * rows
-                stack[first : first + rows, :] = source[band, part, 0]
+                stack[first : first + rows, :] = data[band, which, part, 0]
         for part in range(2):
             @pl.loop(0, 2)
             def _(i, part=part, target=target):
@@ -240,11 +237,11 @@
                 gradients[which, b, 1] = total[low, high] - total[high, low]
 
 
-def spectral_filter(first, modes, spectrum, pulled, forward, backward, inner, inner_t, outer_t, *ties):
-    bands, _, _, rows, half = spectrum.shape
+def spectral_filter(first, modes, spectra, forward, backward, inner, inner_t, outer_t, *ties):
+    bands, _, _, _, rows, half = spectra.shape
     lats = bands * rows
     wide = 2 * half
-    data = pl.BlockSpec((bands, 2, 1, rows, half), lambda i: (0, 0, first + i, 0, 0))
+    data = pl.BlockSpec((bands, 2, 2, 1, rows, half), lambda i: (0, 0, 0, first + i, 0, 0))
 
     def whole(*shape):
         return pl.BlockSpec(shape, lambda i: (0,) * len(shape), pipeline_mode=pl.Buffered(1))
@@ -255,7 +252,7 @@
     return pl.pallas_call(
         filter_body,
         grid=(modes,),
-        in_specs=[data, data, square, square, weight, weight, weight]
+        in_specs=[data, square, square, weight, weight, weight]
         + [pl.BlockSpec(memory_space=pl.ANY)] * len(ties),
         out_specs=[
             pl.BlockSpec((bands, 2, 1, rows, half), lambda i: (0, 0, i, 0, 0)),
@@ -281,7 +278,7 @@
             transcendentals=modes * 2 * lats * half * 2,
         ),
         name="spectral_filter",
-    )(spectrum, pulled, forward, backward, inner, inner_t, outer_t, *ties)
+    )(spectra, forward, backward, inner, inner_t, outer_t, *ties)
 
 
 def relay_body(t, has_own, has_recv, has_prev, ties, scal, *refs):
@@ -501,11 +498,12 @@
     downward = [(i + 2, i) for i in range(lon_count - 2)]
 
     core_now = core.reshape(1).astype(jnp.int32)
-    first_sent = pick(core_now, fields, DELAY * row_block, row_block)
-    fields_sent = pick(core_now, fields, rows, row_block, first_sent)
-    fields_first = lax.ppermute(first_sent, "lon", swap)
+    early = []
+    for array in (fields, cotangent):
+        early.append(pick(core_now, array, FIRST * row_block, row_block, *early))
+    fields_sent = pick(core_now, fields, rows, row_block, early[1])
+    fields_first, cot_first = [lax.ppermute(array, "lon", swap) for array in early]
     fields_other = lax.ppermute(fields_sent, "lon", swap)
-    cot_other = None
 
     q = jnp.arange(coefs, dtype=jnp.int32)
     part_of = q // per_part % 2
@@ -519,16 +517,18 @@
          (lon ^ 1) * cols + jnp.arange(cols, dtype=jnp.int32)]
     )
     cos_rows, sin_rows = trig_rows(mode_ids, places, LONS)
-    per_piece = per_part // PIECES
     base = jnp.where(imag_row[:, None], -sin_rows, cos_rows)
     weights = jnp.where(mode_ids == 0, 1.0, 2.0).astype(BF16)
     both = jnp.stack([base, base * weights[:, None]], axis=0)
-    tables = both.reshape(2, 2, PARTS, coefs, 2, cols).transpose(2, 0, 1, 4, 3, 5)
-    panels = (
-        base.reshape(2 * PARTS, 2 * lat_count, PIECES, per_piece, 2, cols)
-        .transpose(4, 5, 0, 2, 1, 3)
-        .reshape(2, cols, 2 * PARTS * coefs)
-    )
+    tables = both.reshape(2, 2, PARTS, coefs, 2, cols).transpose(2, 1, 0, 4, 3, 5)
+    some = per_part // 2
+    calls = [(s, 0, per_part) for s in range(PARTS - 1)]
+    calls += [(PARTS - 1, 0, some), (PARTS - 1, some, per_part - some)]
+    by_mode = base.reshape(2, PARTS, 2 * lat_count, per_part, 2, cols)
+    panels = jnp.concatenate(
+        [by_mode[:, s, :, f : f + n].reshape(2, -1, 2, cols) for s, f, n in calls], axis=1
+    )
+    panels = panels.transpose(2, 3, 0, 1).reshape(2, cols, 2 * PARTS * coefs)
 
     lat_ids = jnp.arange(LATS, dtype=jnp.int32)
     lat_cos, lat_sin = trig_rows(lat_ids, lat_ids, LATS)
@@ -549,14 +549,14 @@
     )
     inner_t, outer_t = inner.T, outer.T
 
-    order = [(s, a, r) for s in range(PARTS) for a in range(2) for r in range(blocks)]
+    order = [(s, r) for s in range(PARTS) for r in range(blocks)]
     count = len(order)
     slots = count + DELAY * (chips - 1)
     slot_ids = jnp.arange(slots, dtype=jnp.int32)
 
     def schedule(late):
         v = jnp.clip(slot_ids - DELAY * late, 0, count - 1)
-        return [v // blocks % 2, v % blocks, v // (2 * blocks)]
+        return [v % blocks, v // blocks]
 
     def has_chunk(late):
         v = slot_ids - DELAY * late
@@ -572,24 +572,24 @@
     def across(array):
         return lax.all_to_all(array, "lat", split_axis=0, concat_axis=0, tiled=True)
 
-    last = []
+    last = [fields_sent]
     sent, gathered, every_row, spread, terms = {}, {}, {}, [], []
     others = {"cot": None}
 
     def hop_slot(t):
         v = t - DELAY * (chips - 1)
-        if t < DELAY:
-            arrays = (fields, fields, fields_first, fields_first)
-        elif t < blocks:
-            arrays = (fields, fields, fields_other, fields_other)
+        if t < FIRST:
+            arrays = (fields, cotangent, fields_first, cot_first)
         else:
             arrays = (fields, cotangent, fields_other, others["cot"])
         recv = sent.pop(t - DELAY, None)
         key, final_at, prev = None, None, None
         if v >= 0:
-            key, final_at = order[v][:2], order[v][2]
+            key, final_at = order[v]
             prev = gathered.get(key)
-        result = hop(t, hop_plan, arrays, tables, recv, prev, final_at, row_block, rows, last)
+        result = hop(
+            t, lat_count, hop_plan, arrays, tables, recv, prev, final_at, row_block, rows, last
+        )
         last[:] = [result[0]]
         if v >= 0:
             gathered[key] = result[2]
@@ -600,30 +600,28 @@
                 lax.ppermute(result[0], "lon", upward),
                 lax.ppermute(result[1], "lon", downward),
             )
-        if t == DELAY - 1:
+        if t == 0:
             cot_sent = pick(core_now, cotangent, rows, row_block, *last)
             last[:] = [cot_sent]
             others["cot"] = lax.ppermute(cot_sent, "lon", swap)
 
     def filter_piece(n):
-        s, piece = n // PIECES, n % PIECES
-        shape = (lat_count, 2, per_part, rows, half)
+        s, first, some = calls[n]
+        spectra = every_row[s].reshape(lat_count, 2, 2, per_part, rows, half)
         adjoint, part = spectral_filter(
-            piece * per_piece, per_piece,
-            every_row[s, 0].reshape(shape), every_row[s, 1].reshape(shape),
-            forward, backward, inner, inner_t, outer_t, *last,
+            first, some, spectra, forward, backward, inner, inner_t, outer_t, *last
         )
         last[:] = [adjoint]
         terms.append(part)
-        spread.append(across(adjoint.reshape(-1, rows, half)))
+        array = across(adjoint.reshape(-1, rows, half))
+        spread.extend((array, i) for i in range(array.shape[0] // CHUNK))
 
     def add_up():
         at_end = (chip == 0) | (chip == chips - 1)
         now = jnp.where(at_end, sum(terms), 0.0).reshape(lat_count, -1, LANES)
         return jnp.sum(across(now), axis=0)
 
-    per_spread = coefs // (PIECES * CHUNK)
-    relay_count = PARTS * PIECES * per_spread
+    relay_count = PARTS * coefs // CHUNK
     relay_slots = relay_count + DELAY * (chips - 1)
     relay_ids = jnp.arange(relay_slots, dtype=jnp.int32)
 
@@ -642,7 +640,7 @@
     def relay_slot(t, *ties):
         own, own_at = (None, None)
         if t < relay_count:
-            own, own_at = spread[t // per_spread], t % per_spread
+            own, own_at = spread[t]
         up, down, *kept[:] = relay(
             t, relay_plan, own, own_at, passed.pop(t - DELAY, None), tuple(kept) or None,
             relay_count, (CHUNK, rows, half), last + list(ties),
@@ -652,16 +650,14 @@
             passed[t] = (lax.ppermute(up, "lon", upward), lax.ppermute(down, "lon", downward))
 
     for t in range(slots):
-        if t in (slots - 9, slots - 6):
-            filter_piece(len(spread))
+        if t in (slots - 16, slots - 9, slots - 2):
+            filter_piece(len(terms))
         hop_slot(t)
-        if slots - 6 <= t < slots - 2:
+        if t >= slots - 6:
             relay_slot(t - slots + 6)
-    filter_piece(2)
-    filter_piece(3)
-    for t in range(4, relay_slots):
-        if t in (7, 8, 10, 12):
-            filter_piece(len(spread))
+    for t in range(6, relay_slots):
+        if t in (10, 11):
+            filter_piece(len(terms))
         ties = []
         if t == 13:
             share = add_up()

time: 1260 us -> 1200 us (0.952)
  blocking collectives: 61.1 us -> 0 us
  Pallas kernels: 543 us -> 579 us
  waiting for transfers between devices: 211 us -> 189 us
    all_to_all x2 -> x0, blocking collectives: 61.1 us -> none  [across(): return lax.all_to_all(array, 'lat', split_axis=0, concat_axis=0, tiled=True)]
    pallas_call x42 -> x39, Pallas kernels: 384 us -> 413 us  [the longest x34 265 us: hop(): pl.pallas_call(functools.partial(hop_body, t, bands, row_block, recv is n...]
    ppermute x20, waiting for transfers between devices: 30.7 us -> 47.6 us  [relay_slot(): lax.ppermute(up, 'lon', upward)]
    ppermute x20, waiting for transfers between devices: 63.1 us -> 46.2 us  [relay_slot(): lax.ppermute(down, 'lon', downward)]
    ppermute x32, starting transfers between devices: 166 us -> 150 us  [hop_slot(): lax.ppermute(result[0], 'lon', upward)]
    ppermute x32, waiting for transfers between devices: 70.9 us -> 58.2 us  [hop_slot(): lax.ppermute(result[1], 'lon', downward)]
    pallas_call x3 -> x4, Pallas kernels: 23.4 us -> 30.6 us  [pick(): pl.pallas_call(pick_body, grid_spec=pltpu.PrefetchScalarGridSpec(num_scal...]
    all_to_all x11 -> x10, starting transfers between devices: 49.5 us -> 47 us  [across(): return lax.all_to_all(array, 'lat', split_axis=0, concat_axis=0, tiled=True)]
  transfers between devices with their start and end apart: 122 -> 122, of which waited for: 55 -> 51; matrix products, arithmetic and copies ran while one was open for 3% -> 3% of each run, Pallas kernels for 43% -> 44%
where the time goes in v4:
time: 1200 us; the launch traced here: 1180 us
  Pallas kernels  579 us (48%)
  starting transfers between devices  351 us (29%)
  waiting for transfers between devices  189 us (16%)
  other arithmetic  24.6 us (2%)
  local copies, waits for them, and re-layouts  22 us (2%)
  between operations  16.6 us (1%)
    pallas_call x34, Pallas kernels, hop(): pl.pallas_call(functools.partial(hop_body, t, bands, row_block, recv is n...  265 us
    ppermute x32, starting transfers between devices, hop_slot(): lax.ppermute(result[0], 'lon', upward)  150 us
    pallas_call x5, Pallas kernels, spectral_filter(): pl.pallas_call(filter_body, grid=(modes,), in_specs=[data, square, square...  148 us
    pallas_call x22, Pallas kernels, relay(): pl.pallas_call(functools.partial(relay_body, t, own is not None, recv is...  88.9 us
    ppermute x20, starting transfers between devices, relay_slot(): lax.ppermute(up, 'lon', upward)  84.9 us
    ppermute x32, waiting for transfers between devices, hop_slot(): lax.ppermute(result[1], 'lon', downward)  58.2 us
    ppermute x20, waiting for transfers between devices, relay_slot(): lax.ppermute(up, 'lon', upward)  47.6 us
    all_to_all x10, starting transfers between devices, across(): return lax.all_to_all(array, 'lat', split_axis=0, concat_axis=0, tiled=True)  47 us
  transfers between devices with their start and end apart: 122, of which 51 were waited for; matrix products, arithmetic and copies ran while one was open for 3% of the time, Pallas kernels for 44%

profile of v4, /device:TPU:0, one launch (start us, length us, event | category | flops | bytes accessed | tf_op | source)
XLA Modules:
  0.0 1182.8 jit_solution(16322331699270722583)
XLA Ops:
  18.0 10.1 pick.6.refs_5_
  38.4 10.2 pick.7.refs_5_
  58.6 9.6 collective-permute-done.6.refs_5_
  142.5 8.6 longitude_hop.40
  159.3 8.9 longitude_hop.41
  176.1 8.8 longitude_hop.42
  192.9 8.8 longitude_hop.43
  226.9 8.8 longitude_hop.45
  242.0 8.7 longitude_hop.46
  268.5 9.8 collective-permute-done.24.refs_5_
  283.8 8.8 longitude_hop.47
  301.3 8.9 longitude_hop.48
  316.9 8.7 longitude_hop.49
  347.0 8.8 longitude_hop.50
  361.7 8.8 longitude_hop.51
  377.5 35.8 %spectral_filter.5 = (bf16[4,2,4,112,384]{4,3,2,1,0:T(8,128)(2,1)}, f32[2,4,2,96,96]{4,3,2,1,0:T(8,128)}) custom-call(bf16[4,2,2,4,112,384]{5,4,3,2,1,0:T(8,128)(2,1)} %bitcast.2.data, bf16[896,896]{1,0:T(8,128)(2,1)} %get-tuple-element.392.forward, bf16[896,896]{1,0:T(8,128)(2,1)} %get-tuple-element.391.backward, bf16[768,768]{1,0:T(8,128)(2,1)} %copy.117.inner, ...), custom_call_target="tpu_custom_call" | custom-call | flops 17968398336 | bytes 8257536 | tf_op jit(solution)/shard_map/spectral_filter/pallas_call | solution.py:252
  414.5 8.8 longitude_hop.52
  423.3 8.7 longitude_hop.53
  462.9 8.6 longitude_hop.54
  479.7 8.8 longitude_hop.55
  496.6 8.8 longitude_hop.56
  513.9 8.8 longitude_hop.57
  529.7 8.7 longitude_hop.58
  544.1 35.9 %spectral_filter.6 = (bf16[4,2,4,112,384]{4,3,2,1,0:T(8,128)(2,1)}, f32[2,4,2,96,96]{4,3,2,1,0:T(8,128)}) custom-call(bf16[4,2,2,4,112,384]{5,4,3,2,1,0:T(8,128)(2,1)} %bitcast.9.data, bf16[896,896]{1,0:T(8,128)(2,1)} %get-tuple-element.392.forward, bf16[896,896]{1,0:T(8,128)(2,1)} %get-tuple-element.391.backward, bf16[768,768]{1,0:T(8,128)(2,1)} %copy.117.inner, ...), custom_call_target="tpu_custom_call" | custom-call | flops 17968398336 | bytes 8257536 | tf_op jit(solution)/shard_map/spectral_filter/pallas_call | solution.py:252
  590.4 8.8 longitude_hop.60
  630.4 8.8 longitude_hop.61
  727.7 35.8 %spectral_filter.7 = (bf16[4,2,4,112,384]{4,3,2,1,0:T(8,128)(2,1)}, f32[2,4,2,96,96]{4,3,2,1,0:T(8,128)}) custom-call(bf16[4,2,2,4,112,384]{5,4,3,2,1,0:T(8,128)(2,1)} %bitcast.11.data, bf16[896,896]{1,0:T(8,128)(2,1)} %get-tuple-element.392.forward, bf16[896,896]{1,0:T(8,128)(2,1)} %get-tuple-element.391.backward, bf16[768,768]{1,0:T(8,128)(2,1)} %copy.117.inner, ...), custom_call_target="tpu_custom_call" | custom-call | flops 17968398336 | bytes 8257536 | tf_op jit(solution)/shard_map/spectral_filter/pallas_call | solution.py:252
  794.0 11.5 collective-permute-done.72.refs_1_
  901.8 20.4 %spectral_filter.8 = (bf16[4,2,2,112,384]{4,3,2,1,0:T(8,128)(2,1)}, f32[2,4,2,96,96]{4,3,2,1,0:T(8,128)}) custom-call(bf16[4,2,2,4,112,384]{5,4,3,2,1,0:T(8,128)(2,1)} %bitcast.13.data, bf16[896,896]{1,0:T(8,128)(2,1)} %get-tuple-element.392.forward, bf16[896,896]{1,0:T(8,128)(2,1)} %get-tuple-element.391.backward, bf16[768,768]{1,0:T(8,128)(2,1)} %copy.117.inner, ...), custom_call_target="tpu_custom_call" | custom-call | flops 8984199168 | bytes 4128768 | tf_op jit(solution)/shard_map/spectral_filter/pallas_call | solution.py:252
  927.2 20.5 %spectral_filter.9 = (bf16[4,2,2,112,384]{4,3,2,1,0:T(8,128)(2,1)}, f32[2,4,2,96,96]{4,3,2,1,0:T(8,128)}) custom-call(bf16[4,2,2,4,112,384]{5,4,3,2,1,0:T(8,128)(2,1)} %bitcast.13.data, bf16[896,896]{1,0:T(8,128)(2,1)} %get-tuple-element.392.forward, bf16[896,896]{1,0:T(8,128)(2,1)} %get-tuple-element.391.backward, bf16[768,768]{1,0:T(8,128)(2,1)} %copy.117.inner, ...), custom_call_target="tpu_custom_call" | custom-call | flops 8984199168 | bytes 4128768 | tf_op jit(solution)/shard_map/spectral_filter/pallas_call | solution.py:252
  1124.3 20.0 %longitude_grid.2 = (bf16[112,112,768]{2,1,0:T(8,128)(2,1)}, bf16[64,112,384]{2,1,0:T(8,128)(2,1)}) custom-call(s32[1]{0:T(128)} %bitcast.core, bf16[17,8,112,384]{3,2,1,0:T(8,128)(2,1)} %get-tuple-element.383.refs_0_, bf16[17,8,112,384]{3,2,1,0:T(8,128)(2,1)} %get-tuple-element.384.refs_1_, bf16[2,112,256]{2,1,0:T(8,128)(2,1)} %reshape.517.refs_2_), custom_call_target="tpu_custom_call" | custom-call | flops 2818572288 | bytes 23592960 | tf_op jit(solution)/shard_map/longitude_grid/pallas_call | solution.py:385
  1144.3 15.9 %longitude_grid.3 = (bf16[112,112,768]{2,1,0:T(8,128)(2,1)}, bf16[48,112,384]{2,1,0:T(8,128)(2,1)}) custom-call(s32[1]{0:T(128)} %bitcast.core, bf16[17,8,112,384]{3,2,1,0:T(8,128)(2,1)} %get-tuple-element.383.refs_0_, bf16[17,8,112,384]{3,2,1,0:T(8,128)(2,1)} %get-tuple-element.384.refs_1_, ...), custom_call_target="tpu_custom_call", output_to_operand_aliasing={{0}: (4, {})} | custom-call | flops 2113929216 | bytes 17694720 | tf_op jit(solution)/shard_map/longitude_grid/pallas_call | solution.py:385
  (460 shorter events, 755.4 us)
Async XLA Ops:
  28.1 62.2 %collective-permute-start = (bf16[112,112,384]{2,1,0:T(8,128)(2,1)}, bf16[112,112,384]{2,1,0:T(8,128)(2,1)}, u32[]{:S(2)}, u32[]{:S(2)}) collective-permute-start(bf16[112,112,384]{2,1,0:T(8,128)(2,1)} %pick.6.refs_5_), channel_id=1, source_target_pairs={{0,1},{1,0},{2,3},{3,2},{4,5},{5,4},{6,7},{7,6},{8,9},{9,8},{10,11... | collective-permute-start | bytes 28901384 | tf_op jit(solution)/shard_map/ppermute | solution.py:506
  48.6 41.7 %collective-permute-start.3 = (bf16[112,112,384]{2,1,0:T(8,128)(2,1)}, bf16[112,112,384]{2,1,0:T(8,128)(2,1)}, u32[]{:S(2)}, u32[]{:S(2)}) collective-permute-start(bf16[112,112,384]{2,1,0:T(8,128)(2,1)} %pick.7.refs_5_), channel_id=1, source_target_pairs={{0,1},{1,0},{2,3},{3,2},{4,5},{5,4},{6,7},{7,6},{8,9},{9,8},{10,11... | collective-permute-start | bytes 28901384 | tf_op jit(solution)/shard_map/ppermute | solution.py:606
  250.6 126.8 %all-to-all-start = ((bf16[64,112,384]{2,1,0:T(8,128)(2,1)}), bf16[64,112,384]{2,1,0:T(8,128)(2,1)}, u32[]{:S(2)}, u32[]{:S(2)}) async-start(bf16[64,112,384]{2,1,0:T(8,128)(2,1)} %get-tuple-element.243), calls=%async_computation | async-start | bytes 11010048 | tf_op jit(solution)/shard_map/all_to_all | solution.py:573
  261.7 39.6 %collective-permute-start.30 = (bf16[64,16,384]{2,1,0:T(8,128)(2,1)}, bf16[64,16,384]{2,1,0:T(8,128)(2,1)}, u32[]{:S(2)}, u32[]{:S(2)}) collective-permute-start(bf16[64,16,384]{2,1,0:T(8,128)(2,1)} %get-tuple-element.226.refs_7_), channel_id=1, source_target_pairs={{0,2},{1,3},{2,4},{3,5},{4,6},{5,7},{8,10},{9,11},{10,12},{11,13},... | collective-permute-start | bytes 2359304 | tf_op jit(solution)/shard_map/ppermute | solution.py:600
  267.1 34.2 %collective-permute-start.31 = (bf16[64,16,384]{2,1,0:T(8,128)(2,1)}, bf16[64,16,384]{2,1,0:T(8,128)(2,1)}, u32[]{:S(2)}, u32[]{:S(2)}) collective-permute-start(bf16[64,16,384]{2,1,0:T(8,128)(2,1)} %get-tuple-element.229), channel_id=1, source_target_pairs={{2,0},{3,1},{4,2},{5,3},{6,4},{7,5},{10,8},{11,9},{12,10},{13,11},... | collective-permute-start | bytes 2359304 | tf_op jit(solution)/shard_map/ppermute | solution.py:601
  310.2 36.8 %collective-permute-start.34 = (bf16[64,16,384]{2,1,0:T(8,128)(2,1)}, bf16[64,16,384]{2,1,0:T(8,128)(2,1)}, u32[]{:S(2)}, u32[]{:S(2)}) collective-permute-start(bf16[64,16,384]{2,1,0:T(8,128)(2,1)} %get-tuple-element.232.refs_8_), channel_id=1, source_target_pairs={{0,2},{1,3},{2,4},{3,5},{4,6},{5,7},{8,10},{9,11},{10,12},{11,13},... | collective-permute-start | bytes 2359304 | tf_op jit(solution)/shard_map/ppermute | solution.py:600
  315.6 31.4 %collective-permute-start.35 = (bf16[64,16,384]{2,1,0:T(8,128)(2,1)}, bf16[64,16,384]{2,1,0:T(8,128)(2,1)}, u32[]{:S(2)}, u32[]{:S(2)}) collective-permute-start(bf16[64,16,384]{2,1,0:T(8,128)(2,1)} %get-tuple-element.235), channel_id=1, source_target_pairs={{2,0},{3,1},{4,2},{5,3},{6,4},{7,5},{10,8},{11,9},{12,10},{13,11},... | collective-permute-start | bytes 2359304 | tf_op jit(solution)/shard_map/ppermute | solution.py:601
  325.6 36.0 %collective-permute-start.32 = (bf16[64,16,384]{2,1,0:T(8,128)(2,1)}, bf16[64,16,384]{2,1,0:T(8,128)(2,1)}, u32[]{:S(2)}, u32[]{:S(2)}) collective-permute-start(bf16[64,16,384]{2,1,0:T(8,128)(2,1)} %get-tuple-element.233.refs_8_), channel_id=1, source_target_pairs={{0,2},{1,3},{2,4},{3,5},{4,6},{5,7},{8,10},{9,11},{10,12},{11,13},... | collective-permute-start | bytes 2359304 | tf_op jit(solution)/shard_map/ppermute | solution.py:600
  355.9 57.5 %collective-permute-start.38 = (bf16[64,16,384]{2,1,0:T(8,128)(2,1)}, bf16[64,16,384]{2,1,0:T(8,128)(2,1)S(1)}, u32[]{:S(2)}, u32[]{:S(2)}) collective-permute-start(bf16[64,16,384]{2,1,0:T(8,128)(2,1)} %get-tuple-element.238.refs_8_), channel_id=1, source_target_pairs={{0,2},{1,3},{2,4},{3,5},{4,6},{5,7},{8,10},{9,11},{10,12},{11,13},... | collective-permute-start | bytes 2359304 | tf_op jit(solution)/shard_map/ppermute | solution.py:600
  360.3 53.0 %collective-permute-start.39 = (bf16[64,16,384]{2,1,0:T(8,128)(2,1)}, bf16[64,16,384]{2,1,0:T(8,128)(2,1)S(1)}, u32[]{:S(2)}, u32[]{:S(2)}) collective-permute-start(bf16[64,16,384]{2,1,0:T(8,128)(2,1)} %get-tuple-element.241), channel_id=1, source_target_pairs={{2,0},{3,1},{4,2},{5,3},{6,4},{7,5},{10,8},{11,9},{12,10},{13,11},... | collective-permute-start | bytes 2359304 | tf_op jit(solution)/shard_map/ppermute | solution.py:601
  370.5 52.8 %collective-permute-start.36 = (bf16[64,16,384]{2,1,0:T(8,128)(2,1)}, bf16[64,16,384]{2,1,0:T(8,128)(2,1)}, u32[]{:S(2)}, u32[]{:S(2)}) collective-permute-start(bf16[64,16,384]{2,1,0:T(8,128)(2,1)} %get-tuple-element.239.refs_0_), channel_id=1, source_target_pairs={{0,2},{1,3},{2,4},{3,5},{4,6},{5,7},{8,10},{9,11},{10,12},{11,13},... | collective-permute-start | bytes 2359304 | tf_op jit(solution)/shard_map/ppermute | solution.py:600
  376.0 47.3 %collective-permute-start.37 = (bf16[64,16,384]{2,1,0:T(8,128)(2,1)}, bf16[64,16,384]{2,1,0:T(8,128)(2,1)}, u32[]{:S(2)}, u32[]{:S(2)}) collective-permute-start(bf16[64,16,384]{2,1,0:T(8,128)(2,1)} %get-tuple-element.240), channel_id=1, source_target_pairs={{2,0},{3,1},{4,2},{5,3},{6,4},{7,5},{10,8},{11,9},{12,10},{13,11},... | collective-permute-start | bytes 2359304 | tf_op jit(solution)/shard_map/ppermute | solution.py:601
  432.0 76.4 %all-to-all-start.1 = ((bf16[64,112,384]{2,1,0:T(8,128)(2,1)}), bf16[64,112,384]{2,1,0:T(8,128)(2,1)}, u32[]{:S(2)}, u32[]{:S(2)}) async-start(bf16[64,112,384]{2,1,0:T(8,128)(2,1)} %get-tuple-element.263), calls=%async_computation.1 | async-start | bytes 11010048 | tf_op jit(solution)/shard_map/all_to_all | solution.py:573
  443.6 31.5 %collective-permute-start.40 = (bf16[64,16,384]{2,1,0:T(8,128)(2,1)S(1)}, bf16[64,16,384]{2,1,0:T(8,128)(2,1)}, u32[]{:S(2)}, u32[]{:S(2)}) collective-permute-start(bf16[64,16,384]{2,1,0:T(8,128)(2,1)S(1)} %copy-done.12), channel_id=1, source_target_pairs={{0,2},{1,3},{2,4},{3,5},{4,6},{5,7},{8,10},{9,11},{10,12},{11,13},... | collective-permute-start | bytes 2359304 | tf_op jit(solution)/shard_map/ppermute | solution.py:600
  508.4 90.8 %all-to-all-start.2 = ((bf16[32,112,384]{2,1,0:T(8,128)(2,1)}), bf16[32,112,384]{2,1,0:T(8,128)(2,1)}, u32[]{:S(2)}, u32[]{:S(2)}) async-start(bf16[32,112,384]{2,1,0:T(8,128)(2,1)} %bitcast.47), calls=%async_computation.2 | async-start | bytes 5505024 | tf_op jit(solution)/shard_map/all_to_all | solution.py:573
  522.7 57.3 %collective-permute-start.48 = (bf16[64,16,384]{2,1,0:T(8,128)(2,1)}, bf16[64,16,384]{2,1,0:T(8,128)(2,1)S(1)}, u32[]{:S(2)}, u32[]{:S(2)}) collective-permute-start(bf16[64,16,384]{2,1,0:T(8,128)(2,1)} %get-tuple-element.258.refs_8_), channel_id=1, source_target_pairs={{0,2},{1,3},{2,4},{3,5},{4,6},{5,7},{8,10},{9,11},{10,12},{11,13},... | collective-permute-start | bytes 2359304 | tf_op jit(solution)/shard_map/ppermute | solution.py:600
  527.2 52.8 %collective-permute-start.49 = (bf16[64,16,384]{2,1,0:T(8,128)(2,1)}, bf16[64,16,384]{2,1,0:T(8,128)(2,1)}, u32[]{:S(2)}, u32[]{:S(2)}) collective-permute-start(bf16[64,16,384]{2,1,0:T(8,128)(2,1)} %get-tuple-element.259), channel_id=1, source_target_pairs={{2,0},{3,1},{4,2},{5,3},{6,4},{7,5},{10,8},{11,9},{12,10},{13,11},... | collective-permute-start | bytes 2359304 | tf_op jit(solution)/shard_map/ppermute | solution.py:601
  538.4 51.1 %collective-permute-start.54 = (bf16[64,16,384]{2,1,0:T(8,128)(2,1)}, bf16[64,16,384]{2,1,0:T(8,128)(2,1)S(1)}, u32[]{:S(2)}, u32[]{:S(2)}) collective-permute-start(bf16[64,16,384]{2,1,0:T(8,128)(2,1)} %get-tuple-element.264.refs_0_), channel_id=1, source_target_pairs={{0,2},{1,3},{2,4},{3,5},{4,6},{5,7},{8,10},{9,11},{10,12},{11,13},... | collective-permute-start | bytes 2359304 | tf_op jit(solution)/shard_map/ppermute | solution.py:600
  542.8 46.7 %collective-permute-start.55 = (bf16[64,16,384]{2,1,0:T(8,128)(2,1)}, bf16[64,16,384]{2,1,0:T(8,128)(2,1)}, u32[]{:S(2)}, u32[]{:S(2)}) collective-permute-start(bf16[64,16,384]{2,1,0:T(8,128)(2,1)} %get-tuple-element.268), channel_id=1, source_target_pairs={{2,0},{3,1},{4,2},{5,3},{6,4},{7,5},{10,8},{11,9},{12,10},{13,11},... | collective-permute-start | bytes 2359304 | tf_op jit(solution)/shard_map/ppermute | solution.py:601
  599.2 103.6 %all-to-all-start.3 = ((bf16[64,112,384]{2,1,0:T(8,128)(2,1)}), bf16[64,112,384]{2,1,0:T(8,128)(2,1)}, u32[]{:S(2)}, u32[]{:S(2)}) async-start(bf16[64,112,384]{2,1,0:T(8,128)(2,1)} %get-tuple-element.295), calls=%async_computation.3 | async-start | bytes 11010048 | tf_op jit(solution)/shard_map/all_to_all | solution.py:573
  653.4 42.1 %collective-permute-start.62 = (bf16[64,16,384]{2,1,0:T(8,128)(2,1)}, bf16[64,16,384]{2,1,0:T(8,128)(2,1)S(1)}, u32[]{:S(2)}, u32[]{:S(2)}) collective-permute-start(bf16[64,16,384]{2,1,0:T(8,128)(2,1)} %get-tuple-element.276.refs_1_), channel_id=1, source_target_pairs={{0,2},{1,3},{2,4},{3,5},{4,6},{5,7},{8,10},{9,11},{10,12},{11,13},... | collective-permute-start | bytes 2359304 | tf_op jit(solution)/shard_map/ppermute | solution.py:600
  657.6 43.9 %collective-permute-start.63 = (bf16[64,16,384]{2,1,0:T(8,128)(2,1)}, bf16[64,16,384]{2,1,0:T(8,128)(2,1)S(1)}, u32[]{:S(2)}, u32[]{:S(2)}) collective-permute-start(bf16[64,16,384]{2,1,0:T(8,128)(2,1)} %get-tuple-element.280), channel_id=1, source_target_pairs={{2,0},{3,1},{4,2},{5,3},{6,4},{7,5},{10,8},{11,9},{12,10},{13,11},... | collective-permute-start | bytes 2359304 | tf_op jit(solution)/shard_map/ppermute | solution.py:601
  675.6 41.9 %collective-permute-start.60 = (bf16[64,16,384]{2,1,0:T(8,128)(2,1)}, bf16[64,16,384]{2,1,0:T(8,128)(2,1)}, u32[]{:S(2)}, u32[]{:S(2)}) collective-permute-start(bf16[64,16,384]{2,1,0:T(8,128)(2,1)} %get-tuple-element.278.refs_3_), channel_id=1, source_target_pairs={{0,2},{1,3},{2,4},{3,5},{4,6},{5,7},{8,10},{9,11},{10,12},{11,13},... | collective-permute-start | bytes 2359304 | tf_op jit(solution)/shard_map/ppermute | solution.py:600
  682.4 35.1 %collective-permute-start.61 = (bf16[64,16,384]{2,1,0:T(8,128)(2,1)}, bf16[64,16,384]{2,1,0:T(8,128)(2,1)}, u32[]{:S(2)}, u32[]{:S(2)}) collective-permute-start(bf16[64,16,384]{2,1,0:T(8,128)(2,1)} %get-tuple-element.279), channel_id=1, source_target_pairs={{2,0},{3,1},{4,2},{5,3},{6,4},{7,5},{10,8},{11,9},{12,10},{13,11},... | collective-permute-start | bytes 2359304 | tf_op jit(solution)/shard_map/ppermute | solution.py:601
  702.8 60.7 %all-to-all-start.4 = ((bf16[32,112,384]{2,1,0:T(8,128)(2,1)}), bf16[32,112,384]{2,1,0:T(8,128)(2,1)}, u32[]{:S(2)}, u32[]{:S(2)}) async-start(bf16[32,112,384]{2,1,0:T(8,128)(2,1)} %bitcast.46), calls=%async_computation.4 | async-start | bytes 5505024 | tf_op jit(solution)/shard_map/all_to_all | solution.py:573
  763.5 60.0 %all-to-all-start.6 = ((bf16[32,112,384]{2,1,0:T(8,128)(2,1)}), bf16[32,112,384]{2,1,0:T(8,128)(2,1)}, u32[]{:S(2)}, u32[]{:S(2)}) async-start(bf16[32,112,384]{2,1,0:T(8,128)(2,1)} %bitcast.48), calls=%async_computation.6 | async-start | bytes 5505024 | tf_op jit(solution)/shard_map/all_to_all | solution.py:573
  775.0 41.5 %collective-permute-start.66 = (bf16[64,16,384]{2,1,0:T(8,128)(2,1)}, bf16[64,16,384]{2,1,0:T(8,128)(2,1)S(1)}, u32[]{:S(2)}, u32[]{:S(2)}) collective-permute-start(bf16[64,16,384]{2,1,0:T(8,128)(2,1)} %get-tuple-element.291.refs_5_), channel_id=1, source_target_pairs={{0,2},{1,3},{2,4},{3,5},{4,6},{5,7},{8,10},{9,11},{10,12},{11,13},... | collective-permute-start | bytes 2359304 | tf_op jit(solution)/shard_map/ppermute | solution.py:600
  779.6 36.9 %collective-permute-start.67 = (bf16[64,16,384]{2,1,0:T(8,128)(2,1)}, bf16[64,16,384]{2,1,0:T(8,128)(2,1)S(1)}, u32[]{:S(2)}, u32[]{:S(2)}) collective-permute-start(bf16[64,16,384]{2,1,0:T(8,128)(2,1)} %get-tuple-element.292), channel_id=1, source_target_pairs={{2,0},{3,1},{4,2},{5,3},{6,4},{7,5},{10,8},{11,9},{12,10},{13,11},... | collective-permute-start | bytes 2359304 | tf_op jit(solution)/shard_map/ppermute | solution.py:601
  823.5 78.3 %all-to-all-start.5 = ((bf16[64,112,384]{2,1,0:T(8,128)(2,1)}), bf16[64,112,384]{2,1,0:T(8,128)(2,1)}, u32[]{:S(2)}, u32[]{:S(2)}) async-start(bf16[64,112,384]{2,1,0:T(8,128)(2,1)} %get-tuple-element.307), calls=%async_computation.5 | async-start | bytes 11010048 | tf_op jit(solution)/shard_map/all_to_all | solution.py:573
  890.7 31.6 %collective-permute-start.82 = (bf16[8,112,384]{2,1,0:T(8,128)(2,1)}, bf16[8,112,384]{2,1,0:T(8,128)(2,1)S(1)}, u32[]{:S(2)}, u32[]{:S(2)}) collective-permute-start(bf16[8,112,384]{2,1,0:T(8,128)(2,1)} %get-tuple-element.324.refs_5_), channel_id=1, source_target_pairs={{0,2},{1,3},{2,4},{3,5},{4,6},{5,7},{8,10},{9,11},{10,12},{11,13},... | collective-permute-start | bytes 2064392 | tf_op jit(solution)/shard_map/ppermute | solution.py:650
  991.2 117.8 %all-gather.6.cloned.1.call-start = ((), (), s32[]{:S(2)}) async-start(), calls=%async_computation.11 | async-start | bytes 1327104 | tf_op jit(solution)/shard_map/all_gather | solution.py:665
  1016.4 127.9 %all-gather.4.cloned.1.call-start = ((), (), s32[]{:S(2)}) async-start(), calls=%async_computation.10 | async-start | bytes 1474560 | tf_op jit(solution)/shard_map/all_gather | solution.py:667
  (147 other events, 2267.7 us)
Sparse Core Ops, SparseCore 0:
  1016.5 31.1 all-gather.5
  1111.3 29.5 all-gather.3

commit v5 on v4

--- a/solution.py
+++ b/solution.py
@@ -650,13 +650,14 @@
             passed[t] = (lax.ppermute(up, "lon", upward), lax.ppermute(down, "lon", downward))
 
     for t in range(slots):
-        if t in (slots - 16, slots - 9, slots - 2):
+        if t in (slots - 16, slots - 9, slots - 4):
             filter_piece(len(terms))
-        hop_slot(t)
         if t >= slots - 6:
             relay_slot(t - slots + 6)
+        hop_slot(t)
     for t in range(6, relay_slots):
-        if t in (10, 11):
+        if t == 10:
+            filter_piece(len(terms))
             filter_piece(len(terms))
         ties = []
         if t == 13:

time: 1200 us -> 1220 us (1.017)
  waiting for transfers between devices: 189 us -> 206 us
    ppermute x20, waiting for transfers between devices: 46.2 us -> 74.2 us  [relay_slot(): lax.ppermute(down, 'lon', downward)]
  transfers between devices with their start and end apart: 122 -> 122, of which waited for: 51 -> 49; matrix products, arithmetic and copies ran while one was open for 3% -> 3% of each run, Pallas kernels for 44% -> 43%
where the time goes in v5:
time: 1220 us; the launch traced here: 1200 us
  Pallas kernels  580 us (48%)
  starting transfers between devices  350 us (29%)
  waiting for transfers between devices  206 us (17%)
  other arithmetic  24.6 us (2%)
  local copies, waits for them, and re-layouts  22.9 us (2%)
  between operations  16.5 us (1%)
    pallas_call x34, Pallas kernels, hop(): pl.pallas_call(functools.partial(hop_body, t, bands, row_block, recv is n...  265 us
    ppermute x32, starting transfers between devices, hop_slot(): lax.ppermute(result[0], 'lon', upward)  154 us
    pallas_call x5, Pallas kernels, spectral_filter(): pl.pallas_call(filter_body, grid=(modes,), in_specs=[data, square, square...  149 us
    pallas_call x22, Pallas kernels, relay(): pl.pallas_call(functools.partial(relay_body, t, own is not None, recv is...  89.4 us
    ppermute x20, starting transfers between devices, relay_slot(): lax.ppermute(up, 'lon', upward)  79.3 us
    ppermute x20, waiting for transfers between devices, relay_slot(): lax.ppermute(down, 'lon', downward)  74.2 us
    ppermute x32, waiting for transfers between devices, hop_slot(): lax.ppermute(result[1], 'lon', downward)  52.7 us
    all_to_all x10, starting transfers between devices, across(): return lax.all_to_all(array, 'lat', split_axis=0, concat_axis=0, tiled=True)  47.7 us
  transfers between devices with their start and end apart: 122, of which 49 were waited for; matrix products, arithmetic and copies ran while one was open for 3% of the time, Pallas kernels for 43%

profile of v5, /device:TPU:0, one launch (start us, length us, event | category | flops | bytes accessed | tf_op | source)
XLA Modules:
  0.0 1199.7 jit_solution(6392684897324140740)
XLA Ops:
  18.0 10.1 pick.6.refs_5_
  38.4 10.2 pick.7.refs_5_
  58.5 9.6 collective-permute-done.6.refs_5_
  142.4 8.8 longitude_hop.40
  159.3 9.0 longitude_hop.41
  176.0 8.8 longitude_hop.42
  192.9 8.8 longitude_hop.43
  226.8 8.8 longitude_hop.45
  241.9 8.7 longitude_hop.46
  268.6 9.8 collective-permute-done.24.refs_5_
  284.0 8.8 longitude_hop.47
  301.2 8.9 longitude_hop.48
  316.8 8.8 longitude_hop.49
  347.0 8.8 longitude_hop.50
  361.7 8.7 longitude_hop.51
  377.6 35.8 %spectral_filter.5 = (bf16[4,2,4,112,384]{4,3,2,1,0:T(8,128)(2,1)}, f32[2,4,2,96,96]{4,3,2,1,0:T(8,128)}) custom-call(bf16[4,2,2,4,112,384]{5,4,3,2,1,0:T(8,128)(2,1)} %bitcast.2.data, bf16[896,896]{1,0:T(8,128)(2,1)} %get-tuple-element.392.forward, bf16[896,896]{1,0:T(8,128)(2,1)} %get-tuple-element.391.backward, bf16[768,768]{1,0:T(8,128)(2,1)} %copy.117.inner, ...), custom_call_target="tpu_custom_call" | custom-call | flops 17968398336 | bytes 8257536 | tf_op jit(solution)/shard_map/spectral_filter/pallas_call | solution.py:252
  414.5 8.7 longitude_hop.52
  423.3 8.7 longitude_hop.53
  462.8 8.7 longitude_hop.54
  496.5 8.8 longitude_hop.56
  544.2 35.9 %spectral_filter.6 = (bf16[4,2,4,112,384]{4,3,2,1,0:T(8,128)(2,1)}, f32[2,4,2,96,96]{4,3,2,1,0:T(8,128)}) custom-call(bf16[4,2,2,4,112,384]{5,4,3,2,1,0:T(8,128)(2,1)} %bitcast.9.data, bf16[896,896]{1,0:T(8,128)(2,1)} %get-tuple-element.392.forward, bf16[896,896]{1,0:T(8,128)(2,1)} %get-tuple-element.391.backward, bf16[768,768]{1,0:T(8,128)(2,1)} %copy.117.inner, ...), custom_call_target="tpu_custom_call" | custom-call | flops 17968398336 | bytes 8257536 | tf_op jit(solution)/shard_map/spectral_filter/pallas_call | solution.py:252
  590.5 8.9 longitude_hop.60
  630.4 8.8 longitude_hop.61
  690.0 35.8 %spectral_filter.7 = (bf16[4,2,4,112,384]{4,3,2,1,0:T(8,128)(2,1)}, f32[2,4,2,96,96]{4,3,2,1,0:T(8,128)}) custom-call(bf16[4,2,2,4,112,384]{5,4,3,2,1,0:T(8,128)(2,1)} %bitcast.11.data, bf16[896,896]{1,0:T(8,128)(2,1)} %get-tuple-element.392.forward, bf16[896,896]{1,0:T(8,128)(2,1)} %get-tuple-element.391.backward, bf16[768,768]{1,0:T(8,128)(2,1)} %copy.117.inner, ...), custom_call_target="tpu_custom_call" | custom-call | flops 17968398336 | bytes 8257536 | tf_op jit(solution)/shard_map/spectral_filter/pallas_call | solution.py:252
  778.1 9.7 collective-permute-done.72.refs_1_
  892.6 20.4 %spectral_filter.8 = (bf16[4,2,2,112,384]{4,3,2,1,0:T(8,128)(2,1)}, f32[2,4,2,96,96]{4,3,2,1,0:T(8,128)}) custom-call(bf16[4,2,2,4,112,384]{5,4,3,2,1,0:T(8,128)(2,1)} %bitcast.13.data, bf16[896,896]{1,0:T(8,128)(2,1)} %get-tuple-element.392.forward, bf16[896,896]{1,0:T(8,128)(2,1)} %get-tuple-element.391.backward, bf16[768,768]{1,0:T(8,128)(2,1)} %copy.117.inner, ...), custom_call_target="tpu_custom_call" | custom-call | flops 8984199168 | bytes 4128768 | tf_op jit(solution)/shard_map/spectral_filter/pallas_call | solution.py:252
  913.0 20.5 %spectral_filter.9 = (bf16[4,2,2,112,384]{4,3,2,1,0:T(8,128)(2,1)}, f32[2,4,2,96,96]{4,3,2,1,0:T(8,128)}) custom-call(bf16[4,2,2,4,112,384]{5,4,3,2,1,0:T(8,128)(2,1)} %bitcast.13.data, bf16[896,896]{1,0:T(8,128)(2,1)} %get-tuple-element.392.forward, bf16[896,896]{1,0:T(8,128)(2,1)} %get-tuple-element.391.backward, bf16[768,768]{1,0:T(8,128)(2,1)} %copy.117.inner, ...), custom_call_target="tpu_custom_call" | custom-call | flops 8984199168 | bytes 4128768 | tf_op jit(solution)/shard_map/spectral_filter/pallas_call | solution.py:252
  1028.3 9.1 collective-permute-done.92.refs_1_
  1082.9 15.1 %collective-permute-done.103.refs_1_ = bf16[8,112,384]{2,1,0:T(8,128)(2,1)} collective-permute-done((bf16[8,112,384]{2,1,0:T(8,128)(2,1)}, bf16[8,112,384]{2,1,0:T(8,128)(2,1)}, u32[]{:S(2)}, u32[]{:S(2)}) %collective-permute-start.103) | collective-permute-done | bytes 688160 | tf_op jit(solution)/shard_map/ppermute | solution.py:650
  1118.0 14.5 %collective-permute-done.107.refs_1_ = bf16[8,112,384]{2,1,0:T(8,128)(2,1)} collective-permute-done((bf16[8,112,384]{2,1,0:T(8,128)(2,1)}, bf16[8,112,384]{2,1,0:T(8,128)(2,1)}, u32[]{:S(2)}, u32[]{:S(2)}) %collective-permute-start.107) | collective-permute-done | bytes 688160 | tf_op jit(solution)/shard_map/ppermute | solution.py:650
  1141.2 20.0 %longitude_grid.2 = (bf16[112,112,768]{2,1,0:T(8,128)(2,1)}, bf16[64,112,384]{2,1,0:T(8,128)(2,1)}) custom-call(s32[1]{0:T(128)} %bitcast.core, bf16[17,8,112,384]{3,2,1,0:T(8,128)(2,1)} %get-tuple-element.383.refs_0_, bf16[17,8,112,384]{3,2,1,0:T(8,128)(2,1)} %get-tuple-element.384.refs_1_, bf16[2,112,256]{2,1,0:T(8,128)(2,1)} %reshape.517.refs_2_), custom_call_target="tpu_custom_call" | custom-call | flops 2818572288 | bytes 23592960 | tf_op jit(solution)/shard_map/longitude_grid/pallas_call | solution.py:385
  1161.2 15.9 %longitude_grid.3 = (bf16[112,112,768]{2,1,0:T(8,128)(2,1)}, bf16[48,112,384]{2,1,0:T(8,128)(2,1)}) custom-call(s32[1]{0:T(128)} %bitcast.core, bf16[17,8,112,384]{3,2,1,0:T(8,128)(2,1)} %get-tuple-element.383.refs_0_, bf16[17,8,112,384]{3,2,1,0:T(8,128)(2,1)} %get-tuple-element.384.refs_1_, ...), custom_call_target="tpu_custom_call", output_to_operand_aliasing={{0}: (4, {})} | custom-call | flops 2113929216 | bytes 17694720 | tf_op jit(solution)/shard_map/longitude_grid/pallas_call | solution.py:385
  (456 shorter events, 761.1 us)
Async XLA Ops:
  28.1 62.2 %collective-permute-start = (bf16[112,112,384]{2,1,0:T(8,128)(2,1)}, bf16[112,112,384]{2,1,0:T(8,128)(2,1)}, u32[]{:S(2)}, u32[]{:S(2)}) collective-permute-start(bf16[112,112,384]{2,1,0:T(8,128)(2,1)} %pick.6.refs_5_), channel_id=1, source_target_pairs={{0,1},{1,0},{2,3},{3,2},{4,5},{5,4},{6,7},{7,6},{8,9},{9,8},{10,11... | collective-permute-start | bytes 28901384 | tf_op jit(solution)/shard_map/ppermute | solution.py:506
  48.6 41.7 %collective-permute-start.3 = (bf16[112,112,384]{2,1,0:T(8,128)(2,1)}, bf16[112,112,384]{2,1,0:T(8,128)(2,1)}, u32[]{:S(2)}, u32[]{:S(2)}) collective-permute-start(bf16[112,112,384]{2,1,0:T(8,128)(2,1)} %pick.7.refs_5_), channel_id=1, source_target_pairs={{0,1},{1,0},{2,3},{3,2},{4,5},{5,4},{6,7},{7,6},{8,9},{9,8},{10,11... | collective-permute-start | bytes 28901384 | tf_op jit(solution)/shard_map/ppermute | solution.py:606
  250.6 126.9 %all-to-all-start = ((bf16[64,112,384]{2,1,0:T(8,128)(2,1)}), bf16[64,112,384]{2,1,0:T(8,128)(2,1)}, u32[]{:S(2)}, u32[]{:S(2)}) async-start(bf16[64,112,384]{2,1,0:T(8,128)(2,1)} %get-tuple-element.243), calls=%async_computation | async-start | bytes 11010048 | tf_op jit(solution)/shard_map/all_to_all | solution.py:573
  261.8 39.4 %collective-permute-start.30 = (bf16[64,16,384]{2,1,0:T(8,128)(2,1)}, bf16[64,16,384]{2,1,0:T(8,128)(2,1)}, u32[]{:S(2)}, u32[]{:S(2)}) collective-permute-start(bf16[64,16,384]{2,1,0:T(8,128)(2,1)} %get-tuple-element.226.refs_7_), channel_id=1, source_target_pairs={{0,2},{1,3},{2,4},{3,5},{4,6},{5,7},{8,10},{9,11},{10,12},{11,13},... | collective-permute-start | bytes 2359304 | tf_op jit(solution)/shard_map/ppermute | solution.py:600
  310.2 36.8 %collective-permute-start.34 = (bf16[64,16,384]{2,1,0:T(8,128)(2,1)}, bf16[64,16,384]{2,1,0:T(8,128)(2,1)}, u32[]{:S(2)}, u32[]{:S(2)}) collective-permute-start(bf16[64,16,384]{2,1,0:T(8,128)(2,1)} %get-tuple-element.232.refs_8_), channel_id=1, source_target_pairs={{0,2},{1,3},{2,4},{3,5},{4,6},{5,7},{8,10},{9,11},{10,12},{11,13},... | collective-permute-start | bytes 2359304 | tf_op jit(solution)/shard_map/ppermute | solution.py:600
  355.8 57.6 %collective-permute-start.38 = (bf16[64,16,384]{2,1,0:T(8,128)(2,1)}, bf16[64,16,384]{2,1,0:T(8,128)(2,1)S(1)}, u32[]{:S(2)}, u32[]{:S(2)}) collective-permute-start(bf16[64,16,384]{2,1,0:T(8,128)(2,1)} %get-tuple-element.238.refs_8_), channel_id=1, source_target_pairs={{0,2},{1,3},{2,4},{3,5},{4,6},{5,7},{8,10},{9,11},{10,12},{11,13},... | collective-permute-start | bytes 2359304 | tf_op jit(solution)/shard_map/ppermute | solution.py:600
  360.4 53.0 %collective-permute-start.39 = (bf16[64,16,384]{2,1,0:T(8,128)(2,1)}, bf16[64,16,384]{2,1,0:T(8,128)(2,1)S(1)}, u32[]{:S(2)}, u32[]{:S(2)}) collective-permute-start(bf16[64,16,384]{2,1,0:T(8,128)(2,1)} %get-tuple-element.241), channel_id=1, source_target_pairs={{2,0},{3,1},{4,2},{5,3},{6,4},{7,5},{10,8},{11,9},{12,10},{13,11},... | collective-permute-start | bytes 2359304 | tf_op jit(solution)/shard_map/ppermute | solution.py:601
  370.5 52.8 %collective-permute-start.36 = (bf16[64,16,384]{2,1,0:T(8,128)(2,1)}, bf16[64,16,384]{2,1,0:T(8,128)(2,1)}, u32[]{:S(2)}, u32[]{:S(2)}) collective-permute-start(bf16[64,16,384]{2,1,0:T(8,128)(2,1)} %get-tuple-element.239.refs_0_), channel_id=1, source_target_pairs={{0,2},{1,3},{2,4},{3,5},{4,6},{5,7},{8,10},{9,11},{10,12},{11,13},... | collective-permute-start | bytes 2359304 | tf_op jit(solution)/shard_map/ppermute | solution.py:600
  376.1 47.2 %collective-permute-start.37 = (bf16[64,16,384]{2,1,0:T(8,128)(2,1)}, bf16[64,16,384]{2,1,0:T(8,128)(2,1)}, u32[]{:S(2)}, u32[]{:S(2)}) collective-permute-start(bf16[64,16,384]{2,1,0:T(8,128)(2,1)} %get-tuple-element.240), channel_id=1, source_target_pairs={{2,0},{3,1},{4,2},{5,3},{6,4},{7,5},{10,8},{11,9},{12,10},{13,11},... | collective-permute-start | bytes 2359304 | tf_op jit(solution)/shard_map/ppermute | solution.py:601
  432.0 76.4 %all-to-all-start.1 = ((bf16[64,112,384]{2,1,0:T(8,128)(2,1)}), bf16[64,112,384]{2,1,0:T(8,128)(2,1)}, u32[]{:S(2)}, u32[]{:S(2)}) async-start(bf16[64,112,384]{2,1,0:T(8,128)(2,1)} %get-tuple-element.263), calls=%async_computation.1 | async-start | bytes 11010048 | tf_op jit(solution)/shard_map/all_to_all | solution.py:573
  508.4 90.9 %all-to-all-start.2 = ((bf16[32,112,384]{2,1,0:T(8,128)(2,1)}), bf16[32,112,384]{2,1,0:T(8,128)(2,1)}, u32[]{:S(2)}, u32[]{:S(2)}) async-start(bf16[32,112,384]{2,1,0:T(8,128)(2,1)} %bitcast.46), calls=%async_computation.2 | async-start | bytes 5505024 | tf_op jit(solution)/shard_map/all_to_all | solution.py:573
  522.6 57.5 %collective-permute-start.48 = (bf16[64,16,384]{2,1,0:T(8,128)(2,1)}, bf16[64,16,384]{2,1,0:T(8,128)(2,1)S(1)}, u32[]{:S(2)}, u32[]{:S(2)}) collective-permute-start(bf16[64,16,384]{2,1,0:T(8,128)(2,1)} %get-tuple-element.258.refs_8_), channel_id=1, source_target_pairs={{0,2},{1,3},{2,4},{3,5},{4,6},{5,7},{8,10},{9,11},{10,12},{11,13},... | collective-permute-start | bytes 2359304 | tf_op jit(solution)/shard_map/ppermute | solution.py:600
  527.3 52.8 %collective-permute-start.49 = (bf16[64,16,384]{2,1,0:T(8,128)(2,1)}, bf16[64,16,384]{2,1,0:T(8,128)(2,1)}, u32[]{:S(2)}, u32[]{:S(2)}) collective-permute-start(bf16[64,16,384]{2,1,0:T(8,128)(2,1)} %get-tuple-element.259), channel_id=1, source_target_pairs={{2,0},{3,1},{4,2},{5,3},{6,4},{7,5},{10,8},{11,9},{12,10},{13,11},... | collective-permute-start | bytes 2359304 | tf_op jit(solution)/shard_map/ppermute | solution.py:601
  538.4 51.2 %collective-permute-start.54 = (bf16[64,16,384]{2,1,0:T(8,128)(2,1)}, bf16[64,16,384]{2,1,0:T(8,128)(2,1)S(1)}, u32[]{:S(2)}, u32[]{:S(2)}) collective-permute-start(bf16[64,16,384]{2,1,0:T(8,128)(2,1)} %get-tuple-element.264.refs_0_), channel_id=1, source_target_pairs={{0,2},{1,3},{2,4},{3,5},{4,6},{5,7},{8,10},{9,11},{10,12},{11,13},... | collective-permute-start | bytes 2359304 | tf_op jit(solution)/shard_map/ppermute | solution.py:600
  542.9 46.7 %collective-permute-start.55 = (bf16[64,16,384]{2,1,0:T(8,128)(2,1)}, bf16[64,16,384]{2,1,0:T(8,128)(2,1)}, u32[]{:S(2)}, u32[]{:S(2)}) collective-permute-start(bf16[64,16,384]{2,1,0:T(8,128)(2,1)} %get-tuple-element.268), channel_id=1, source_target_pairs={{2,0},{3,1},{4,2},{5,3},{6,4},{7,5},{10,8},{11,9},{12,10},{13,11},... | collective-permute-start | bytes 2359304 | tf_op jit(solution)/shard_map/ppermute | solution.py:601
  599.3 53.6 %all-to-all-start.3 = ((bf16[64,112,384]{2,1,0:T(8,128)(2,1)}), bf16[64,112,384]{2,1,0:T(8,128)(2,1)}, u32[]{:S(2)}, u32[]{:S(2)}) async-start(bf16[64,112,384]{2,1,0:T(8,128)(2,1)} %get-tuple-element.288), calls=%async_computation.3 | async-start | bytes 11010048 | tf_op jit(solution)/shard_map/all_to_all | solution.py:573
  611.8 45.7 %collective-permute-start.58 = (bf16[64,16,384]{2,1,0:T(8,128)(2,1)S(1)}, bf16[64,16,384]{2,1,0:T(8,128)(2,1)S(1)}, u32[]{:S(2)}, u32[]{:S(2)}) collective-permute-start(bf16[64,16,384]{2,1,0:T(8,128)(2,1)S(1)} %copy-done.2), channel_id=1, source_target_pairs={{0,2},{1,3},{2,4},{3,5},{4,6},{5,7},{8,10},{9,11},{10,12},{11,13},... | collective-permute-start | bytes 2359304 | tf_op jit(solution)/shard_map/ppermute | solution.py:600
  616.4 41.1 %collective-permute-start.59 = (bf16[64,16,384]{2,1,0:T(8,128)(2,1)}, bf16[64,16,384]{2,1,0:T(8,128)(2,1)}, u32[]{:S(2)}, u32[]{:S(2)}) collective-permute-start(bf16[64,16,384]{2,1,0:T(8,128)(2,1)} %get-tuple-element.273), channel_id=1, source_target_pairs={{2,0},{3,1},{4,2},{5,3},{6,4},{7,5},{10,8},{11,9},{12,10},{13,11},... | collective-permute-start | bytes 2359304 | tf_op jit(solution)/shard_map/ppermute | solution.py:601
  647.4 41.1 %collective-permute-start.64 = (bf16[8,112,384]{2,1,0:T(8,128)(2,1)}, bf16[8,112,384]{2,1,0:T(8,128)(2,1)}, u32[]{:S(2)}, u32[]{:S(2)}) collective-permute-start(bf16[8,112,384]{2,1,0:T(8,128)(2,1)} %get-tuple-element.275.refs_8_), channel_id=1, source_target_pairs={{0,2},{1,3},{2,4},{3,5},{4,6},{5,7},{8,10},{9,11},{10,12},{11,13},... | collective-permute-start | bytes 2064392 | tf_op jit(solution)/shard_map/ppermute | solution.py:650
  652.9 72.9 %all-to-all-start.4 = ((bf16[32,112,384]{2,1,0:T(8,128)(2,1)}), bf16[32,112,384]{2,1,0:T(8,128)(2,1)}, u32[]{:S(2)}, u32[]{:S(2)}) async-start(bf16[32,112,384]{2,1,0:T(8,128)(2,1)} %bitcast.47), calls=%async_computation.4 | async-start | bytes 5505024 | tf_op jit(solution)/shard_map/all_to_all | solution.py:573
  664.4 73.5 %collective-permute-start.62 = (bf16[64,16,384]{2,1,0:T(8,128)(2,1)}, bf16[64,16,384]{2,1,0:T(8,128)(2,1)S(1)}, u32[]{:S(2)}, u32[]{:S(2)}) collective-permute-start(bf16[64,16,384]{2,1,0:T(8,128)(2,1)} %get-tuple-element.279.refs_3_), channel_id=1, source_target_pairs={{0,2},{1,3},{2,4},{3,5},{4,6},{5,7},{8,10},{9,11},{10,12},{11,13},... | collective-permute-start | bytes 2359304 | tf_op jit(solution)/shard_map/ppermute | solution.py:600
  670.2 73.1 %collective-permute-start.63 = (bf16[64,16,384]{2,1,0:T(8,128)(2,1)}, bf16[64,16,384]{2,1,0:T(8,128)(2,1)S(1)}, u32[]{:S(2)}, u32[]{:S(2)}) collective-permute-start(bf16[64,16,384]{2,1,0:T(8,128)(2,1)} %get-tuple-element.283), channel_id=1, source_target_pairs={{2,0},{3,1},{4,2},{5,3},{6,4},{7,5},{10,8},{11,9},{12,10},{13,11},... | collective-permute-start | bytes 2359304 | tf_op jit(solution)/shard_map/ppermute | solution.py:601
  675.2 55.2 %collective-permute-start.65 = (bf16[8,112,384]{2,1,0:T(8,128)(2,1)}, bf16[8,112,384]{2,1,0:T(8,128)(2,1)}, u32[]{:S(2)}, u32[]{:S(2)}) collective-permute-start(bf16[8,112,384]{2,1,0:T(8,128)(2,1)} %get-tuple-element.285), channel_id=1, source_target_pairs={{2,0},{3,1},{4,2},{5,3},{6,4},{7,5},{10,8},{11,9},{12,10},{13,11},... | collective-permute-start | bytes 2064392 | tf_op jit(solution)/shard_map/ppermute | solution.py:650
  676.5 78.3 %collective-permute-start.66 = (bf16[8,112,384]{2,1,0:T(8,128)(2,1)}, bf16[8,112,384]{2,1,0:T(8,128)(2,1)}, u32[]{:S(2)}, u32[]{:S(2)}) collective-permute-start(bf16[8,112,384]{2,1,0:T(8,128)(2,1)} %get-tuple-element.280.refs_8_), channel_id=1, source_target_pairs={{0,2},{1,3},{2,4},{3,5},{4,6},{5,7},{8,10},{9,11},{10,12},{11,13},... | collective-permute-start | bytes 2064392 | tf_op jit(solution)/shard_map/ppermute | solution.py:650
  688.5 71.4 %collective-permute-start.67 = (bf16[8,112,384]{2,1,0:T(8,128)(2,1)}, bf16[8,112,384]{2,1,0:T(8,128)(2,1)}, u32[]{:S(2)}, u32[]{:S(2)}) collective-permute-start(bf16[8,112,384]{2,1,0:T(8,128)(2,1)} %get-tuple-element.292), channel_id=1, source_target_pairs={{2,0},{3,1},{4,2},{5,3},{6,4},{7,5},{10,8},{11,9},{12,10},{13,11},... | collective-permute-start | bytes 2064392 | tf_op jit(solution)/shard_map/ppermute | solution.py:650
  725.8 100.4 %all-to-all-start.6 = ((bf16[32,112,384]{2,1,0:T(8,128)(2,1)}), bf16[32,112,384]{2,1,0:T(8,128)(2,1)}, u32[]{:S(2)}, u32[]{:S(2)}) async-start(bf16[32,112,384]{2,1,0:T(8,128)(2,1)} %bitcast.48), calls=%async_computation.6 | async-start | bytes 5505024 | tf_op jit(solution)/shard_map/all_to_all | solution.py:573
  750.2 44.9 %collective-permute-start.70 = (bf16[64,16,384]{2,1,0:T(8,128)(2,1)}, bf16[64,16,384]{2,1,0:T(8,128)(2,1)S(1)}, u32[]{:S(2)}, u32[]{:S(2)}) collective-permute-start(bf16[64,16,384]{2,1,0:T(8,128)(2,1)} %get-tuple-element.295.refs_5_), channel_id=1, source_target_pairs={{0,2},{1,3},{2,4},{3,5},{4,6},{5,7},{8,10},{9,11},{10,12},{11,13},... | collective-permute-start | bytes 2359304 | tf_op jit(solution)/shard_map/ppermute | solution.py:600
  761.2 39.3 %collective-permute-start.71 = (bf16[64,16,384]{2,1,0:T(8,128)(2,1)}, bf16[64,16,384]{2,1,0:T(8,128)(2,1)}, u32[]{:S(2)}, u32[]{:S(2)}) collective-permute-start(bf16[64,16,384]{2,1,0:T(8,128)(2,1)} %get-tuple-element.299), channel_id=1, source_target_pairs={{2,0},{3,1},{4,2},{5,3},{6,4},{7,5},{10,8},{11,9},{12,10},{13,11},... | collective-permute-start | bytes 2359304 | tf_op jit(solution)/shard_map/ppermute | solution.py:601
  772.7 46.6 %collective-permute-start.68 = (bf16[64,16,384]{2,1,0:T(8,128)(2,1)}, bf16[64,16,384]{2,1,0:T(8,128)(2,1)S(1)}, u32[]{:S(2)}, u32[]{:S(2)}) collective-permute-start(bf16[64,16,384]{2,1,0:T(8,128)(2,1)} %get-tuple-element.297.refs_5_), channel_id=1, source_target_pairs={{0,2},{1,3},{2,4},{3,5},{4,6},{5,7},{8,10},{9,11},{10,12},{11,13},... | collective-permute-start | bytes 2359304 | tf_op jit(solution)/shard_map/ppermute | solution.py:600
  826.2 66.4 %all-to-all-start.5 = ((bf16[64,112,384]{2,1,0:T(8,128)(2,1)}), bf16[64,112,384]{2,1,0:T(8,128)(2,1)}, u32[]{:S(2)}, u32[]{:S(2)}) async-start(bf16[64,112,384]{2,1,0:T(8,128)(2,1)} %get-tuple-element.311), calls=%async_computation.5 | async-start | bytes 11010048 | tf_op jit(solution)/shard_map/all_to_all | solution.py:573
  988.3 126.6 %all-gather.6.cloned.1.call-start = ((), (), s32[]{:S(2)}) async-start(), calls=%async_computation.11 | async-start | bytes 1327104 | tf_op jit(solution)/shard_map/all_gather | solution.py:666
  1013.5 147.7 %all-gather.4.cloned.1.call-start = ((), (), s32[]{:S(2)}) async-start(), calls=%async_computation.10 | async-start | bytes 1474560 | tf_op jit(solution)/shard_map/all_gather | solution.py:668
  (145 other events, 2411.6 us)
Sparse Core Ops, SparseCore 0:
  1013.6 30.2 all-gather.5
  1117.2 30.4 all-gather.3
